TPU v7x, 128 devices: a whole 4x4x4 slice. The times are simulated.
128 devices in a mesh: src: 16 (over y_hi, z, core), frq: 8 (over y_lo, x).
Axes of the slice: x: 4, y: 4 (y_hi: 2, y_lo: 2; y = y_hi * 2 + y_lo), z: 4, core: 2. Of those that a mesh axis runs over, the one named last changes fastest.
Arguments:
- coeffs: bfloat16 [256, 2048, 2, 256], P('frq', 'src'), may hold values from -6 to 6
- angles: bfloat16 [3, 256, 2048, 256], P(None, 'frq', 'src'), may hold values from -3.140625 to 3.140625
- interp: bfloat16 [3, 2, 2, 256, 256], replicated, may hold values from -0.375 to 0.375
- pattern: int32 [3, 4, 2], replicated, may hold values from 0 to 3, all different within a row
- target_map: bfloat16 [256, 256], replicated, may hold values from -0.375 to 0.375
Outputs:
- result: float32 [256, 2048, 2, 256], P(None, ('src', 'frq'))
Inputs may be any that keep to these rules, and one draw needn't show every extreme that they name: `pattern`: each row of a level names 2 different blocks, and every block is named at some level.
All inputs are finite; a program needn't handle non-finite values.
Results may differ from a plain program's by a relative error of at most 0.007.
Values may be sent and summed in bfloat16 or wider, within the bound.
No kernel may reach another device: no remote copies, remote signals or barrier semaphores. Data moves between devices by JAX's collectives and lax.ppermute only.
A program may use at most 128 MiB of HBM per device.

v0:
```python
import jax
import jax.numpy as jnp
from jax import lax
from jax.sharding import PartitionSpec as P

BLOCK = 64
LEVELS = 3


def partner_2(value, axis, distance):
    return lax.ppermute(value, axis, [(i, i ^ 1 << distance) for i in range(lax.axis_size(axis))])


def block_mask(pattern_row):
    blocks = pattern_row.shape[0]
    small = jnp.any(
        pattern_row[:, :, None] == jnp.arange(blocks, dtype=jnp.int32)[None, None, :], axis=1
    )
    return jnp.repeat(jnp.repeat(small.T, BLOCK, axis=0), BLOCK, axis=1)


def rotate(current, phases):
    angle_f = phases.astype(jnp.float32)
    cos_part = jnp.cos(angle_f)
    sin_part = jnp.sin(angle_f)
    real_part = current[:, :, 0].astype(jnp.float32)
    imag_part = current[:, :, 1].astype(jnp.float32)
    turned = jnp.stack(
        [real_part * cos_part - imag_part * sin_part, real_part * sin_part + imag_part * cos_part],
        axis=2,
    )
    return turned.astype(jnp.bfloat16)


def combine(rotated, partner, interp_level, pattern_row, height):
    masked = jnp.where(
        block_mask(pattern_row)[None, None], interp_level, jnp.zeros((), jnp.bfloat16)
    )
    own_bit = lax.axis_index("src") >> height & 1
    chosen = lax.dynamic_index_in_dim(masked, own_bit, 0, keepdims=False)
    w_own = lax.dynamic_index_in_dim(chosen, own_bit, 0, keepdims=False)
    w_partner = lax.dynamic_index_in_dim(chosen, 1 - own_bit, 0, keepdims=False)
    total = jnp.einsum("fscp,pq->fscq", rotated, w_own, preferred_element_type=jnp.float32)
    total = total + jnp.einsum(
        "fscp,pq->fscq", partner, w_partner, preferred_element_type=jnp.float32
    )
    return total.astype(jnp.bfloat16)


def on_device(coeffs, angles, interp, pattern, target_map):
    current = coeffs
    for height in range(LEVELS - 1):
        rotated = rotate(current, angles[height])
        partner = partner_2(rotated, "src", height)
        current = combine(rotated, partner, interp[height], pattern[height], height)
    final_height = LEVELS - 1
    rotated = rotate(current, angles[final_height])
    partner = partner_2(rotated, "src", final_height)
    current = combine(rotated, partner, interp[final_height], pattern[final_height], final_height)
    current = lax.all_to_all(current, "frq", split_axis=1, concat_axis=0, tiled=True)
    return jnp.einsum("gf,fscp->gscp", target_map, current, preferred_element_type=jnp.float32)


def solution(mesh):
    return jax.shard_map(
        on_device,
        mesh=mesh,
        in_specs=(P("frq", "src", None, None), P(None, "frq", "src", None), P(), P(), P()),
        out_specs=P(None, ("src", "frq"), None, None),
        check_vma=False,
    )
```

profile of v0, /device:TPU:0, one launch (start us, length us, event | category | flops | bytes accessed | tf_op | source)
XLA Modules:
  0.0 362.0 jit_solution(13461998414036845114)
XLA Ops:
  0.0 0.0 copy-start
  0.0 9.1 %fusion.48 = (bf16[32,128,1,256]{3,2,1,0:T(2,128)(2,1)S(1)}, bf16[32,128,1,256]{3,2,1,0:T(2,128)(2,1)S(1)}) fusion(bf16[32,128,2,256]{3,2,1,0:T(2,128)(2,1)} %param.5), kind=kLoop, calls=%fused_computation.79 | loop fusion | bytes 8388608 | tf_op jit(solution)/shard_map/slice | solution.py:26
  9.1 17.3 %fusion.1 = (bf16[32,128,1,256]{3,1,2,0:T(8,128)(2,1)S(1)}, bf16[32,128,1,256]{3,1,2,0:T(8,128)(2,1)S(1)}) fusion(bf16[3,32,128,256]{3,2,1,0:T(8,128)(2,1)} %param.6, bf16[32,128,1,256]{3,2,1,0:T(2,128)(2,1)S(1)} %get-tuple-element.12, bf16[32,128,1,256]{3,2,1,0:T(2,128)(2,1)S(1)} %get-tuple-element.11), kind=kLoop, calls=%fused_computation.22 | loop fusion | flops 11534336 | bytes 10485760 | tf_op jit(solution)/shard_map/convert.4
  26.5 0.0 copy-start.1
  26.5 0.0 copy-start.5
  26.5 2.7 pad_maximum_fusion
  29.2 0.0 copy-done.1
  29.2 0.0 collective-permute-start
  29.2 0.0 copy-done.5
  29.2 0.1 fusion.39
  29.3 0.1 broadcast_in_dim.51
  29.4 0.1 reshape.96
  29.5 0.2 copy.50
  29.7 0.1 broadcast_in_dim.56
  29.7 0.1 reshape.97
  29.9 0.2 copy.51
  30.0 0.1 fusion.41
  30.1 0.1 broadcast_in_dim.60
  30.2 0.1 reshape.98
  30.3 0.2 copy.52
  30.5 0.0 copy-start.2
  30.5 1.7 bitcast_select_fusion.2
  32.2 0.3 copy-done.2
  32.6 1.3 fusion.31
  33.8 2.9 collective-permute-done
  36.7 3.5 add_convert_fusion.2
  40.2 17.3 %fusion.7 = (bf16[32,128,1,256]{3,1,2,0:T(8,128)(2,1)S(1)}, bf16[32,128,1,256]{3,1,2,0:T(8,128)(2,1)S(1)}) fusion(bf16[32,128,2,256]{3,1,2,0:T(8,128)(2,1)S(1)} %add_convert_fusion.2, bf16[3,32,128,256]{3,2,1,0:T(8,128)(2,1)} %param.6), kind=kLoop, calls=%fused_computation.28 | loop fusion | flops 11534336 | bytes 10485760 | tf_op jit(solution)/shard_map/convert.2
  57.5 0.0 copy-start.4
  57.5 2.7 pad_maximum_fusion.1
  60.2 0.0 copy-done.4
  60.2 2.0 collective-permute-start.1
  62.2 2.9 fusion.28
  65.1 88.3 %collective-permute-done.1 = bf16[32,128,2,256]{3,1,2,0:T(8,128)(2,1)} collective-permute-done((bf16[32,128,2,256]{3,1,2,0:T(8,128)(2,1)}, bf16[32,128,2,256]{3,1,2,0:T(8,128)(2,1)}, u32[]{:S(2)}, u32[]{:S(2)}) %collective-permute-start.1) | collective-permute-done | bytes 4194336 | tf_op jit(solution)/shard_map/ppermute | solution.py:11
  153.4 3.5 add_convert_fusion.1
  156.9 17.3 %fusion.13 = (bf16[32,128,1,256]{3,1,2,0:T(8,128)(2,1)S(1)}, bf16[32,128,1,256]{3,1,2,0:T(8,128)(2,1)S(1)}) fusion(bf16[32,128,2,256]{3,1,2,0:T(8,128)(2,1)S(1)} %add_convert_fusion.1, bf16[3,32,128,256]{3,2,1,0:T(8,128)(2,1)} %param.6), kind=kLoop, calls=%fused_computation.34 | loop fusion | flops 11534336 | bytes 10485760 | tf_op jit(solution)/shard_map/convert
  174.2 0.0 copy-start.3
  174.2 2.7 pad_maximum_fusion.2
  176.9 0.0 copy-done.3
  176.9 3.7 %collective-permute-start.2 = (bf16[32,128,2,256]{3,1,2,0:T(8,128)(2,1)}, bf16[32,128,2,256]{3,1,2,0:T(8,128)(2,1)}, u32[]{:S(2)}, u32[]{:S(2)}) collective-permute-start(bf16[32,128,2,256]{3,1,2,0:T(8,128)(2,1)} %pad_maximum_fusion.2), channel_id=1, source_target_pairs={{0,32},{8,40},{16,48},{24,56},{32,0},{40,8},{48,16},{56,24},{64,96... | collective-permute-start | bytes 12582920 | tf_op jit(solution)/shard_map/ppermute | solution.py:11
  180.6 2.8 fusion.25
  183.5 87.5 %collective-permute-done.2 = bf16[32,128,2,256]{3,1,2,0:T(8,128)(2,1)} collective-permute-done((bf16[32,128,2,256]{3,1,2,0:T(8,128)(2,1)}, bf16[32,128,2,256]{3,1,2,0:T(8,128)(2,1)}, u32[]{:S(2)}, u32[]{:S(2)}) %collective-permute-start.2) | collective-permute-done | bytes 4194336 | tf_op jit(solution)/shard_map/ppermute | solution.py:11
  271.0 5.5 %add_convert_fusion = bf16[32,128,2,256]{3,1,2,0:T(8,128)(2,1)} fusion(f32[32,128,2,256]{3,1,2,0:T(8,128)S(1)} %fusion.25, bf16[32,128,2,256]{3,1,2,0:T(8,128)(2,1)} %collective-permute-done.2, bf16[2,2,256,256]{3,2,1,0:T(8,128)(2,1)S(1)} %get-tuple-element.14, s32[]{:T(128)S(6)} %select_n.57, s32[]{:T(128)S(6)} %select_n.59), kind=kOutput, calls=%fused_computation | convolution fusion | flops 1077936128 | bytes 16908296 | tf_op jit(solution)/shard_map/fscp,pq->fscq/dot_general | solution.py:44
  276.5 6.5 %copy.53 = bf16[32,128,2,256]{3,2,0,1:T(2,128)(2,1)S(1)} copy(bf16[32,128,2,256]{3,1,2,0:T(8,128)(2,1)} %add_convert_fusion) | data formatting | bytes 8388608 | tf_op jit(solution)/shard_map/convert_element_type | solution.py:47
  283.0 53.5 %all_to_all.18 = bf16[32,128,2,256]{3,2,0,1:T(2,128)(2,1)S(1)} all-to-all(bf16[32,128,2,256]{3,2,0,1:T(2,128)(2,1)S(1)} %copy.53), channel_id=1, replica_groups=mesh['src'=16,'frq'=8] {'frq'}, dimensions={1} | all-to-all | bytes 8388608 | tf_op jit(solution)/shard_map/all_to_all | solution.py:60
  336.5 3.4 copy.54
  339.9 0.6 copy.55
  340.6 8.3 %fusion.20 = f32[256,16,2,256]{0,3,2,1:T(8,128)} fusion(bf16[256,16,2,256]{3,1,2,0:T(8,128)(2,1)S(1)} %bitcast.128, bf16[256,256]{1,0:T(8,128)(2,1)S(1)} %copy-done), kind=kOutput, calls=%fused_computation.44 | convolution fusion | flops 1073741824 | bytes 12713984 | tf_op jit(solution)/shard_map/gf,fscp->gscp/dot_general | solution.py:61
  348.9 13.1 %copy.57 = f32[256,16,2,256]{3,2,1,0:T(2,128)} copy(f32[256,16,2,256]{0,3,2,1:T(8,128)} %fusion.20) | data formatting | bytes 16777216 | tf_op jit(solution)/shard_map/gf,fscp->gscp/dot_general | solution.py:61
  (5 shorter events, 0.1 us)
Async XLA Ops:
  0.0 340.6 %copy-start = (bf16[256,256]{1,0:T(8,128)(2,1)S(1)}, bf16[256,256]{1,0:T(8,128)(2,1)}, u32[]{:S(2)}) copy-start(bf16[256,256]{1,0:T(8,128)(2,1)} %param.9) | copy-start | bytes 393220
  26.5 2.7 copy-start.1
  26.5 2.7 copy-start.5
  29.2 7.5 %collective-permute-start = (bf16[32,128,2,256]{3,1,2,0:T(8,128)(2,1)}, bf16[32,128,2,256]{3,1,2,0:T(8,128)(2,1)}, u32[]{:S(2)}, u32[]{:S(2)}) collective-permute-start(bf16[32,128,2,256]{3,1,2,0:T(8,128)(2,1)} %pad_maximum_fusion), channel_id=1, source_target_pairs={{0,8},{8,0},{16,24},{24,16},{32,40},{40,32},{48,56},{56,48},{64,72... | collective-permute-start | bytes 12582920 | tf_op jit(solution)/shard_map/ppermute | solution.py:11
  30.5 2.1 copy-start.2
  57.5 2.7 copy-start.4
  60.2 93.2 %collective-permute-start.1 = (bf16[32,128,2,256]{3,1,2,0:T(8,128)(2,1)}, bf16[32,128,2,256]{3,1,2,0:T(8,128)(2,1)}, u32[]{:S(2)}, u32[]{:S(2)}) collective-permute-start(bf16[32,128,2,256]{3,1,2,0:T(8,128)(2,1)} %pad_maximum_fusion.1), channel_id=1, source_target_pairs={{0,16},{8,24},{16,0},{24,8},{32,48},{40,56},{48,32},{56,40},{64,80... | collective-permute-start | bytes 12582920 | tf_op jit(solution)/shard_map/ppermute | solution.py:11
  174.2 2.7 copy-start.3
  176.9 94.1 %collective-permute-start.2 = (bf16[32,128,2,256]{3,1,2,0:T(8,128)(2,1)}, bf16[32,128,2,256]{3,1,2,0:T(8,128)(2,1)}, u32[]{:S(2)}, u32[]{:S(2)}) collective-permute-start(bf16[32,128,2,256]{3,1,2,0:T(8,128)(2,1)} %pad_maximum_fusion.2), channel_id=1, source_target_pairs={{0,32},{8,40},{16,48},{24,56},{32,0},{40,8},{48,16},{56,24},{64,96... | collective-permute-start | bytes 12582920 | tf_op jit(solution)/shard_map/ppermute | solution.py:11
where the time goes:
time: 363 us; the launch traced here: 362 us
  waiting for transfers between devices  179 us (49%)
  other arithmetic  61.9 us (17%)
  blocking collectives  53.5 us (15%)
  local copies, waits for them, and re-layouts  34.2 us (9%)
  matrix products  27.7 us (8%)
  starting transfers between devices  5.73 us (2%)
    ppermute x3, waiting for transfers between devices, partner_2(): lax.ppermute(value, axis, [(i, i ^ 1 << distance) for i in range(lax.axis...  179 us
    all_to_all x1, blocking collectives, on_device(): lax.all_to_all(current, 'frq', split_axis=1, concat_axis=0, tiled=True)  53.5 us
    another operation x3, other arithmetic  51.9 us
    dot_general x1, local copies, waits for them, and re-layouts, on_device(): jnp.einsum('gf,fscp->gscp', target_map, current, preferred_element_type=j...  13.1 us
    dot_general x3, matrix products, combine(): jnp.einsum('fscp,pq->fscq', partner, w_partner, preferred_element_type=jn...  12.5 us
    slice x1, local copies, waits for them, and re-layouts, rotate(): real_part = current[:, :, 0].astype(jnp.float32)  9.14 us
    dot_general x1, matrix products, on_device(): jnp.einsum('gf,fscp->gscp', target_map, current, preferred_element_type=j...  8.31 us
    another operation x3, other arithmetic, rotate(): jnp.stack([real_part * cos_part - imag_part * sin_part, real_part * sin_p...  8.07 us
  transfers between devices with their start and end apart: 3, of which 3 were waited for; matrix products, arithmetic and copies ran while one was open for 3% of the time, Pallas kernels for 0%

commit v1 on v0

v1 whole, which is shorter than its diff:
```python
import functools

import jax
import jax.numpy as jnp
import numpy as np
from jax import lax
from jax.experimental import pallas as pl
from jax.experimental.pallas import tpu as pltpu
from jax.sharding import PartitionSpec as P

BLOCK = 64
LEVELS = 3
CHUNKS = (4, 4, 4, 4)
STEP = 2
SB = 128
W = 256
BF = jnp.bfloat16
F32 = jnp.float32

_x = np.cos((np.arange(400) + 0.5) * np.pi / 400) * 3.1410
_u = (_x * _x) / 10.0
COS = np.linalg.lstsq(np.stack([_u**k for k in range(6)], 1), np.cos(_x), rcond=None)[0]
SIN = np.linalg.lstsq(np.stack([_x * _u**k for k in range(5)], 1), np.sin(_x), rcond=None)[0]
COS = [float(c / 10.0**k) for k, c in enumerate(COS)]
SIN = [float(c / 10.0**k) for k, c in enumerate(SIN)]


def cos_sin(x):
    u = x * x
    c = COS[5] * u + COS[4]
    for k in (3, 2, 1, 0):
        c = c * u + COS[k]
    s = SIN[4] * u + SIN[3]
    for k in (2, 1, 0):
        s = s * u + SIN[k]
    return c, s * x


def turn(re, im, angle):
    c, s = cos_sin(angle.astype(F32))
    return (re * c - im * s).astype(BF), (re * s + im * c).astype(BF)


def dot(a, b):
    return jnp.dot(a, b, preferred_element_type=F32)


def call(kernel, name, grid, in_specs, out_specs, out_shape, prefetch=0, scratch=(), flops=0, nbytes=0):
    return pl.pallas_call(
        kernel,
        out_shape=out_shape,
        grid_spec=pltpu.PrefetchScalarGridSpec(
            num_scalar_prefetch=prefetch, grid=grid, in_specs=in_specs, out_specs=out_specs, scratch_shapes=list(scratch)
        ),
        compiler_params=pltpu.CompilerParams(vmem_limit_bytes=40 << 20),
        cost_estimate=pl.CostEstimate(flops=int(flops), bytes_accessed=int(nbytes), transcendentals=0),
        name=name,
    )


def weights_kernel(meta, pattern, interp, out):
    t = pl.program_id(0)
    slot = t // 2
    level = jnp.where(slot < 2, 1, jnp.where(slot == 2, 0, 2))
    rows = lax.broadcasted_iota(jnp.int32, (W, W), 0) // BLOCK
    cols = lax.broadcasted_iota(jnp.int32, (W, W), 1) // BLOCK
    keep = None
    for q in range(4):
        for k in range(2):
            hit = (cols == q) & (rows == pattern[level * 8 + q * 2 + k])
            keep = hit if keep is None else keep | hit
    w = interp[0, 0, 0].astype(F32)
    out[0] = jnp.where(keep, w, jnp.zeros_like(w)).astype(BF)


def weights(meta, pattern, interp):
    def pick(t, meta, pattern):
        slot = t // 2
        level = jnp.where(slot < 2, 1, jnp.where(slot == 2, 0, 2))
        bit = meta[level]
        return level, bit ^ jnp.where(slot == 1, 1, 0), bit ^ (t & 1), 0, 0

    return call(
        weights_kernel, "masked_weights", (8,),
        [pl.BlockSpec((1, 1, 1, W, W), pick)],
        pl.BlockSpec((1, W, W), lambda t, *_: (t // 2, t % 2, 0)),
        jax.ShapeDtypeStruct((4, 2 * W, W), BF), prefetch=2, flops=0, nbytes=2 << 20,
    )(meta, pattern, interp)


def first_kernel(shuffle, coeffs, angles, out):
    for a in range(2):
        for i in range(STEP):
            x = jnp.concatenate([coeffs[a, i, : 2 * SB], coeffs[a, i, 2 * SB :]], axis=1)
            y = dot(shuffle[...], x)
            for part in range(2):
                lanes = slice(part * 128, part * 128 + 128)
                for r in range(0, 64, 32):
                    row = [y[k * 64 + r : k * 64 + r + 32, lanes] for k in range(4)]
                    at = part * 64 + r
                    re, im = turn(
                        jnp.concatenate(row[:2], axis=1), jnp.concatenate(row[2:], axis=1), angles[0, a, i, at : at + 32]
                    )
                    out[a, i, at : at + 32, :W] = re
                    out[a, i, at : at + 32, W:] = im


def first(shuffle, coeffs, angles, off, n):
    return call(
        first_kernel, "rotate_0", (n // STEP,),
        [
            pl.BlockSpec((W, W), lambda t: (0, 0)),
            pl.BlockSpec((2, STEP, 4 * SB, 128), lambda t: (0, off // STEP + t, 0, 0)),
            pl.BlockSpec((1, 2, STEP, SB, W), lambda t: (0, 0, off // STEP + t, 0, 0)),
        ],
        pl.BlockSpec((2, STEP, SB, 2 * W), lambda t: (0, t, 0, 0)),
        jax.ShapeDtypeStruct((2, n, SB, 2 * W), BF), flops=n * 2e8, nbytes=n * 700e3,
    )(shuffle, coeffs, angles)


def sides(own, other):
    return jnp.concatenate(
        [jnp.concatenate([own[:, :W], other[:, :W]], axis=1), jnp.concatenate([own[:, W:], other[:, W:]], axis=1)], axis=0
    )


def turn_rows(y, angles, store):
    for r in range(0, SB, 32):
        re, im = turn(y[r : r + 32], y[SB + r : SB + r + 32], angles[r : r + 32])
        store(r, re, im)


def second_kernel(meta, own, other, w, angles, keep, send):
    h = meta[3]
    for out, a in ((send, 1 - h), (keep, h)):
        for i in range(STEP):
            y = dot(sides(own[a, i], other[a, i]), w[0])

            def store(r, re, im, out=out, i=i):
                out[i, r : r + 32, :W] = re
                out[i, r : r + 32, W:] = im

            turn_rows(y, angles.at[0, a, i], store)


def second(meta, own, other, w, angles, off, n):
    both = pl.BlockSpec((2, STEP, SB, 2 * W), lambda t, *_: (0, t, 0, 0))
    one = pl.BlockSpec((STEP, SB, 2 * W), lambda t, *_: (t, 0, 0))
    return call(
        second_kernel, "mix_0_rotate_1", (n // STEP,),
        [
            both,
            both,
            pl.BlockSpec((1, 2 * W, W), lambda t, *_: (2, 0, 0)),
            pl.BlockSpec((1, 2, STEP, SB, W), lambda t, *_: (1, 0, off // STEP + t, 0, 0)),
        ],
        [one, one],
        [jax.ShapeDtypeStruct((n, SB, 2 * W), BF)] * 2, prefetch=1, flops=n * 2e8, nbytes=n * 1e6,
    )(meta, own, other, w, angles)


def third_kernel(meta, own, other, w, angles, angles_other, out):
    for i in range(STEP):
        x = sides(own[i], other[i])
        for g, angle in ((0, angles.at[0, 0, i]), (1, angles_other.at[i])):
            y = dot(x, w[g])

            def store(r, re, im, g=g, i=i):
                out[g, i, r : r + 32, :W] = re
                out[g, i, r : r + 32, W:] = im

            turn_rows(y, angle, store)


def third(meta, own, other, w, angles, angles_other, off, n):
    one = pl.BlockSpec((STEP, SB, 2 * W), lambda t, *_: (t, 0, 0))
    return call(
        third_kernel, "mix_1_rotate_2", (n // STEP,),
        [
            one,
            one,
            pl.BlockSpec((2, 2 * W, W), lambda t, *_: (0, 0, 0)),
            pl.BlockSpec((1, 1, STEP, SB, W), lambda t, meta: (2, meta[3], off // STEP + t, 0, 0)),
            pl.BlockSpec((STEP, SB, W), lambda t, *_: (off // STEP + t, 0, 0)),
        ],
        pl.BlockSpec((2, STEP, SB, 2 * W), lambda t, *_: (0, t, 0, 0)),
        jax.ShapeDtypeStruct((2, n, SB, 2 * W), BF), prefetch=1, flops=n * 2e8, nbytes=n * 700e3,
    )(meta, own, other, w, angles, angles_other)


def back_kernel(own, other, w, out):
    for i in range(STEP):
        y = dot(sides(own[0, i], other[0, i]), w[0])
        out[i, :, :W] = y[:SB].astype(BF)
        out[i, :, W:] = y[SB:].astype(BF)


def back(own, other, w, n):
    return call(
        back_kernel, "mix_2_other", (n // STEP,),
        [
            pl.BlockSpec((1, STEP, SB, 2 * W), lambda t: (1, t, 0, 0)),
            pl.BlockSpec((1, STEP, SB, 2 * W), lambda t: (0, t, 0, 0)),
            pl.BlockSpec((1, 2 * W, W), lambda t: (3, 0, 0)),
        ],
        pl.BlockSpec((STEP, SB, 2 * W), lambda t: (t, 0, 0)),
        jax.ShapeDtypeStruct((n, SB, 2 * W), BF), flops=n * 1e8, nbytes=n * 400e3,
    )(own, other, w)


def split_kernel(meta, own, other, w, came, *outs_scratch):
    outs, held = outs_scratch[:8], outs_scratch[8]
    q = meta[4]
    for i in range(STEP):
        y = dot(sides(own[0, i], other[0, i]), w[0])
        held[i, :, :W] = y[:SB].astype(BF)
        held[i, :, W:] = y[SB:].astype(BF)
    for m in range(8):
        at = pl.ds(pl.multiple_of((q ^ m) * 16, 16), 16)
        for i in range(STEP):
            outs[m][0, i] = held[i, at, :]
            outs[m][1, i] = came[i, at, :]


def split(meta, own, other, w, came, n):
    return call(
        split_kernel, "mix_2_own_split", (n // STEP,),
        [
            pl.BlockSpec((1, STEP, SB, 2 * W), lambda t, *_: (0, t, 0, 0)),
            pl.BlockSpec((1, STEP, SB, 2 * W), lambda t, *_: (1, t, 0, 0)),
            pl.BlockSpec((1, 2 * W, W), lambda t, *_: (3, 0, 0)),
            pl.BlockSpec((STEP, SB, 2 * W), lambda t, *_: (t, 0, 0)),
        ],
        [pl.BlockSpec((2, STEP, 16, 2 * W), lambda t, *_: (0, t, 0, 0))] * 8,
        [jax.ShapeDtypeStruct((2, n, 16, 2 * W), BF)] * 8, prefetch=1,
        scratch=[pltpu.VMEM((STEP, SB, 2 * W), BF)], flops=n * 1e8, nbytes=n * 800e3,
    )(meta, own, other, w, came)


def gather_kernel(n, shuffle, *refs):
    pieces, out = refs[:8], refs[8]
    per = 16 // (2 * n)
    for group in range(8 // per):
        rows = []
        for m in range(group * per, group * per + per):
            for half in range(2):
                for i in range(n):
                    rows.append(pieces[m][half, i])
        y = dot(shuffle[...], jnp.concatenate(rows, axis=0)).astype(BF)
        for j in range(16):
            out[j, group * 16 : group * 16 + 16, :] = y[j * 16 : j * 16 + 16]


def gather(shuffle, pieces, n):
    return call(
        functools.partial(gather_kernel, n), "gather_frequencies", (1,),
        [pl.BlockSpec((W, W), lambda t: (0, 0))] + [pl.BlockSpec((2, n, 16, 2 * W), lambda t: (0, 0, 0, 0))] * 8,
        pl.BlockSpec((16, 16 * n, 2 * W), lambda t: (0, 0, 0)),
        jax.ShapeDtypeStruct((16, 16 * n, 2 * W), BF), flops=n * 1e8, nbytes=n * 500e3,
    )(shuffle, *pieces)


def target_kernel(chunks, t_map, *refs):
    parts, out = refs[:chunks], refs[chunks]
    for j in range(2):
        y = dot(t_map[...], jnp.concatenate([p[j] for p in parts], axis=0))
        for c in range(2):
            for half in range(2):
                at = c * W + half * 128
                out[:, j * 4 + half * 2 + c, :] = y[:, at : at + 128]


def target(t_map, parts):
    return call(
        functools.partial(target_kernel, len(parts)), "target_map", (8,),
        [pl.BlockSpec((W, W), lambda t: (0, 0))]
        + [pl.BlockSpec((2, p.shape[1], 2 * W), lambda t: (t, 0, 0)) for p in parts],
        pl.BlockSpec((W, 8, 128), lambda t: (0, t, 0)),
        jax.ShapeDtypeStruct((W, 64, 128), F32), flops=1e9, nbytes=12 << 20,
    )(t_map, *parts)


def swap(value, axis, mask):
    return lax.ppermute(value, axis, [(i, i ^ mask) for i in range(lax.axis_size(axis))])


def shuffles():
    first_rows = np.zeros((W, W), np.float32)
    last_rows = np.zeros((W, W), np.float32)
    for j in range(64):
        for half in range(2):
            for c in range(2):
                first_rows[(c * 2 + half) * 64 + j, j * 4 + half * 2 + c] = 1
    for j in range(16):
        for f in range(16):
            last_rows[j * 16 + f, f * 16 + j] = 1
    return jnp.asarray(first_rows, BF), jnp.asarray(last_rows, BF)


def on_device(coeffs, angles, interp, pattern, target_map):
    src, frq = lax.axis_index("src"), lax.axis_index("frq")
    bits = [src >> k & 1 for k in range(LEVELS)]
    h = bits[1] ^ bits[2]
    meta = jnp.stack([*bits, h, frq]).astype(jnp.int32)
    spread, close = shuffles()
    coeffs = coeffs.reshape(2, 16, SB, 2, 2, 128).transpose(0, 1, 2, 4, 3, 5).reshape(2, 16, 4 * SB, 128)
    angles = angles.reshape(LEVELS, 2, 16, SB, W)

    offs = np.cumsum((0,) + CHUNKS)[:-1].tolist()
    order = np.concatenate(
        [
            np.asarray([m << 5 | half << 4 | off + i for m in range(8) for half in range(2) for i in range(n)])
            for off, n in zip(offs, CHUNKS)
        ]
    )
    chosen = jnp.asarray(order, jnp.int32) ^ (frq << 5) ^ (h << 4)
    hot = (jnp.arange(W, dtype=jnp.int32)[:, None] == chosen[None, :]).astype(BF)
    t_map = jnp.dot(target_map, hot, preferred_element_type=F32).astype(BF)

    angles_other = swap(lax.dynamic_index_in_dim(angles[2], 1 - h, 0, keepdims=False), "src", 2)
    w = weights(meta, pattern.reshape(-1), interp)
    parts = []
    for off, n in zip(offs, CHUNKS):
        turned = first(spread, coeffs, angles, off, n)
        keep, send = second(meta, turned, swap(turned, "src", 1), w, angles, off, n)
        turned = third(meta, keep, swap(send, "src", 2), w, angles, angles_other, off, n)
        other = swap(turned, "src", 6)
        came = swap(back(turned, other, w, n), "src", 2)
        pieces = split(meta, turned, other, w, came, n)
        pieces = [pieces[0]] + [swap(pieces[m], "frq", m) for m in range(1, 8)]
        parts.append(gather(close, pieces, n))
    out = target(t_map, parts)
    return out.reshape(W, 16, 2, 2, 128).transpose(0, 1, 3, 2, 4).reshape(W, 16, 2, W)


def solution(mesh):
    return jax.shard_map(
        on_device,
        mesh=mesh,
        in_specs=(P("frq", "src", None, None), P(None, "frq", "src", None), P(), P(), P()),
        out_specs=P(None, ("src", "frq"), None, None),
        check_vma=False,
    )
```

time: 363 us -> 240 us (0.66)
  waiting for transfers between devices: 179 us -> 81.3 us
  starting transfers between devices: 5.73 us -> 74.5 us
  other arithmetic: 61.9 us -> 0.01 us
  Pallas kernels: 0 us -> 54.4 us
  blocking collectives: 53.5 us -> 0 us
  matrix products: 27.7 us -> 0.2 us
  local copies, waits for them, and re-layouts: 34.2 us -> 27.6 us
    ppermute x3 -> x45, waiting for transfers between devices: 179 us -> 81.3 us  [swap(): lax.ppermute(value, axis, [(i, i ^ mask) for i in range(lax.axis_size(axi...]
    ppermute x3 -> x45, starting transfers between devices: 5.73 us -> 74.5 us  [swap(): lax.ppermute(value, axis, [(i, i ^ mask) for i in range(lax.axis_size(axi...]
    another operation x6 -> x0, other arithmetic: 60 us -> none
    pallas_call x0 -> x26, Pallas kernels: none -> 54.4 us  [the longest x4 12.8 us: second(): call(second_kernel, 'mix_0_rotate_1', (n // STEP,), [both, both, pl.Block...]
    all_to_all x1 -> x0, blocking collectives: 53.5 us -> none  [on_device(): lax.all_to_all(current, 'frq', split_axis=1, concat_axis=0, tiled=True)]
    dot_general x7 -> x1, matrix products: 27.7 us -> 0.2 us  [on_device(): t_map = jnp.dot(target_map, hot, preferred_element_type=F32).astype(BF)]
    unnamed x12 -> x89, local copies, waits for them, and re-layouts: 0.36 us -> 23.5 us
    dot_general x1 -> x0, local copies, waits for them, and re-layouts: 13.1 us -> none  [on_device(): jnp.einsum('gf,fscp->gscp', target_map, current, preferred_element_type=j...]
  transfers between devices with their start and end apart: 3 -> 45, of which waited for: 3 -> 10; matrix products, arithmetic and copies ran while one was open for 3% -> 2% of each run, Pallas kernels for 0% -> 18%
where the time goes in v1:
time: 240 us; the launch traced here: 238 us
  waiting for transfers between devices  81.3 us (34%)
  starting transfers between devices  74.5 us (31%)
  Pallas kernels  54.4 us (23%)
  local copies, waits for them, and re-layouts  27.6 us (12%)
    ppermute x45, waiting for transfers between devices, swap(): lax.ppermute(value, axis, [(i, i ^ mask) for i in range(lax.axis_size(axi...  81.3 us
    ppermute x45, starting transfers between devices, swap(): lax.ppermute(value, axis, [(i, i ^ mask) for i in range(lax.axis_size(axi...  74.5 us
    unnamed x89, local copies, waits for them, and re-layouts  23.5 us
    pallas_call x4, Pallas kernels, second(): call(second_kernel, 'mix_0_rotate_1', (n // STEP,), [both, both, pl.Block...  12.8 us
    pallas_call x4, Pallas kernels, first(): call(first_kernel, 'rotate_0', (n // STEP,), [pl.BlockSpec((W, W), lambda...  8.38 us
    pallas_call x4, Pallas kernels, third(): call(third_kernel, 'mix_1_rotate_2', (n // STEP,), [one, one, pl.BlockSpe...  8.32 us
    pallas_call x1, Pallas kernels, target(): call(functools.partial(target_kernel, len(parts)), 'target_map', (8,), [p...  7.62 us
    pallas_call x4, Pallas kernels, split(): call(split_kernel, 'mix_2_own_split', (n // STEP,), [pl.BlockSpec((1, STE...  6.61 us
  transfers between devices with their start and end apart: 45, of which 10 were waited for; matrix products, arithmetic and copies ran while one was open for 2% of the time, Pallas kernels for 18%

profile of v1, /device:TPU:0, one launch (start us, length us, event | category | flops | bytes accessed | tf_op | source)
XLA Modules:
  0.0 238.5 jit_solution(6564065489540133881)
XLA Ops:
  0.0 2.8 %copy-done.1 = bf16[3,32,128,256]{3,2,1,0:T(8,128)(2,1)S(1)} copy-done((bf16[3,32,128,256]{3,2,1,0:T(8,128)(2,1)S(1)}, bf16[3,32,128,256]{3,2,1,0:T(8,128)(2,1)}, u32[]{:S(2)}) %copy-start.1) | copy-done | bytes 6291480
  2.8 2.2 copy-done.3
  5.9 2.3 rotate_0.4.own
  8.2 2.3 rotate_0.5.own
  11.0 2.3 rotate_0.6.own
  17.0 2.3 dynamic-slice_bitcast_fusion
  19.3 2.0 collective-permute-start.2
  23.0 4.5 %masked_weights.1.w = bf16[4,512,256]{2,1,0:T(8,128)(2,1)S(1)} custom-call(s32[5]{0:T(128)S(1)} %stack.23.meta, s32[24]{0:T(128)S(1)} %reshape.24.pattern, bf16[3,2,2,256,256]{4,3,2,1,0:T(8,128)(2,1)S(1)} %copy-done.6), custom_call_target="tpu_custom_call" | custom-call | bytes 2097152 | tf_op jit(solution)/shard_map/masked_weights/pallas_call | solution.py:83
  27.5 2.8 %copy-done.2 = bf16[3,32,128,256]{3,2,1,0:T(8,128)(2,1)S(1)} copy-done((bf16[3,32,128,256]{3,2,1,0:T(8,128)(2,1)S(1)}, bf16[3,32,128,256]{3,2,1,0:T(8,128)(2,1)}, u32[]{:S(2)}) %copy-start.2) | copy-done | bytes 6291480
  30.3 3.2 %mix_0_rotate_1.4 = (bf16[4,128,512]{2,1,0:T(8,128)(2,1)S(1)}, bf16[4,128,512]{2,1,0:T(8,128)(2,1)S(1)}) custom-call(s32[5]{0:T(128)S(1)} %stack.23.meta, bf16[2,4,128,512]{3,2,1,0:T(8,128)(2,1)} %rotate_0.4.own, bf16[2,4,128,512]{3,2,1,0:T(8,128)(2,1)} %collective-permute-done.other, bf16[4,512,256]{2,1,0:T(8,128)(2,1)S(1)} %masked_weights.1.w, ...), custom_call_target="tpu_custom_call" | custom-call | flops 800000000 | bytes 4000000 | tf_op jit(solution)/shard_map/mix_0_rotate_1/pallas_call | solution.py:149
  33.6 3.2 %mix_0_rotate_1.5 = (bf16[4,128,512]{2,1,0:T(8,128)(2,1)S(1)}, bf16[4,128,512]{2,1,0:T(8,128)(2,1)S(1)}) custom-call(s32[5]{0:T(128)S(1)} %stack.23.meta, bf16[2,4,128,512]{3,2,1,0:T(8,128)(2,1)} %rotate_0.5.own, bf16[2,4,128,512]{3,2,1,0:T(8,128)(2,1)} %collective-permute-done.12.other, bf16[4,512,256]{2,1,0:T(8,128)(2,1)S(1)} %masked_weights.1.w, ...), custom_call_target="tpu_custom_call" | custom-call | flops 800000000 | bytes 4000000 | tf_op jit(solution)/shard_map/mix_0_rotate_1/pallas_call | solution.py:149
  36.9 2.1 collective-permute-start.13
  39.0 3.2 %mix_0_rotate_1.6 = (bf16[4,128,512]{2,1,0:T(8,128)(2,1)S(1)}, bf16[4,128,512]{2,1,0:T(8,128)(2,1)S(1)}) custom-call(s32[5]{0:T(128)S(1)} %stack.23.meta, bf16[2,4,128,512]{3,2,1,0:T(8,128)(2,1)} %rotate_0.6.own, bf16[2,4,128,512]{3,2,1,0:T(8,128)(2,1)} %collective-permute-done.23.other, bf16[4,512,256]{2,1,0:T(8,128)(2,1)S(1)} %masked_weights.1.w, ...), custom_call_target="tpu_custom_call" | custom-call | flops 800000000 | bytes 4000000 | tf_op jit(solution)/shard_map/mix_0_rotate_1/pallas_call | solution.py:149
  42.3 3.1 %mix_0_rotate_1.7 = (bf16[4,128,512]{2,1,0:T(8,128)(2,1)S(1)}, bf16[4,128,512]{2,1,0:T(8,128)(2,1)S(1)}) custom-call(s32[5]{0:T(128)S(1)} %stack.23.meta, bf16[2,4,128,512]{3,2,1,0:T(8,128)(2,1)S(1)} %rotate_0.7.own, bf16[2,4,128,512]{3,2,1,0:T(8,128)(2,1)} %collective-permute-done.34.other, bf16[4,512,256]{2,1,0:T(8,128)(2,1)S(1)} %masked_weights.1.w, ...), custom_call_target="tpu_custom_call" | custom-call | flops 800000000 | bytes 4000000 | tf_op jit(solution)/shard_map/mix_0_rotate_1/pallas_call | solution.py:149
  45.4 2.1 collective-permute-start.35
  47.5 9.2 %collective-permute-done.1.other = bf16[4,128,512]{2,1,0:T(8,128)(2,1)S(1)} collective-permute-done((bf16[4,128,512]{2,1,0:T(8,128)(2,1)S(1)}, bf16[4,128,512]{2,1,0:T(8,128)(2,1)S(1)}, u32[]{:S(2)}, u32[]{:S(2)}) %collective-permute-start.1) | collective-permute-done | bytes 524320 | tf_op jit(solution)/shard_map/ppermute | solution.py:284
  56.7 2.1 mix_1_rotate_2.4.own
  58.8 4.2 %collective-permute-start.3 = (bf16[2,4,128,512]{3,2,1,0:T(8,128)(2,1)S(1)}, bf16[2,4,128,512]{3,2,1,0:T(8,128)(2,1)S(1)}, u32[]{:S(2)}, u32[]{:S(2)}) collective-permute-start(bf16[2,4,128,512]{3,2,1,0:T(8,128)(2,1)S(1)} %mix_1_rotate_2.4.own), channel_id=1, source_target_pairs={{0,48},{8,56},{16,32},{24,40},{32,16},{40,24},{48,0},{56,8},{64,11... | collective-permute-start | bytes 3145736 | tf_op jit(solution)/shard_map/ppermute | solution.py:284
  63.1 4.9 %collective-permute-done.13.other = bf16[4,128,512]{2,1,0:T(8,128)(2,1)S(1)} collective-permute-done((bf16[4,128,512]{2,1,0:T(8,128)(2,1)S(1)}, bf16[4,128,512]{2,1,0:T(8,128)(2,1)S(1)}, u32[]{:S(2)}, u32[]{:S(2)}) %collective-permute-start.13) | collective-permute-done | bytes 524320 | tf_op jit(solution)/shard_map/ppermute | solution.py:284
  68.0 2.1 mix_1_rotate_2.5.own
  70.1 4.4 %collective-permute-start.14 = (bf16[2,4,128,512]{3,2,1,0:T(8,128)(2,1)S(1)}, bf16[2,4,128,512]{3,2,1,0:T(8,128)(2,1)S(1)}, u32[]{:S(2)}, u32[]{:S(2)}) collective-permute-start(bf16[2,4,128,512]{3,2,1,0:T(8,128)(2,1)S(1)} %mix_1_rotate_2.5.own), channel_id=1, source_target_pairs={{0,48},{8,56},{16,32},{24,40},{32,16},{40,24},{48,0},{56,8},{64,11... | collective-permute-start | bytes 3145736 | tf_op jit(solution)/shard_map/ppermute | solution.py:284
  74.5 4.7 %collective-permute-done.24.other = bf16[4,128,512]{2,1,0:T(8,128)(2,1)S(1)} collective-permute-done((bf16[4,128,512]{2,1,0:T(8,128)(2,1)S(1)}, bf16[4,128,512]{2,1,0:T(8,128)(2,1)S(1)}, u32[]{:S(2)}, u32[]{:S(2)}) %collective-permute-start.24) | collective-permute-done | bytes 524320 | tf_op jit(solution)/shard_map/ppermute | solution.py:284
  79.2 2.1 mix_1_rotate_2.6.own
  81.3 4.2 %collective-permute-start.25 = (bf16[2,4,128,512]{3,2,1,0:T(8,128)(2,1)S(1)}, bf16[2,4,128,512]{3,2,1,0:T(8,128)(2,1)S(1)}, u32[]{:S(2)}, u32[]{:S(2)}) collective-permute-start(bf16[2,4,128,512]{3,2,1,0:T(8,128)(2,1)S(1)} %mix_1_rotate_2.6.own), channel_id=1, source_target_pairs={{0,48},{8,56},{16,32},{24,40},{32,16},{40,24},{48,0},{56,8},{64,11... | collective-permute-start | bytes 3145736 | tf_op jit(solution)/shard_map/ppermute | solution.py:284
  85.5 4.3 %collective-permute-done.35.other = bf16[4,128,512]{2,1,0:T(8,128)(2,1)S(1)} collective-permute-done((bf16[4,128,512]{2,1,0:T(8,128)(2,1)S(1)}, bf16[4,128,512]{2,1,0:T(8,128)(2,1)S(1)}, u32[]{:S(2)}, u32[]{:S(2)}) %collective-permute-start.35) | collective-permute-done | bytes 524320 | tf_op jit(solution)/shard_map/ppermute | solution.py:284
  89.8 2.1 mix_1_rotate_2.7.own
  91.9 3.9 %collective-permute-start.36 = (bf16[2,4,128,512]{3,2,1,0:T(8,128)(2,1)S(1)}, bf16[2,4,128,512]{3,2,1,0:T(8,128)(2,1)S(1)}, u32[]{:S(2)}, u32[]{:S(2)}) collective-permute-start(bf16[2,4,128,512]{3,2,1,0:T(8,128)(2,1)S(1)} %mix_1_rotate_2.7.own), channel_id=1, source_target_pairs={{0,48},{8,56},{16,32},{24,40},{32,16},{40,24},{48,0},{56,8},{64,11... | collective-permute-start | bytes 3145736 | tf_op jit(solution)/shard_map/ppermute | solution.py:284
  96.6 13.1 %collective-permute-done.14.other = bf16[2,4,128,512]{3,2,1,0:T(8,128)(2,1)S(1)} collective-permute-done((bf16[2,4,128,512]{3,2,1,0:T(8,128)(2,1)S(1)}, bf16[2,4,128,512]{3,2,1,0:T(8,128)(2,1)S(1)}, u32[]{:S(2)}, u32[]{:S(2)}) %collective-permute-start.14) | collective-permute-done | bytes 1048608 | tf_op jit(solution)/shard_map/ppermute | solution.py:284
  110.3 21.8 %collective-permute-done.25.other = bf16[2,4,128,512]{3,2,1,0:T(8,128)(2,1)S(1)} collective-permute-done((bf16[2,4,128,512]{3,2,1,0:T(8,128)(2,1)S(1)}, bf16[2,4,128,512]{3,2,1,0:T(8,128)(2,1)S(1)}, u32[]{:S(2)}, u32[]{:S(2)}) %collective-permute-start.25) | collective-permute-done | bytes 1048608 | tf_op jit(solution)/shard_map/ppermute | solution.py:284
  132.8 19.2 %collective-permute-done.36.other = bf16[2,4,128,512]{3,2,1,0:T(8,128)(2,1)S(1)} collective-permute-done((bf16[2,4,128,512]{3,2,1,0:T(8,128)(2,1)S(1)}, bf16[2,4,128,512]{3,2,1,0:T(8,128)(2,1)S(1)}, u32[]{:S(2)}, u32[]{:S(2)}) %collective-permute-start.36) | collective-permute-done | bytes 1048608 | tf_op jit(solution)/shard_map/ppermute | solution.py:284
  155.7 2.7 %collective-permute-start.6 = (bf16[2,4,16,512]{3,2,1,0:T(8,128)(2,1)S(1)}, bf16[2,4,16,512]{3,2,1,0:T(8,128)(2,1)S(1)}, u32[]{:S(2)}, u32[]{:S(2)}) collective-permute-start(bf16[2,4,16,512]{3,2,1,0:T(8,128)(2,1)S(1)} %get-tuple-element.49), channel_id=1, source_target_pairs={{0,2},{1,3},{2,0},{3,1},{4,6},{5,7},{6,4},{7,5},{8,10},{9,11},{10,... | collective-permute-start | bytes 393224 | tf_op jit(solution)/shard_map/ppermute | solution.py:284
  158.9 1.9 mix_2_own_split.5
  162.5 1.7 collective-permute-done.37.came
  164.2 2.5 %collective-permute-start.9 = (bf16[2,4,16,512]{3,2,1,0:T(8,128)(2,1)S(1)}, bf16[2,4,16,512]{3,2,1,0:T(8,128)(2,1)S(1)}, u32[]{:S(2)}, u32[]{:S(2)}) collective-permute-start(bf16[2,4,16,512]{3,2,1,0:T(8,128)(2,1)S(1)} %get-tuple-element.52), channel_id=1, source_target_pairs={{0,5},{1,4},{2,7},{3,6},{4,1},{5,0},{6,3},{7,2},{8,13},{9,12},{10,... | collective-permute-start | bytes 393224 | tf_op jit(solution)/shard_map/ppermute | solution.py:284
  166.7 2.6 %collective-permute-start.10 = (bf16[2,4,16,512]{3,2,1,0:T(8,128)(2,1)S(1)}, bf16[2,4,16,512]{3,2,1,0:T(8,128)(2,1)S(1)}, u32[]{:S(2)}, u32[]{:S(2)}) collective-permute-start(bf16[2,4,16,512]{3,2,1,0:T(8,128)(2,1)S(1)} %get-tuple-element.53), channel_id=1, source_target_pairs={{0,6},{1,7},{2,4},{3,5},{4,2},{5,3},{6,0},{7,1},{8,14},{9,15},{10,... | collective-permute-start | bytes 393224 | tf_op jit(solution)/shard_map/ppermute | solution.py:284
  171.1 3.9 %collective-permute-start.17 = (bf16[2,4,16,512]{3,2,1,0:T(8,128)(2,1)S(1)}, bf16[2,4,16,512]{3,2,1,0:T(8,128)(2,1)S(1)}, u32[]{:S(2)}, u32[]{:S(2)}) collective-permute-start(bf16[2,4,16,512]{3,2,1,0:T(8,128)(2,1)S(1)} %get-tuple-element.59), channel_id=1, source_target_pairs={{0,2},{1,3},{2,0},{3,1},{4,6},{5,7},{6,4},{7,5},{8,10},{9,11},{10,... | collective-permute-start | bytes 393224 | tf_op jit(solution)/shard_map/ppermute | solution.py:284
  180.1 2.4 %collective-permute-start.21 = (bf16[2,4,16,512]{3,2,1,0:T(8,128)(2,1)S(1)}, bf16[2,4,16,512]{3,2,1,0:T(8,128)(2,1)S(1)}, u32[]{:S(2)}, u32[]{:S(2)}) collective-permute-start(bf16[2,4,16,512]{3,2,1,0:T(8,128)(2,1)S(1)} %get-tuple-element.63), channel_id=1, source_target_pairs={{0,6},{1,7},{2,4},{3,5},{4,2},{5,3},{6,0},{7,1},{8,14},{9,15},{10,... | collective-permute-start | bytes 393224 | tf_op jit(solution)/shard_map/ppermute | solution.py:284
  182.5 2.0 mix_2_own_split.6
  187.8 3.3 %collective-permute-start.22 = (bf16[2,4,16,512]{3,2,1,0:T(8,128)(2,1)}, bf16[2,4,16,512]{3,2,1,0:T(8,128)(2,1)}, u32[]{:S(2)}, u32[]{:S(2)}) collective-permute-start(bf16[2,4,16,512]{3,2,1,0:T(8,128)(2,1)} %get-tuple-element.64), channel_id=1, source_target_pairs={{0,7},{1,6},{2,5},{3,4},{4,3},{5,2},{6,1},{7,0},{8,15},{9,14},{10,... | collective-permute-start | bytes 393224 | tf_op jit(solution)/shard_map/ppermute | solution.py:284
  192.5 3.0 %collective-permute-start.28 = (bf16[2,4,16,512]{3,2,1,0:T(8,128)(2,1)}, bf16[2,4,16,512]{3,2,1,0:T(8,128)(2,1)}, u32[]{:S(2)}, u32[]{:S(2)}) collective-permute-start(bf16[2,4,16,512]{3,2,1,0:T(8,128)(2,1)} %get-tuple-element.69), channel_id=1, source_target_pairs={{0,2},{1,3},{2,0},{3,1},{4,6},{5,7},{6,4},{7,5},{8,10},{9,11},{10,... | collective-permute-start | bytes 393224 | tf_op jit(solution)/shard_map/ppermute | solution.py:284
  196.2 1.7 collective-permute-start.29
  201.6 3.3 %collective-permute-start.32 = (bf16[2,4,16,512]{3,2,1,0:T(8,128)(2,1)}, bf16[2,4,16,512]{3,2,1,0:T(8,128)(2,1)S(1)}, u32[]{:S(2)}, u32[]{:S(2)}) collective-permute-start(bf16[2,4,16,512]{3,2,1,0:T(8,128)(2,1)} %copy-done.40), channel_id=1, source_target_pairs={{0,6},{1,7},{2,4},{3,5},{4,2},{5,3},{6,0},{7,1},{8,14},{9,15},{10,... | collective-permute-start | bytes 393224 | tf_op jit(solution)/shard_map/ppermute | solution.py:284
  204.9 3.1 %collective-permute-start.33 = (bf16[2,4,16,512]{3,2,1,0:T(8,128)(2,1)}, bf16[2,4,16,512]{3,2,1,0:T(8,128)(2,1)S(1)}, u32[]{:S(2)}, u32[]{:S(2)}) collective-permute-start(bf16[2,4,16,512]{3,2,1,0:T(8,128)(2,1)} %copy-done.39), channel_id=1, source_target_pairs={{0,7},{1,6},{2,5},{3,4},{4,3},{5,2},{6,1},{7,0},{8,15},{9,14},{10,... | collective-permute-start | bytes 393224 | tf_op jit(solution)/shard_map/ppermute | solution.py:284
  208.1 3.0 %collective-permute-start.39 = (bf16[2,4,16,512]{3,2,1,0:T(8,128)(2,1)S(1)}, bf16[2,4,16,512]{3,2,1,0:T(8,128)(2,1)S(1)}, u32[]{:S(2)}, u32[]{:S(2)}) collective-permute-start(bf16[2,4,16,512]{3,2,1,0:T(8,128)(2,1)S(1)} %get-tuple-element.79), channel_id=1, source_target_pairs={{0,2},{1,3},{2,0},{3,1},{4,6},{5,7},{6,4},{7,5},{8,10},{9,11},{10,... | collective-permute-start | bytes 393224 | tf_op jit(solution)/shard_map/ppermute | solution.py:284
  211.1 1.7 collective-permute-start.40
  213.5 2.1 collective-permute-start.42
  215.6 4.8 %collective-permute-start.43 = (bf16[2,4,16,512]{3,2,1,0:T(8,128)(2,1)S(1)}, bf16[2,4,16,512]{3,2,1,0:T(8,128)(2,1)S(1)}, u32[]{:S(2)}, u32[]{:S(2)}) collective-permute-start(bf16[2,4,16,512]{3,2,1,0:T(8,128)(2,1)S(1)} %get-tuple-element.83), channel_id=1, source_target_pairs={{0,6},{1,7},{2,4},{3,5},{4,2},{5,3},{6,0},{7,1},{8,14},{9,15},{10,... | collective-permute-start | bytes 393224 | tf_op jit(solution)/shard_map/ppermute | solution.py:284
  230.8 7.6 %target_map.1 = f32[256,64,128]{2,1,0:T(8,128)} custom-call(bf16[256,256]{1,0:T(8,128)(2,1)S(1)} %fusion.t_map, bf16[16,64,512]{2,1,0:T(8,128)(2,1)S(1)} %gather_frequencies.4.refs_0_, bf16[16,64,512]{2,1,0:T(8,128)(2,1)S(1)} %gather_frequencies.5.refs_1_, bf16[16,64,512]{2,1,0:T(8,128)(2,1)S(1)} %gather_frequencies.6.refs_2_, ...), custom_call_target="tpu_custom_call" | custom-call | flops 1000000000 | bytes 12582912 | tf_op jit(solution)/shard_map/target_map/pallas_call | solution.py:274
  (163 shorter events, 41.6 us)
Async XLA Ops:
  0.0 220.4 %copy-start = (bf16[256,256]{1,0:T(8,128)(2,1)S(1)}, bf16[256,256]{1,0:T(8,128)(2,1)}, u32[]{:S(2)}) copy-start(bf16[256,256]{1,0:T(8,128)(2,1)} %param.12) | copy-start | bytes 393220
  8.2 19.3 %collective-permute-start = (bf16[2,4,128,512]{3,2,1,0:T(8,128)(2,1)}, bf16[2,4,128,512]{3,2,1,0:T(8,128)(2,1)}, u32[]{:S(2)}, u32[]{:S(2)}) collective-permute-start(bf16[2,4,128,512]{3,2,1,0:T(8,128)(2,1)} %rotate_0.4.own), channel_id=1, source_target_pairs={{0,8},{8,0},{16,24},{24,16},{32,40},{40,32},{48,56},{56,48},{64,72... | collective-permute-start | bytes 3145736 | tf_op jit(solution)/shard_map/ppermute | solution.py:284
  10.5 23.2 %collective-permute-start.12 = (bf16[2,4,128,512]{3,2,1,0:T(8,128)(2,1)}, bf16[2,4,128,512]{3,2,1,0:T(8,128)(2,1)}, u32[]{:S(2)}, u32[]{:S(2)}) collective-permute-start(bf16[2,4,128,512]{3,2,1,0:T(8,128)(2,1)} %rotate_0.5.own), channel_id=1, source_target_pairs={{0,8},{8,0},{16,24},{24,16},{32,40},{40,32},{48,56},{56,48},{64,72... | collective-permute-start | bytes 3145736 | tf_op jit(solution)/shard_map/ppermute | solution.py:284
  13.3 25.7 %collective-permute-start.23 = (bf16[2,4,128,512]{3,2,1,0:T(8,128)(2,1)}, bf16[2,4,128,512]{3,2,1,0:T(8,128)(2,1)}, u32[]{:S(2)}, u32[]{:S(2)}) collective-permute-start(bf16[2,4,128,512]{3,2,1,0:T(8,128)(2,1)} %rotate_0.6.own), channel_id=1, source_target_pairs={{0,8},{8,0},{16,24},{24,16},{32,40},{40,32},{48,56},{56,48},{64,72... | collective-permute-start | bytes 3145736 | tf_op jit(solution)/shard_map/ppermute | solution.py:284
  14.8 27.5 %collective-permute-start.34 = (bf16[2,4,128,512]{3,2,1,0:T(8,128)(2,1)S(1)}, bf16[2,4,128,512]{3,2,1,0:T(8,128)(2,1)}, u32[]{:S(2)}, u32[]{:S(2)}) collective-permute-start(bf16[2,4,128,512]{3,2,1,0:T(8,128)(2,1)S(1)} %rotate_0.7.own), channel_id=1, source_target_pairs={{0,8},{8,0},{16,24},{24,16},{32,40},{40,32},{48,56},{56,48},{64,72... | collective-permute-start | bytes 3145736 | tf_op jit(solution)/shard_map/ppermute | solution.py:284
  19.3 28.2 %collective-permute-start.2 = (bf16[16,128,256]{2,1,0:T(8,128)(2,1)}, bf16[16,128,256]{2,1,0:T(8,128)(2,1)S(1)}, u32[]{:S(2)}, u32[]{:S(2)}) collective-permute-start(bf16[16,128,256]{2,1,0:T(8,128)(2,1)} %dynamic-slice_bitcast_fusion), channel_id=1, source_target_pairs={{0,16},{8,24},{16,0},{24,8},{32,48},{40,56},{48,32},{56,40},{64,80... | collective-permute-start | bytes 3145736 | tf_op jit(solution)/shard_map/ppermute | solution.py:284
  33.5 23.2 %collective-permute-start.1 = (bf16[4,128,512]{2,1,0:T(8,128)(2,1)S(1)}, bf16[4,128,512]{2,1,0:T(8,128)(2,1)S(1)}, u32[]{:S(2)}, u32[]{:S(2)}) collective-permute-start(bf16[4,128,512]{2,1,0:T(8,128)(2,1)S(1)} %get-tuple-element.46), channel_id=1, source_target_pairs={{0,16},{8,24},{16,0},{24,8},{32,48},{40,56},{48,32},{56,40},{64,80... | collective-permute-start | bytes 1572872 | tf_op jit(solution)/shard_map/ppermute | solution.py:284
  36.9 31.1 %collective-permute-start.13 = (bf16[4,128,512]{2,1,0:T(8,128)(2,1)S(1)}, bf16[4,128,512]{2,1,0:T(8,128)(2,1)S(1)}, u32[]{:S(2)}, u32[]{:S(2)}) collective-permute-start(bf16[4,128,512]{2,1,0:T(8,128)(2,1)S(1)} %get-tuple-element.56), channel_id=1, source_target_pairs={{0,16},{8,24},{16,0},{24,8},{32,48},{40,56},{48,32},{56,40},{64,80... | collective-permute-start | bytes 1572872 | tf_op jit(solution)/shard_map/ppermute | solution.py:284
  42.2 37.0 %collective-permute-start.24 = (bf16[4,128,512]{2,1,0:T(8,128)(2,1)S(1)}, bf16[4,128,512]{2,1,0:T(8,128)(2,1)S(1)}, u32[]{:S(2)}, u32[]{:S(2)}) collective-permute-start(bf16[4,128,512]{2,1,0:T(8,128)(2,1)S(1)} %get-tuple-element.66), channel_id=1, source_target_pairs={{0,16},{8,24},{16,0},{24,8},{32,48},{40,56},{48,32},{56,40},{64,80... | collective-permute-start | bytes 1572872 | tf_op jit(solution)/shard_map/ppermute | solution.py:284
  45.4 44.4 %collective-permute-start.35 = (bf16[4,128,512]{2,1,0:T(8,128)(2,1)S(1)}, bf16[4,128,512]{2,1,0:T(8,128)(2,1)S(1)}, u32[]{:S(2)}, u32[]{:S(2)}) collective-permute-start(bf16[4,128,512]{2,1,0:T(8,128)(2,1)S(1)} %get-tuple-element.76), channel_id=1, source_target_pairs={{0,16},{8,24},{16,0},{24,8},{32,48},{40,56},{48,32},{56,40},{64,80... | collective-permute-start | bytes 1572872 | tf_op jit(solution)/shard_map/ppermute | solution.py:284
  58.8 37.0 %collective-permute-start.3 = (bf16[2,4,128,512]{3,2,1,0:T(8,128)(2,1)S(1)}, bf16[2,4,128,512]{3,2,1,0:T(8,128)(2,1)S(1)}, u32[]{:S(2)}, u32[]{:S(2)}) collective-permute-start(bf16[2,4,128,512]{3,2,1,0:T(8,128)(2,1)S(1)} %mix_1_rotate_2.4.own), channel_id=1, source_target_pairs={{0,48},{8,56},{16,32},{24,40},{32,16},{40,24},{48,0},{56,8},{64,11... | collective-permute-start | bytes 3145736 | tf_op jit(solution)/shard_map/ppermute | solution.py:284
  70.1 39.5 %collective-permute-start.14 = (bf16[2,4,128,512]{3,2,1,0:T(8,128)(2,1)S(1)}, bf16[2,4,128,512]{3,2,1,0:T(8,128)(2,1)S(1)}, u32[]{:S(2)}, u32[]{:S(2)}) collective-permute-start(bf16[2,4,128,512]{3,2,1,0:T(8,128)(2,1)S(1)} %mix_1_rotate_2.5.own), channel_id=1, source_target_pairs={{0,48},{8,56},{16,32},{24,40},{32,16},{40,24},{48,0},{56,8},{64,11... | collective-permute-start | bytes 3145736 | tf_op jit(solution)/shard_map/ppermute | solution.py:284
  81.3 50.8 %collective-permute-start.25 = (bf16[2,4,128,512]{3,2,1,0:T(8,128)(2,1)S(1)}, bf16[2,4,128,512]{3,2,1,0:T(8,128)(2,1)S(1)}, u32[]{:S(2)}, u32[]{:S(2)}) collective-permute-start(bf16[2,4,128,512]{3,2,1,0:T(8,128)(2,1)S(1)} %mix_1_rotate_2.6.own), channel_id=1, source_target_pairs={{0,48},{8,56},{16,32},{24,40},{32,16},{40,24},{48,0},{56,8},{64,11... | collective-permute-start | bytes 3145736 | tf_op jit(solution)/shard_map/ppermute | solution.py:284
  91.9 60.2 %collective-permute-start.36 = (bf16[2,4,128,512]{3,2,1,0:T(8,128)(2,1)S(1)}, bf16[2,4,128,512]{3,2,1,0:T(8,128)(2,1)S(1)}, u32[]{:S(2)}, u32[]{:S(2)}) collective-permute-start(bf16[2,4,128,512]{3,2,1,0:T(8,128)(2,1)S(1)} %mix_1_rotate_2.7.own), channel_id=1, source_target_pairs={{0,48},{8,56},{16,32},{24,40},{32,16},{40,24},{48,0},{56,8},{64,11... | collective-permute-start | bytes 3145736 | tf_op jit(solution)/shard_map/ppermute | solution.py:284
  96.5 56.3 %collective-permute-start.4 = (bf16[4,128,512]{2,1,0:T(8,128)(2,1)S(1)}, bf16[4,128,512]{2,1,0:T(8,128)(2,1)S(1)}, u32[]{:S(2)}, u32[]{:S(2)}) collective-permute-start(bf16[4,128,512]{2,1,0:T(8,128)(2,1)S(1)} %mix_2_other.4), channel_id=1, source_target_pairs={{0,16},{8,24},{16,0},{24,8},{32,48},{40,56},{48,32},{56,40},{64,80... | collective-permute-start | bytes 1572872 | tf_op jit(solution)/shard_map/ppermute | solution.py:284
  110.2 48.2 %collective-permute-start.15 = (bf16[4,128,512]{2,1,0:T(8,128)(2,1)S(1)}, bf16[4,128,512]{2,1,0:T(8,128)(2,1)S(1)}, u32[]{:S(2)}, u32[]{:S(2)}) collective-permute-start(bf16[4,128,512]{2,1,0:T(8,128)(2,1)S(1)} %mix_2_other.5), channel_id=1, source_target_pairs={{0,16},{8,24},{16,0},{24,8},{32,48},{40,56},{48,32},{56,40},{64,80... | collective-permute-start | bytes 1572872 | tf_op jit(solution)/shard_map/ppermute | solution.py:284
  132.7 28.1 %collective-permute-start.26 = (bf16[4,128,512]{2,1,0:T(8,128)(2,1)S(1)}, bf16[4,128,512]{2,1,0:T(8,128)(2,1)S(1)}, u32[]{:S(2)}, u32[]{:S(2)}) collective-permute-start(bf16[4,128,512]{2,1,0:T(8,128)(2,1)S(1)} %mix_2_other.6), channel_id=1, source_target_pairs={{0,16},{8,24},{16,0},{24,8},{32,48},{40,56},{48,32},{56,40},{64,80... | collective-permute-start | bytes 1572872 | tf_op jit(solution)/shard_map/ppermute | solution.py:284
  152.7 11.5 %collective-permute-start.37 = (bf16[4,128,512]{2,1,0:T(8,128)(2,1)S(1)}, bf16[4,128,512]{2,1,0:T(8,128)(2,1)S(1)}, u32[]{:S(2)}, u32[]{:S(2)}) collective-permute-start(bf16[4,128,512]{2,1,0:T(8,128)(2,1)S(1)} %mix_2_other.7), channel_id=1, source_target_pairs={{0,16},{8,24},{16,0},{24,8},{32,48},{40,56},{48,32},{56,40},{64,80... | collective-permute-start | bytes 1572872 | tf_op jit(solution)/shard_map/ppermute | solution.py:284
  154.1 12.6 %collective-permute-start.5 = (bf16[2,4,16,512]{3,2,1,0:T(8,128)(2,1)S(1)}, bf16[2,4,16,512]{3,2,1,0:T(8,128)(2,1)S(1)}, u32[]{:S(2)}, u32[]{:S(2)}) collective-permute-start(bf16[2,4,16,512]{3,2,1,0:T(8,128)(2,1)S(1)} %get-tuple-element.48), channel_id=1, source_target_pairs={{0,1},{1,0},{2,3},{3,2},{4,5},{5,4},{6,7},{7,6},{8,9},{9,8},{10,11... | collective-permute-start | bytes 393224 | tf_op jit(solution)/shard_map/ppermute | solution.py:284
  155.7 13.6 %collective-permute-start.6 = (bf16[2,4,16,512]{3,2,1,0:T(8,128)(2,1)S(1)}, bf16[2,4,16,512]{3,2,1,0:T(8,128)(2,1)S(1)}, u32[]{:S(2)}, u32[]{:S(2)}) collective-permute-start(bf16[2,4,16,512]{3,2,1,0:T(8,128)(2,1)S(1)} %get-tuple-element.49), channel_id=1, source_target_pairs={{0,2},{1,3},{2,0},{3,1},{4,6},{5,7},{6,4},{7,5},{8,10},{9,11},{10,... | collective-permute-start | bytes 393224 | tf_op jit(solution)/shard_map/ppermute | solution.py:284
  158.4 12.4 %collective-permute-start.7 = (bf16[2,4,16,512]{3,2,1,0:T(8,128)(2,1)S(1)}, bf16[2,4,16,512]{3,2,1,0:T(8,128)(2,1)S(1)}, u32[]{:S(2)}, u32[]{:S(2)}) collective-permute-start(bf16[2,4,16,512]{3,2,1,0:T(8,128)(2,1)S(1)} %get-tuple-element.50), channel_id=1, source_target_pairs={{0,3},{1,2},{2,1},{3,0},{4,7},{5,6},{6,5},{7,4},{8,11},{9,10},{10,... | collective-permute-start | bytes 393224 | tf_op jit(solution)/shard_map/ppermute | solution.py:284
  160.8 50.3 %copy-start.43 = (s32[256]{0:T(256)S(1)}, s32[256]{0:T(256)}, u32[]{:S(2)}) copy-start(s32[256]{0:T(256)} %constant.33.clone) | copy-start | bytes 3076
  160.8 59.8 %copy-start.5 = (bf16[256,256]{1,0:T(8,128)(2,1)S(1)}, bf16[256,256]{1,0:T(8,128)(2,1)}, u32[]{:S(2)}) copy-start(bf16[256,256]{1,0:T(8,128)(2,1)} %constant.32.clone.shuffle) | copy-start | bytes 393220
  160.8 10.2 %collective-permute-start.8 = (bf16[2,4,16,512]{3,2,1,0:T(8,128)(2,1)S(1)}, bf16[2,4,16,512]{3,2,1,0:T(8,128)(2,1)S(1)}, u32[]{:S(2)}, u32[]{:S(2)}) collective-permute-start(bf16[2,4,16,512]{3,2,1,0:T(8,128)(2,1)S(1)} %get-tuple-element.51), channel_id=1, source_target_pairs={{0,4},{1,5},{2,6},{3,7},{4,0},{5,1},{6,2},{7,3},{8,12},{9,13},{10,... | collective-permute-start | bytes 393224 | tf_op jit(solution)/shard_map/ppermute | solution.py:284
  164.2 10.9 %collective-permute-start.9 = (bf16[2,4,16,512]{3,2,1,0:T(8,128)(2,1)S(1)}, bf16[2,4,16,512]{3,2,1,0:T(8,128)(2,1)S(1)}, u32[]{:S(2)}, u32[]{:S(2)}) collective-permute-start(bf16[2,4,16,512]{3,2,1,0:T(8,128)(2,1)S(1)} %get-tuple-element.52), channel_id=1, source_target_pairs={{0,5},{1,4},{2,7},{3,6},{4,1},{5,0},{6,3},{7,2},{8,13},{9,12},{10,... | collective-permute-start | bytes 393224 | tf_op jit(solution)/shard_map/ppermute | solution.py:284
  166.7 9.5 %collective-permute-start.10 = (bf16[2,4,16,512]{3,2,1,0:T(8,128)(2,1)S(1)}, bf16[2,4,16,512]{3,2,1,0:T(8,128)(2,1)S(1)}, u32[]{:S(2)}, u32[]{:S(2)}) collective-permute-start(bf16[2,4,16,512]{3,2,1,0:T(8,128)(2,1)S(1)} %get-tuple-element.53), channel_id=1, source_target_pairs={{0,6},{1,7},{2,4},{3,5},{4,2},{5,3},{6,0},{7,1},{8,14},{9,15},{10,... | collective-permute-start | bytes 393224 | tf_op jit(solution)/shard_map/ppermute | solution.py:284
  169.3 10.1 %collective-permute-start.11 = (bf16[2,4,16,512]{3,2,1,0:T(8,128)(2,1)S(1)}, bf16[2,4,16,512]{3,2,1,0:T(8,128)(2,1)S(1)}, u32[]{:S(2)}, u32[]{:S(2)}) collective-permute-start(bf16[2,4,16,512]{3,2,1,0:T(8,128)(2,1)S(1)} %get-tuple-element.54), channel_id=1, source_target_pairs={{0,7},{1,6},{2,5},{3,4},{4,3},{5,2},{6,1},{7,0},{8,15},{9,14},{10,... | collective-permute-start | bytes 393224 | tf_op jit(solution)/shard_map/ppermute | solution.py:284
  170.8 9.3 %collective-permute-start.16 = (bf16[2,4,16,512]{3,2,1,0:T(8,128)(2,1)S(1)}, bf16[2,4,16,512]{3,2,1,0:T(8,128)(2,1)S(1)}, u32[]{:S(2)}, u32[]{:S(2)}) collective-permute-start(bf16[2,4,16,512]{3,2,1,0:T(8,128)(2,1)S(1)} %get-tuple-element.58), channel_id=1, source_target_pairs={{0,1},{1,0},{2,3},{3,2},{4,5},{5,4},{6,7},{7,6},{8,9},{9,8},{10,11... | collective-permute-start | bytes 393224 | tf_op jit(solution)/shard_map/ppermute | solution.py:284
  171.1 16.1 %collective-permute-start.17 = (bf16[2,4,16,512]{3,2,1,0:T(8,128)(2,1)S(1)}, bf16[2,4,16,512]{3,2,1,0:T(8,128)(2,1)S(1)}, u32[]{:S(2)}, u32[]{:S(2)}) collective-permute-start(bf16[2,4,16,512]{3,2,1,0:T(8,128)(2,1)S(1)} %get-tuple-element.59), channel_id=1, source_target_pairs={{0,2},{1,3},{2,0},{3,1},{4,6},{5,7},{6,4},{7,5},{8,10},{9,11},{10,... | collective-permute-start | bytes 393224 | tf_op jit(solution)/shard_map/ppermute | solution.py:284
  175.0 16.1 %collective-permute-start.18 = (bf16[2,4,16,512]{3,2,1,0:T(8,128)(2,1)S(1)}, bf16[2,4,16,512]{3,2,1,0:T(8,128)(2,1)S(1)}, u32[]{:S(2)}, u32[]{:S(2)}) collective-permute-start(bf16[2,4,16,512]{3,2,1,0:T(8,128)(2,1)S(1)} %get-tuple-element.60), channel_id=1, source_target_pairs={{0,3},{1,2},{2,1},{3,0},{4,7},{5,6},{6,5},{7,4},{8,11},{9,10},{10,... | collective-permute-start | bytes 393224 | tf_op jit(solution)/shard_map/ppermute | solution.py:284
  176.1 15.7 %collective-permute-start.19 = (bf16[2,4,16,512]{3,2,1,0:T(8,128)(2,1)S(1)}, bf16[2,4,16,512]{3,2,1,0:T(8,128)(2,1)S(1)}, u32[]{:S(2)}, u32[]{:S(2)}) collective-permute-start(bf16[2,4,16,512]{3,2,1,0:T(8,128)(2,1)S(1)} %get-tuple-element.61), channel_id=1, source_target_pairs={{0,4},{1,5},{2,6},{3,7},{4,0},{5,1},{6,2},{7,3},{8,12},{9,13},{10,... | collective-permute-start | bytes 393224 | tf_op jit(solution)/shard_map/ppermute | solution.py:284
  179.4 16.1 %collective-permute-start.20 = (bf16[2,4,16,512]{3,2,1,0:T(8,128)(2,1)S(1)}, bf16[2,4,16,512]{3,2,1,0:T(8,128)(2,1)S(1)}, u32[]{:S(2)}, u32[]{:S(2)}) collective-permute-start(bf16[2,4,16,512]{3,2,1,0:T(8,128)(2,1)S(1)} %get-tuple-element.62), channel_id=1, source_target_pairs={{0,5},{1,4},{2,7},{3,6},{4,1},{5,0},{6,3},{7,2},{8,13},{9,12},{10,... | collective-permute-start | bytes 393224 | tf_op jit(solution)/shard_map/ppermute | solution.py:284
  180.1 17.7 %collective-permute-start.21 = (bf16[2,4,16,512]{3,2,1,0:T(8,128)(2,1)S(1)}, bf16[2,4,16,512]{3,2,1,0:T(8,128)(2,1)S(1)}, u32[]{:S(2)}, u32[]{:S(2)}) collective-permute-start(bf16[2,4,16,512]{3,2,1,0:T(8,128)(2,1)S(1)} %get-tuple-element.63), channel_id=1, source_target_pairs={{0,6},{1,7},{2,4},{3,5},{4,2},{5,3},{6,0},{7,1},{8,14},{9,15},{10,... | collective-permute-start | bytes 393224 | tf_op jit(solution)/shard_map/ppermute | solution.py:284
  187.8 13.7 %collective-permute-start.22 = (bf16[2,4,16,512]{3,2,1,0:T(8,128)(2,1)}, bf16[2,4,16,512]{3,2,1,0:T(8,128)(2,1)}, u32[]{:S(2)}, u32[]{:S(2)}) collective-permute-start(bf16[2,4,16,512]{3,2,1,0:T(8,128)(2,1)} %get-tuple-element.64), channel_id=1, source_target_pairs={{0,7},{1,6},{2,5},{3,4},{4,3},{5,2},{6,1},{7,0},{8,15},{9,14},{10,... | collective-permute-start | bytes 393224 | tf_op jit(solution)/shard_map/ppermute | solution.py:284
  191.8 9.8 %collective-permute-start.27 = (bf16[2,4,16,512]{3,2,1,0:T(8,128)(2,1)}, bf16[2,4,16,512]{3,2,1,0:T(8,128)(2,1)}, u32[]{:S(2)}, u32[]{:S(2)}) collective-permute-start(bf16[2,4,16,512]{3,2,1,0:T(8,128)(2,1)} %get-tuple-element.68), channel_id=1, source_target_pairs={{0,1},{1,0},{2,3},{3,2},{4,5},{5,4},{6,7},{7,6},{8,9},{9,8},{10,11... | collective-permute-start | bytes 393224 | tf_op jit(solution)/shard_map/ppermute | solution.py:284
  192.5 12.5 %collective-permute-start.28 = (bf16[2,4,16,512]{3,2,1,0:T(8,128)(2,1)}, bf16[2,4,16,512]{3,2,1,0:T(8,128)(2,1)}, u32[]{:S(2)}, u32[]{:S(2)}) collective-permute-start(bf16[2,4,16,512]{3,2,1,0:T(8,128)(2,1)} %get-tuple-element.69), channel_id=1, source_target_pairs={{0,2},{1,3},{2,0},{3,1},{4,6},{5,7},{6,4},{7,5},{8,10},{9,11},{10,... | collective-permute-start | bytes 393224 | tf_op jit(solution)/shard_map/ppermute | solution.py:284
  196.2 11.9 %collective-permute-start.29 = (bf16[2,4,16,512]{3,2,1,0:T(8,128)(2,1)}, bf16[2,4,16,512]{3,2,1,0:T(8,128)(2,1)}, u32[]{:S(2)}, u32[]{:S(2)}) collective-permute-start(bf16[2,4,16,512]{3,2,1,0:T(8,128)(2,1)} %get-tuple-element.70), channel_id=1, source_target_pairs={{0,3},{1,2},{2,1},{3,0},{4,7},{5,6},{6,5},{7,4},{8,11},{9,10},{10,... | collective-permute-start | bytes 393224 | tf_op jit(solution)/shard_map/ppermute | solution.py:284
  198.5 9.6 %collective-permute-start.30 = (bf16[2,4,16,512]{3,2,1,0:T(8,128)(2,1)}, bf16[2,4,16,512]{3,2,1,0:T(8,128)(2,1)}, u32[]{:S(2)}, u32[]{:S(2)}) collective-permute-start(bf16[2,4,16,512]{3,2,1,0:T(8,128)(2,1)} %get-tuple-element.71), channel_id=1, source_target_pairs={{0,4},{1,5},{2,6},{3,7},{4,0},{5,1},{6,2},{7,3},{8,12},{9,13},{10,... | collective-permute-start | bytes 393224 | tf_op jit(solution)/shard_map/ppermute | solution.py:284
  201.5 9.6 %collective-permute-start.31 = (bf16[2,4,16,512]{3,2,1,0:T(8,128)(2,1)}, bf16[2,4,16,512]{3,2,1,0:T(8,128)(2,1)S(1)}, u32[]{:S(2)}, u32[]{:S(2)}) collective-permute-start(bf16[2,4,16,512]{3,2,1,0:T(8,128)(2,1)} %copy-done.41), channel_id=1, source_target_pairs={{0,5},{1,4},{2,7},{3,6},{4,1},{5,0},{6,3},{7,2},{8,13},{9,12},{10,... | collective-permute-start | bytes 393224 | tf_op jit(solution)/shard_map/ppermute | solution.py:284
  201.6 11.3 %collective-permute-start.32 = (bf16[2,4,16,512]{3,2,1,0:T(8,128)(2,1)}, bf16[2,4,16,512]{3,2,1,0:T(8,128)(2,1)S(1)}, u32[]{:S(2)}, u32[]{:S(2)}) collective-permute-start(bf16[2,4,16,512]{3,2,1,0:T(8,128)(2,1)} %copy-done.40), channel_id=1, source_target_pairs={{0,6},{1,7},{2,4},{3,5},{4,2},{5,3},{6,0},{7,1},{8,14},{9,15},{10,... | collective-permute-start | bytes 393224 | tf_op jit(solution)/shard_map/ppermute | solution.py:284
  204.9 8.5 %collective-permute-start.33 = (bf16[2,4,16,512]{3,2,1,0:T(8,128)(2,1)}, bf16[2,4,16,512]{3,2,1,0:T(8,128)(2,1)S(1)}, u32[]{:S(2)}, u32[]{:S(2)}) collective-permute-start(bf16[2,4,16,512]{3,2,1,0:T(8,128)(2,1)} %copy-done.39), channel_id=1, source_target_pairs={{0,7},{1,6},{2,5},{3,4},{4,3},{5,2},{6,1},{7,0},{8,15},{9,14},{10,... | collective-permute-start | bytes 393224 | tf_op jit(solution)/shard_map/ppermute | solution.py:284
  208.1 7.5 %collective-permute-start.38 = (bf16[2,4,16,512]{3,2,1,0:T(8,128)(2,1)S(1)}, bf16[2,4,16,512]{3,2,1,0:T(8,128)(2,1)S(1)}, u32[]{:S(2)}, u32[]{:S(2)}) collective-permute-start(bf16[2,4,16,512]{3,2,1,0:T(8,128)(2,1)S(1)} %get-tuple-element.78), channel_id=1, source_target_pairs={{0,1},{1,0},{2,3},{3,2},{4,5},{5,4},{6,7},{7,6},{8,9},{9,8},{10,11... | collective-permute-start | bytes 393224 | tf_op jit(solution)/shard_map/ppermute | solution.py:284
  208.1 12.3 %collective-permute-start.39 = (bf16[2,4,16,512]{3,2,1,0:T(8,128)(2,1)S(1)}, bf16[2,4,16,512]{3,2,1,0:T(8,128)(2,1)S(1)}, u32[]{:S(2)}, u32[]{:S(2)}) collective-permute-start(bf16[2,4,16,512]{3,2,1,0:T(8,128)(2,1)S(1)} %get-tuple-element.79), channel_id=1, source_target_pairs={{0,2},{1,3},{2,0},{3,1},{4,6},{5,7},{6,4},{7,5},{8,10},{9,11},{10,... | collective-permute-start | bytes 393224 | tf_op jit(solution)/shard_map/ppermute | solution.py:284
  211.1 19.2 %collective-permute-start.40 = (bf16[2,4,16,512]{3,2,1,0:T(8,128)(2,1)S(1)}, bf16[2,4,16,512]{3,2,1,0:T(8,128)(2,1)S(1)}, u32[]{:S(2)}, u32[]{:S(2)}) collective-permute-start(bf16[2,4,16,512]{3,2,1,0:T(8,128)(2,1)S(1)} %get-tuple-element.80), channel_id=1, source_target_pairs={{0,3},{1,2},{2,1},{3,0},{4,7},{5,6},{6,5},{7,4},{8,11},{9,10},{10,... | collective-permute-start | bytes 393224 | tf_op jit(solution)/shard_map/ppermute | solution.py:284
  212.9 17.5 %collective-permute-start.41 = (bf16[2,4,16,512]{3,2,1,0:T(8,128)(2,1)S(1)}, bf16[2,4,16,512]{3,2,1,0:T(8,128)(2,1)S(1)}, u32[]{:S(2)}, u32[]{:S(2)}) collective-permute-start(bf16[2,4,16,512]{3,2,1,0:T(8,128)(2,1)S(1)} %get-tuple-element.81), channel_id=1, source_target_pairs={{0,4},{1,5},{2,6},{3,7},{4,0},{5,1},{6,2},{7,3},{8,12},{9,13},{10,... | collective-permute-start | bytes 393224 | tf_op jit(solution)/shard_map/ppermute | solution.py:284
  213.5 16.9 %collective-permute-start.42 = (bf16[2,4,16,512]{3,2,1,0:T(8,128)(2,1)S(1)}, bf16[2,4,16,512]{3,2,1,0:T(8,128)(2,1)S(1)}, u32[]{:S(2)}, u32[]{:S(2)}) collective-permute-start(bf16[2,4,16,512]{3,2,1,0:T(8,128)(2,1)S(1)} %get-tuple-element.82), channel_id=1, source_target_pairs={{0,5},{1,4},{2,7},{3,6},{4,1},{5,0},{6,3},{7,2},{8,13},{9,12},{10,... | collective-permute-start | bytes 393224 | tf_op jit(solution)/shard_map/ppermute | solution.py:284
  215.6 14.8 %collective-permute-start.43 = (bf16[2,4,16,512]{3,2,1,0:T(8,128)(2,1)S(1)}, bf16[2,4,16,512]{3,2,1,0:T(8,128)(2,1)S(1)}, u32[]{:S(2)}, u32[]{:S(2)}) collective-permute-start(bf16[2,4,16,512]{3,2,1,0:T(8,128)(2,1)S(1)} %get-tuple-element.83), channel_id=1, source_target_pairs={{0,6},{1,7},{2,4},{3,5},{4,2},{5,3},{6,0},{7,1},{8,14},{9,15},{10,... | collective-permute-start | bytes 393224 | tf_op jit(solution)/shard_map/ppermute | solution.py:284
  220.4 10.0 %collective-permute-start.44 = (bf16[2,4,16,512]{3,2,1,0:T(8,128)(2,1)S(1)}, bf16[2,4,16,512]{3,2,1,0:T(8,128)(2,1)S(1)}, u32[]{:S(2)}, u32[]{:S(2)}) collective-permute-start(bf16[2,4,16,512]{3,2,1,0:T(8,128)(2,1)S(1)} %get-tuple-element.84), channel_id=1, source_target_pairs={{0,7},{1,6},{2,5},{3,4},{4,3},{5,2},{6,1},{7,0},{8,15},{9,14},{10,... | collective-permute-start | bytes 393224 | tf_op jit(solution)/shard_map/ppermute | solution.py:284
  (41 other events, 441.2 us)

commit v2 on v1

v2 whole, which is shorter than its diff:
```python
import functools

import jax
import jax.numpy as jnp
import numpy as np
from jax import lax
from jax.experimental import pallas as pl
from jax.experimental.pallas import tpu as pltpu
from jax.sharding import PartitionSpec as P

BLOCK = 64
LEVELS = 3
CHUNKS = (4, 4, 4, 4)
STEPS = (
    "F0", "W0", "F1", "S0", "F2", "S1", "F3", "S2", "T0", "S3", "T1", "B0",
    "T2", "B1", "X0", "T3", "B2", "X1", "B3", "X2", "G0", "X3", "G1", "G2",
    "G3",
)
AFTER = {"W0": ("F0",), "F1": ("W0",), "S0": ("F1",), "F2": ("S0",), "S1": ("F2",), "F3": ("S1",), "S2": ("F3",), "T0": ("S2",), "S3": ("T0",), "T1": ("S3",), "B0": ("T1",), "T2": ("B0",), "B1": ("T2",), "X0": ("B1",), "T3": ("X0",), "B2": ("T3",), "X1": ("B2",), "B3": ("X1",), "X2": ("B3",), "G0": ("X2",), "X3": ("G0",), "G1": ("X3",), "G2": ("G1",), "G3": ("G2",)}
STEP = 2
FIRST_LIMIT = 60
LIMIT = 40
COST = 20.0
SB = 128
W = 256
BF = jnp.bfloat16
F32 = jnp.float32

_x = np.cos((np.arange(400) + 0.5) * np.pi / 400) * 3.1410
_u = (_x * _x) / 10.0
COS = np.linalg.lstsq(np.stack([_u**k for k in range(6)], 1), np.cos(_x), rcond=None)[0]
SIN = np.linalg.lstsq(np.stack([_x * _u**k for k in range(5)], 1), np.sin(_x), rcond=None)[0]
COS = [float(c / 10.0**k) for k, c in enumerate(COS)]
SIN = [float(c / 10.0**k) for k, c in enumerate(SIN)]


def cos_sin(x):
    u = x * x
    c = COS[5] * u + COS[4]
    for k in (3, 2, 1, 0):
        c = c * u + COS[k]
    s = SIN[4] * u + SIN[3]
    for k in (2, 1, 0):
        s = s * u + SIN[k]
    return c, s * x


def turn(re, im, angle):
    c, s = cos_sin(angle.astype(F32))
    return (re * c - im * s).astype(BF), (re * s + im * c).astype(BF)


def dot(a, b):
    return jnp.dot(a, b, preferred_element_type=F32)


class Order:
    def __init__(self):
        self.last = []

    def __call__(self, kernel, name, grid, in_specs, out_specs, out_shape, prefetch=0, scratch=(), flops=0, nbytes=0, limit=None):
        at = prefetch + len(in_specs)

        def body(*refs):
            kernel(*refs[:at], *refs[at + len(before) :])

        before = list(self.last)
        run = pl.pallas_call(
            body,
            out_shape=out_shape,
            grid_spec=pltpu.PrefetchScalarGridSpec(
                num_scalar_prefetch=prefetch,
                grid=grid,
                in_specs=list(in_specs) + [pl.BlockSpec(memory_space=pl.ANY)] * len(before),
                out_specs=out_specs,
                scratch_shapes=list(scratch),
            ),
            compiler_params=pltpu.CompilerParams(vmem_limit_bytes=(limit or LIMIT) << 20),
            cost_estimate=pl.CostEstimate(flops=int(flops * COST), bytes_accessed=int(nbytes * COST), transcendentals=0),
            name=name,
        )

        def go(*operands):
            out = run(*operands, *before)
            self.result = out[0] if isinstance(out, (list, tuple)) else out
            return out

        return go


def weights_kernel(meta, pattern, interp, out):
    slot = pl.program_id(0) // 2
    level = jnp.where(slot < 2, 1, jnp.where(slot == 2, 0, 2))
    cols = lax.broadcasted_iota(jnp.int32, (1, W), 1) // BLOCK
    named = []
    for k in range(2):
        row = jnp.full((1, W), pattern[level * 8 + k])
        for q in range(1, 4):
            row = jnp.where(cols == q, pattern[level * 8 + q * 2 + k], row)
        named.append(row)
    for p in range(4):
        at = slice(p * BLOCK, p * BLOCK + BLOCK)
        w = interp[0, 0, 0, at, :].astype(F32)
        out[0, at, :] = jnp.where((named[0] == p) | (named[1] == p), w, 0.0).astype(BF)


def weights(call, meta, pattern, interp):
    def pick(t, meta, pattern):
        slot = t // 2
        level = jnp.where(slot < 2, 1, jnp.where(slot == 2, 0, 2))
        bit = meta[level]
        return level, bit ^ jnp.where(slot == 1, 1, 0), bit ^ (t & 1), 0, 0

    return call(
        weights_kernel, "masked_weights", (8,),
        [pl.BlockSpec((1, 1, 1, W, W), pick)],
        pl.BlockSpec((1, W, W), lambda t, *_: (t // 2, t % 2, 0)),
        jax.ShapeDtypeStruct((4, 2 * W, W), BF), prefetch=2, flops=0, nbytes=2 << 20,
    )(meta, pattern, interp)


def first_kernel(shuffle, coeffs, angles, out):
    for a in range(2):
        for i in range(STEP):
            x = jnp.concatenate([coeffs[a, i, : 2 * SB], coeffs[a, i, 2 * SB :]], axis=1)
            y = dot(shuffle[...], x)
            for part in range(2):
                lanes = slice(part * 128, part * 128 + 128)
                for r in range(0, 64, 32):
                    row = [y[k * 64 + r : k * 64 + r + 32, lanes] for k in range(4)]
                    at = part * 64 + r
                    re, im = turn(
                        jnp.concatenate(row[:2], axis=1), jnp.concatenate(row[2:], axis=1), angles[0, a, i, at : at + 32]
                    )
                    out[a, i, at : at + 32, :W] = re
                    out[a, i, at : at + 32, W:] = im


def first(call, shuffle, coeffs, angles, off, n):
    return call(
        first_kernel, "rotate_0", (n // STEP,),
        [
            pl.BlockSpec((W, W), lambda t: (0, 0)),
            pl.BlockSpec((2, STEP, 4 * SB, 128), lambda t: (0, off // STEP + t, 0, 0)),
            pl.BlockSpec((1, 2, STEP, SB, W), lambda t: (0, 0, off // STEP + t, 0, 0)),
        ],
        pl.BlockSpec((2, STEP, SB, 2 * W), lambda t: (0, t, 0, 0)),
        jax.ShapeDtypeStruct((2, n, SB, 2 * W), BF), flops=n * 2e8, nbytes=n * 700e3, limit=FIRST_LIMIT,
    )(shuffle, coeffs, angles)


def sides(own, other):
    return jnp.concatenate(
        [jnp.concatenate([own[:, :W], other[:, :W]], axis=1), jnp.concatenate([own[:, W : 2 * W], other[:, W : 2 * W]], axis=1)], axis=0
    )


def turn_rows(y, angles, store):
    for r in range(0, SB, 32):
        re, im = turn(y[r : r + 32], y[SB + r : SB + r + 32], angles[r : r + 32])
        store(r, re, im)


def second_kernel(meta, own, other, w, angles, ahead, keep, send):
    h = meta[3]
    send[:, :, 2 * W :] = ahead[0, 0]
    for out, a in ((send, 1 - h), (keep, h)):
        for i in range(STEP):
            y = dot(sides(own[a, i], other[a, i]), w[0])

            def store(r, re, im, out=out, i=i):
                out[i, r : r + 32, :W] = re
                out[i, r : r + 32, W : 2 * W] = im

            turn_rows(y, angles.at[0, a, i], store)


def second(call, meta, own, other, w, angles, off, n):
    both = pl.BlockSpec((2, STEP, SB, 2 * W), lambda t, *_: (0, t, 0, 0))
    return call(
        second_kernel, "mix_0_rotate_1", (n // STEP,),
        [
            both,
            both,
            pl.BlockSpec((1, 2 * W, W), lambda t, *_: (2, 0, 0)),
            pl.BlockSpec((1, 2, STEP, SB, W), lambda t, *_: (1, 0, off // STEP + t, 0, 0)),
            pl.BlockSpec((1, 1, STEP, SB, W), lambda t, meta: (2, 1 - meta[3], off // STEP + t, 0, 0)),
        ],
        [
            pl.BlockSpec((STEP, SB, 2 * W), lambda t, *_: (t, 0, 0)),
            pl.BlockSpec((STEP, SB, 3 * W), lambda t, *_: (t, 0, 0)),
        ],
        [jax.ShapeDtypeStruct((n, SB, 2 * W), BF), jax.ShapeDtypeStruct((n, SB, 3 * W), BF)],
        prefetch=1, flops=n * 2e8, nbytes=n * 1e6,
    )(meta, own, other, w, angles, angles)


def third_kernel(meta, own, other, w, angles, out):
    for i in range(STEP):
        x = sides(own[i], other[i])
        for g, angle in ((0, angles.at[0, 0, i]), (1, other.at[i, :, 2 * W :])):
            y = dot(x, w[g])

            def store(r, re, im, g=g, i=i):
                out[g, i, r : r + 32, :W] = re
                out[g, i, r : r + 32, W:] = im

            turn_rows(y, angle, store)


def third(call, meta, own, other, w, angles, off, n):
    return call(
        third_kernel, "mix_1_rotate_2", (n // STEP,),
        [
            pl.BlockSpec((STEP, SB, 2 * W), lambda t, *_: (t, 0, 0)),
            pl.BlockSpec((STEP, SB, 3 * W), lambda t, *_: (t, 0, 0)),
            pl.BlockSpec((2, 2 * W, W), lambda t, *_: (0, 0, 0)),
            pl.BlockSpec((1, 1, STEP, SB, W), lambda t, meta: (2, meta[3], off // STEP + t, 0, 0)),
        ],
        pl.BlockSpec((2, STEP, SB, 2 * W), lambda t, *_: (0, t, 0, 0)),
        jax.ShapeDtypeStruct((2, n, SB, 2 * W), BF), prefetch=1, flops=n * 2e8, nbytes=n * 700e3,
    )(meta, own, other, w, angles)


def back_kernel(own, other, w, out):
    for i in range(STEP):
        y = dot(sides(own[0, i], other[0, i]), w[0])
        out[i, :, :W] = y[:SB].astype(BF)
        out[i, :, W:] = y[SB:].astype(BF)


def back(call, own, other, w, n):
    return call(
        back_kernel, "mix_2_other", (n // STEP,),
        [
            pl.BlockSpec((1, STEP, SB, 2 * W), lambda t: (1, t, 0, 0)),
            pl.BlockSpec((1, STEP, SB, 2 * W), lambda t: (0, t, 0, 0)),
            pl.BlockSpec((1, 2 * W, W), lambda t: (3, 0, 0)),
        ],
        pl.BlockSpec((STEP, SB, 2 * W), lambda t: (t, 0, 0)),
        jax.ShapeDtypeStruct((n, SB, 2 * W), BF), flops=n * 1e8, nbytes=n * 400e3,
    )(own, other, w)


def split_kernel(own, other, w, came, out):
    for i in range(STEP):
        y = dot(sides(own[0, i], other[0, i]), w[0]).astype(BF)
        for q in range(8):
            out[q, 0, i, :, :W] = y[q * 16 : q * 16 + 16]
            out[q, 0, i, :, W:] = y[SB + q * 16 : SB + q * 16 + 16]
            out[q, 1, i] = came[i, q * 16 : q * 16 + 16]


def split(call, own, other, w, came, n):
    return call(
        split_kernel, "mix_2_own_split", (n // STEP,),
        [
            pl.BlockSpec((1, STEP, SB, 2 * W), lambda t: (0, t, 0, 0)),
            pl.BlockSpec((1, STEP, SB, 2 * W), lambda t: (1, t, 0, 0)),
            pl.BlockSpec((1, 2 * W, W), lambda t: (3, 0, 0)),
            pl.BlockSpec((STEP, SB, 2 * W), lambda t: (t, 0, 0)),
        ],
        pl.BlockSpec((8, 2, STEP, 16, 2 * W), lambda t: (0, 0, t, 0, 0)),
        jax.ShapeDtypeStruct((8, 2, n, 16, 2 * W), BF), flops=n * 1e8, nbytes=n * 800e3,
    )(own, other, w, came)


def gather_kernel(shuffle, pieces, out):
    y = dot(shuffle[...], pieces[...].reshape(W, 2 * W)).astype(BF)
    for j in range(16):
        out[j] = y[j * 16 : j * 16 + 16]


def gather(call, shuffle, pieces, n):
    return call(
        gather_kernel, "gather_frequencies", (n,),
        [pl.BlockSpec((W, W), lambda t: (0, 0)), pl.BlockSpec((8 // n, 2, n, 16, 2 * W), lambda t: (t, 0, 0, 0, 0))],
        pl.BlockSpec((16, 16, 2 * W), lambda t: (0, t, 0)),
        jax.ShapeDtypeStruct((16, 16 * n, 2 * W), BF), flops=n * 1e8, nbytes=n * 500e3,
    )(shuffle, pieces)


def target_kernel(chunks, t_map, *refs):
    parts, out = refs[:chunks], refs[chunks]
    for j in range(2):
        y = dot(t_map[...], jnp.concatenate([p[j] for p in parts], axis=0))
        for c in range(2):
            for half in range(2):
                at = c * W + half * 128
                out[:, j * 4 + half * 2 + c, :] = y[:, at : at + 128]


def target(call, t_map, parts):
    return call(
        functools.partial(target_kernel, len(parts)), "target_map", (8,),
        [pl.BlockSpec((W, W), lambda t: (0, 0))]
        + [pl.BlockSpec((2, p.shape[1], 2 * W), lambda t: (t, 0, 0)) for p in parts],
        pl.BlockSpec((W, 8, 128), lambda t: (0, t, 0)),
        jax.ShapeDtypeStruct((W, 64, 128), F32), flops=1e9, nbytes=12 << 20,
    )(t_map, *parts)


def swap(value, axis, mask):
    return lax.ppermute(value, axis, [(i, i ^ mask) for i in range(lax.axis_size(axis))])


def shuffles():
    first_rows = np.zeros((W, W), np.float32)
    last_rows = np.zeros((W, W), np.float32)
    for j in range(64):
        for half in range(2):
            for c in range(2):
                first_rows[(c * 2 + half) * 64 + j, j * 4 + half * 2 + c] = 1
    for j in range(16):
        for f in range(16):
            last_rows[j * 16 + f, f * 16 + j] = 1
    return jnp.asarray(first_rows, BF), jnp.asarray(last_rows, BF)


def on_device(coeffs, angles, interp, pattern, target_map):
    src = lax.axis_index("src")
    bits = [src >> k & 1 for k in range(LEVELS)]
    h = bits[1] ^ bits[2]
    meta = jnp.stack([*bits, h]).astype(jnp.int32)
    spread, close = shuffles()
    coeffs = coeffs.reshape(2, 16, SB, 2, 2, 128).transpose(0, 1, 2, 4, 3, 5).reshape(2, 16, 4 * SB, 128)
    angles = angles.reshape(LEVELS, 2, 16, SB, W)

    offs = np.cumsum((0,) + CHUNKS)[:-1].tolist()
    order = np.concatenate(
        [
            np.asarray([m << 5 | half << 4 | off + i for m in range(8) for half in range(2) for i in range(n)])
            for off, n in zip(offs, CHUNKS)
        ]
    )
    chosen = jnp.asarray(order, jnp.int32) ^ (h << 4)
    hot = (jnp.arange(W, dtype=jnp.int32)[:, None] == chosen[None, :]).astype(BF)
    t_map = jnp.dot(target_map, hot, preferred_element_type=F32).astype(BF)

    call = Order()
    state, done = {}, {}

    def step(kind, c):
        w = state.get("w")
        if kind == "W":
            state["w"] = weights(call, meta, pattern.reshape(-1), interp)
            return
        off, n = offs[c], CHUNKS[c]
        if kind == "F":
            turned = first(call, spread, coeffs, angles, off, n)
            state["F", c] = turned, swap(turned, "src", 1)
        if kind == "S":
            keep, send = second(call, meta, *state["F", c], w, angles, off, n)
            state["S", c] = keep, swap(send, "src", 2)
        if kind == "T":
            turned = third(call, meta, *state["S", c], w, angles, off, n)
            state["T", c] = turned, swap(turned, "src", 6)
        if kind == "B":
            state["B", c] = swap(back(call, *state["T", c], w, n), "src", 2)
        if kind == "X":
            pieces = split(call, *state["T", c], w, state["B", c], n)
            pieces = lax.all_to_all(pieces.reshape(-1, 2 * W), "frq", 0, 0, tiled=True)
            state["X", c] = pieces.reshape(8, 2, n, 16, 2 * W)
        if kind == "G":
            state["G", c] = gather(call, close, state["X", c], n)

    for name in STEPS:
        call.last = [done[other] for other in AFTER.get(name, ())]
        step(name[0], int(name[1:]))
        done[name] = call.result
    call.last = []
    parts = [state["G", c] for c in range(len(CHUNKS))]
    out = target(call, t_map, parts)
    return out.reshape(W, 16, 2, 2, 128).transpose(0, 1, 3, 2, 4).reshape(W, 16, 2, W)


def solution(mesh):
    return jax.shard_map(
        on_device,
        mesh=mesh,
        in_specs=(P("frq", "src", None, None), P(None, "frq", "src", None), P(), P(), P()),
        out_specs=P(None, ("src", "frq"), None, None),
        check_vma=False,
    )
```

time: 240 us -> 198 us (0.82)
  starting transfers between devices: 74.5 us -> 41.9 us
  waiting for transfers between devices: 81.3 us -> 59.2 us
  Pallas kernels: 54.4 us -> 66.1 us
    ppermute x45 -> x16, starting transfers between devices: 74.5 us -> 21.9 us  [swap(): lax.ppermute(value, axis, [(i, i ^ mask) for i in range(lax.axis_size(axi...]
    ppermute x45 -> x16, waiting for transfers between devices: 81.3 us -> 42.2 us  [swap(): lax.ppermute(value, axis, [(i, i ^ mask) for i in range(lax.axis_size(axi...]
    all_to_all x0 -> x4, starting transfers between devices: none -> 20 us  [step(): pieces = lax.all_to_all(pieces.reshape(-1, 2 * W), 'frq', 0, 0, tiled=True)]
    all_to_all x0 -> x4, waiting for transfers between devices: none -> 17 us  [step(): pieces = lax.all_to_all(pieces.reshape(-1, 2 * W), 'frq', 0, 0, tiled=True)]
    pallas_call x26, Pallas kernels: 54.4 us -> 66.1 us  [go(): out = run(*operands, *before)]
    unnamed x89 -> x83, local copies, waits for them, and re-layouts: 23.5 us -> 28.1 us
  transfers between devices with their start and end apart: 45 -> 20, of which waited for: 10 -> 8; matrix products, arithmetic and copies ran while one was open for 2% -> 0% of each run, Pallas kernels for 18% -> 28%
where the time goes in v2:
time: 198 us; the launch traced here: 196 us
  Pallas kernels  66.1 us (33%)
  waiting for transfers between devices  59.2 us (30%)
  starting transfers between devices  41.9 us (21%)
  local copies, waits for them, and re-layouts  28.2 us (14%)
    pallas_call x26, Pallas kernels, go(): out = run(*operands, *before)  66.1 us
    ppermute x16, waiting for transfers between devices, swap(): lax.ppermute(value, axis, [(i, i ^ mask) for i in range(lax.axis_size(axi...  42.2 us
    unnamed x83, local copies, waits for them, and re-layouts  28.1 us
    ppermute x16, starting transfers between devices, swap(): lax.ppermute(value, axis, [(i, i ^ mask) for i in range(lax.axis_size(axi...  21.9 us
    all_to_all x4, starting transfers between devices, step(): pieces = lax.all_to_all(pieces.reshape(-1, 2 * W), 'frq', 0, 0, tiled=True)  20 us
    all_to_all x4, waiting for transfers between devices, step(): pieces = lax.all_to_all(pieces.reshape(-1, 2 * W), 'frq', 0, 0, tiled=True)  17 us
  transfers between devices with their start and end apart: 20, of which 8 were waited for; matrix products, arithmetic and copies ran while one was open for 0% of the time, Pallas kernels for 28%

profile of v2, /device:TPU:0, one launch (start us, length us, event | category | flops | bytes accessed | tf_op | source)
XLA Modules:
  0.0 196.0 jit_solution(10016827535476277200)
XLA Ops:
  0.0 3.4 %rotate_0.4.refs_3_.refs_1_ = bf16[2,4,128,512]{3,2,1,0:T(8,128)(2,1)} custom-call(bf16[256,256]{1,0:T(8,128)(2,1)} %constant.20.clone.refs_0_, bf16[2,16,512,128]{3,2,1,0:T(8,128)(2,1)} %bitcast.49, bf16[3,2,16,128,256]{4,3,2,1,0:T(8,128)(2,1)} %bitcast.31), custom_call_target="tpu_custom_call" | custom-call | flops 16000000000 | bytes 56000000 | tf_op jit(solution)/shard_map/rotate_0/pallas_call | solution.py:84
  3.7 1.2 copy-done.8
  7.0 3.4 %rotate_0.5.refs_6_.refs_1_ = bf16[2,4,128,512]{3,2,1,0:T(8,128)(2,1)} custom-call(bf16[256,256]{1,0:T(8,128)(2,1)} %constant.20.clone.refs_0_, bf16[2,16,512,128]{3,2,1,0:T(8,128)(2,1)} %bitcast.50, bf16[3,2,16,128,256]{4,3,2,1,0:T(8,128)(2,1)} %bitcast.32, bf16[4,512,256]{2,1,0:T(8,128)(2,1)} %copy-done.4), custom_call_target="tpu_custom_call" | custom-call | flops 16000000000 | bytes 56000000 | tf_op jit(solution)/shard_map/rotate_0/pallas_call | solution.py:84
  11.1 1.2 copy-done.5
  12.3 2.8 %copy-done.10 = bf16[3,32,128,256]{3,2,1,0:T(8,128)(2,1)S(1)} copy-done((bf16[3,32,128,256]{3,2,1,0:T(8,128)(2,1)S(1)}, bf16[3,32,128,256]{3,2,1,0:T(8,128)(2,1)}, u32[]{:S(2)}) %copy-start.10) | copy-done | bytes 6291480
  15.1 1.2 copy-done.18
  16.3 3.7 %mix_0_rotate_1.4 = (bf16[4,128,512]{2,1,0:T(8,128)(2,1)S(1)}, bf16[4,128,768]{2,1,0:T(8,128)(2,1)}) custom-call(s32[4]{0:T(128)S(1)} %pad_add_fusion.refs_0_, bf16[2,4,128,512]{3,2,1,0:T(8,128)(2,1)S(1)} %copy-done.9, bf16[2,4,128,512]{3,2,1,0:T(8,128)(2,1)} %collective-permute-done.refs_2_, bf16[4,512,256]{2,1,0:T(8,128)(2,1)S(1)} %copy-done.5, ...), custom_call_target="tpu_custom_call" | custom-call | flops 16000000000 | bytes 80000000 | tf_op jit(solution)/shard_map/mix_0_rotate_1/pallas_call | solution.py:84
  20.9 2.0 %collective-permute-start.1 = (bf16[4,128,768]{2,1,0:T(8,128)(2,1)}, bf16[4,128,768]{2,1,0:T(8,128)(2,1)}, u32[]{:S(2)}, u32[]{:S(2)}) collective-permute-start(bf16[4,128,768]{2,1,0:T(8,128)(2,1)} %get-tuple-element.14), channel_id=1, source_target_pairs={{0,16},{8,24},{16,0},{24,8},{32,48},{40,56},{48,32},{56,40},{64,80... | collective-permute-start | bytes 2359304 | tf_op jit(solution)/shard_map/ppermute | solution.py:304
  23.0 3.4 %rotate_0.6.refs_6_.refs_1_ = bf16[2,4,128,512]{3,2,1,0:T(8,128)(2,1)} custom-call(bf16[256,256]{1,0:T(8,128)(2,1)} %constant.20.clone.refs_0_, bf16[2,16,512,128]{3,2,1,0:T(8,128)(2,1)} %bitcast.51, bf16[3,2,16,128,256]{4,3,2,1,0:T(8,128)(2,1)} %bitcast.33, bf16[4,128,512]{2,1,0:T(8,128)(2,1)} %copy-done.35), custom_call_target="tpu_custom_call" | custom-call | flops 16000000000 | bytes 56000000 | tf_op jit(solution)/shard_map/rotate_0/pallas_call | solution.py:84
  26.4 2.8 %copy-done.11 = bf16[3,32,128,256]{3,2,1,0:T(8,128)(2,1)S(1)} copy-done((bf16[3,32,128,256]{3,2,1,0:T(8,128)(2,1)S(1)}, bf16[3,32,128,256]{3,2,1,0:T(8,128)(2,1)}, u32[]{:S(2)}) %copy-start.11) | copy-done | bytes 6291480
  29.2 1.2 copy-done.22
  30.4 2.9 %mix_0_rotate_1.5 = (bf16[4,128,512]{2,1,0:T(8,128)(2,1)S(1)}, bf16[4,128,768]{2,1,0:T(8,128)(2,1)}) custom-call(s32[4]{0:T(128)S(1)} %pad_add_fusion.refs_0_, bf16[2,4,128,512]{3,2,1,0:T(8,128)(2,1)S(1)} %copy-done.19, bf16[2,4,128,512]{3,2,1,0:T(8,128)(2,1)S(1)} %collective-permute-done.3.refs_2_, bf16[4,512,256]{2,1,0:T(8,128)(2,1)S(1)} %copy-done.6, ...), custom_call_target="tpu_custom_call" | custom-call | flops 16000000000 | bytes 80000000 | tf_op jit(solution)/shard_map/mix_0_rotate_1/pallas_call | solution.py:84
  34.1 3.4 %rotate_0.7.refs_6_.refs_1_ = bf16[2,4,128,512]{3,2,1,0:T(8,128)(2,1)} custom-call(bf16[256,256]{1,0:T(8,128)(2,1)} %constant.20.clone.refs_0_, bf16[2,16,512,128]{3,2,1,0:T(8,128)(2,1)} %bitcast.52, bf16[3,2,16,128,256]{4,3,2,1,0:T(8,128)(2,1)} %bitcast.34, bf16[4,128,512]{2,1,0:T(8,128)(2,1)} %copy-done.33), custom_call_target="tpu_custom_call" | custom-call | flops 16000000000 | bytes 56000000 | tf_op jit(solution)/shard_map/rotate_0/pallas_call | solution.py:84
  38.0 2.8 %copy-done.12 = bf16[3,32,128,256]{3,2,1,0:T(8,128)(2,1)S(1)} copy-done((bf16[3,32,128,256]{3,2,1,0:T(8,128)(2,1)S(1)}, bf16[3,32,128,256]{3,2,1,0:T(8,128)(2,1)}, u32[]{:S(2)}) %copy-start.12) | copy-done | bytes 6291480
  40.8 1.2 copy-done.20
  42.0 3.1 %mix_0_rotate_1.6 = (bf16[4,128,512]{2,1,0:T(8,128)(2,1)S(1)}, bf16[4,128,768]{2,1,0:T(8,128)(2,1)S(1)}) custom-call(s32[4]{0:T(128)S(1)} %pad_add_fusion.refs_0_, bf16[2,4,128,512]{3,2,1,0:T(8,128)(2,1)S(1)} %copy-done.23, bf16[2,4,128,512]{3,2,1,0:T(8,128)(2,1)} %collective-permute-done.2.refs_2_, bf16[4,512,256]{2,1,0:T(8,128)(2,1)S(1)} %copy-done.6, ...), custom_call_target="tpu_custom_call" | custom-call | flops 16000000000 | bytes 80000000 | tf_op jit(solution)/shard_map/mix_0_rotate_1/pallas_call | solution.py:84
  45.1 3.1 %mix_1_rotate_2.4.refs_6_.refs_0_ = bf16[2,4,128,512]{3,2,1,0:T(8,128)(2,1)S(1)} custom-call(s32[4]{0:T(128)S(1)} %pad_add_fusion.refs_0_, bf16[4,128,512]{2,1,0:T(8,128)(2,1)S(1)} %copy-done.36, bf16[4,128,768]{2,1,0:T(8,128)(2,1)} %collective-permute-done.1.refs_2_, bf16[4,512,256]{2,1,0:T(8,128)(2,1)S(1)} %copy-done.6, ...), custom_call_target="tpu_custom_call" | custom-call | flops 16000000000 | bytes 56000000 | tf_op jit(solution)/shard_map/mix_1_rotate_2/pallas_call | solution.py:84
  48.2 3.9 %collective-permute-start.4 = (bf16[2,4,128,512]{3,2,1,0:T(8,128)(2,1)S(1)}, bf16[2,4,128,512]{3,2,1,0:T(8,128)(2,1)S(1)}, u32[]{:S(2)}, u32[]{:S(2)}) collective-permute-start(bf16[2,4,128,512]{3,2,1,0:T(8,128)(2,1)S(1)} %mix_1_rotate_2.4.refs_6_.refs_0_), channel_id=1, source_target_pairs={{0,48},{8,56},{16,32},{24,40},{32,16},{40,24},{48,0},{56,8},{64,11... | collective-permute-start | bytes 3145736 | tf_op jit(solution)/shard_map/ppermute | solution.py:304
  52.1 2.2 %mix_0_rotate_1.7 = (bf16[4,128,512]{2,1,0:T(8,128)(2,1)S(1)}, bf16[4,128,768]{2,1,0:T(8,128)(2,1)S(1)}) custom-call(s32[4]{0:T(128)S(1)} %pad_add_fusion.refs_0_, bf16[2,4,128,512]{3,2,1,0:T(8,128)(2,1)S(1)} %copy-done.21, bf16[2,4,128,512]{3,2,1,0:T(8,128)(2,1)S(1)} %collective-permute-done.6.refs_2_, bf16[4,512,256]{2,1,0:T(8,128)(2,1)S(1)} %copy-done.6, ...), custom_call_target="tpu_custom_call" | custom-call | flops 16000000000 | bytes 80000000 | tf_op jit(solution)/shard_map/mix_0_rotate_1/pallas_call | solution.py:84
  54.5 2.0 %collective-permute-start.9 = (bf16[4,128,768]{2,1,0:T(8,128)(2,1)S(1)}, bf16[4,128,768]{2,1,0:T(8,128)(2,1)S(1)}, u32[]{:S(2)}, u32[]{:S(2)}) collective-permute-start(bf16[4,128,768]{2,1,0:T(8,128)(2,1)S(1)} %get-tuple-element.19), channel_id=1, source_target_pairs={{0,16},{8,24},{16,0},{24,8},{32,48},{40,56},{48,32},{56,40},{64,80... | collective-permute-start | bytes 2359304 | tf_op jit(solution)/shard_map/ppermute | solution.py:304
  56.5 2.0 %collective-permute-done.5.refs_2_ = bf16[4,128,768]{2,1,0:T(8,128)(2,1)} collective-permute-done((bf16[4,128,768]{2,1,0:T(8,128)(2,1)}, bf16[4,128,768]{2,1,0:T(8,128)(2,1)}, u32[]{:S(2)}, u32[]{:S(2)}) %collective-permute-start.5) | collective-permute-done | bytes 786464 | tf_op jit(solution)/shard_map/ppermute | solution.py:304
  58.5 3.3 %mix_1_rotate_2.5.refs_3_.refs_0_ = bf16[2,4,128,512]{3,2,1,0:T(8,128)(2,1)S(1)} custom-call(s32[4]{0:T(128)S(1)} %pad_add_fusion.refs_0_, bf16[4,128,512]{2,1,0:T(8,128)(2,1)S(1)} %copy-done.34, bf16[4,128,768]{2,1,0:T(8,128)(2,1)} %collective-permute-done.5.refs_2_, bf16[4,512,256]{2,1,0:T(8,128)(2,1)S(1)} %copy-done.6, ...), custom_call_target="tpu_custom_call" | custom-call | flops 16000000000 | bytes 56000000 | tf_op jit(solution)/shard_map/mix_1_rotate_2/pallas_call | solution.py:84
  61.8 4.2 %collective-permute-start.8 = (bf16[2,4,128,512]{3,2,1,0:T(8,128)(2,1)S(1)}, bf16[2,4,128,512]{3,2,1,0:T(8,128)(2,1)S(1)}, u32[]{:S(2)}, u32[]{:S(2)}) collective-permute-start(bf16[2,4,128,512]{3,2,1,0:T(8,128)(2,1)S(1)} %mix_1_rotate_2.5.refs_3_.refs_0_), channel_id=1, source_target_pairs={{0,48},{8,56},{16,32},{24,40},{32,16},{40,24},{48,0},{56,8},{64,11... | collective-permute-start | bytes 3145736 | tf_op jit(solution)/shard_map/ppermute | solution.py:304
  66.1 10.0 %collective-permute-done.4.refs_1_ = bf16[2,4,128,512]{3,2,1,0:T(8,128)(2,1)S(1)} collective-permute-done((bf16[2,4,128,512]{3,2,1,0:T(8,128)(2,1)S(1)}, bf16[2,4,128,512]{3,2,1,0:T(8,128)(2,1)S(1)}, u32[]{:S(2)}, u32[]{:S(2)}) %collective-permute-start.4) | collective-permute-done | bytes 1048608 | tf_op jit(solution)/shard_map/ppermute | solution.py:304
  76.8 15.3 %collective-permute-done.9.refs_2_ = bf16[4,128,768]{2,1,0:T(8,128)(2,1)S(1)} collective-permute-done((bf16[4,128,768]{2,1,0:T(8,128)(2,1)S(1)}, bf16[4,128,768]{2,1,0:T(8,128)(2,1)S(1)}, u32[]{:S(2)}, u32[]{:S(2)}) %collective-permute-start.9) | collective-permute-done | bytes 786464 | tf_op jit(solution)/shard_map/ppermute | solution.py:304
  92.1 2.8 %mix_1_rotate_2.6.refs_3_.refs_0_ = bf16[2,4,128,512]{3,2,1,0:T(8,128)(2,1)} custom-call(s32[4]{0:T(128)S(1)} %pad_add_fusion.refs_0_, bf16[4,128,512]{2,1,0:T(8,128)(2,1)S(1)} %get-tuple-element.16.refs_5_.refs_1_, bf16[4,128,768]{2,1,0:T(8,128)(2,1)S(1)} %collective-permute-done.9.refs_2_, bf16[4,512,256]{2,1,0:T(8,128)(2,1)S(1)} %copy-done.6, ...), custom_call_target="tpu_custom_call" | custom-call | flops 16000000000 | bytes 56000000 | tf_op jit(solution)/shard_map/mix_1_rotate_2/pallas_call | solution.py:84
  94.9 4.2 %collective-permute-start.10 = (bf16[2,4,128,512]{3,2,1,0:T(8,128)(2,1)}, bf16[2,4,128,512]{3,2,1,0:T(8,128)(2,1)}, u32[]{:S(2)}, u32[]{:S(2)}) collective-permute-start(bf16[2,4,128,512]{3,2,1,0:T(8,128)(2,1)} %mix_1_rotate_2.6.refs_3_.refs_0_), channel_id=1, source_target_pairs={{0,48},{8,56},{16,32},{24,40},{32,16},{40,24},{48,0},{56,8},{64,11... | collective-permute-start | bytes 3145736 | tf_op jit(solution)/shard_map/ppermute | solution.py:304
  99.0 1.3 mix_2_other.5.refs_4_
  100.4 2.7 %collective-permute-done.7.refs_3_ = bf16[4,128,512]{2,1,0:T(8,128)(2,1)S(1)} collective-permute-done((bf16[4,128,512]{2,1,0:T(8,128)(2,1)S(1)}, bf16[4,128,512]{2,1,0:T(8,128)(2,1)S(1)}, u32[]{:S(2)}, u32[]{:S(2)}) %collective-permute-start.7) | collective-permute-done | bytes 524320 | tf_op jit(solution)/shard_map/ppermute | solution.py:304
  103.1 1.4 mix_2_own_split.4.refs_5_
  104.5 5.3 %all-to-all-start = ((bf16[8,128,512]{2,1,0:T(8,128)(2,1)}), bf16[8,128,512]{2,1,0:T(8,128)(2,1)S(1)}, u32[]{:S(2)}, u32[]{:S(2)}) async-start(bf16[8,128,512]{2,1,0:T(8,128)(2,1)} %bitcast.11), calls=%async_computation | async-start | bytes 2097152 | tf_op jit(solution)/shard_map/all_to_all | solution.py:362
  109.9 2.8 %copy-done.13 = bf16[3,32,128,256]{3,2,1,0:T(8,128)(2,1)S(1)} copy-done((bf16[3,32,128,256]{3,2,1,0:T(8,128)(2,1)S(1)}, bf16[3,32,128,256]{3,2,1,0:T(8,128)(2,1)}, u32[]{:S(2)}) %copy-start.13) | copy-done | bytes 6291480
  113.7 3.8 %mix_1_rotate_2.7.refs_3_.refs_0_ = bf16[2,4,128,512]{3,2,1,0:T(8,128)(2,1)} custom-call(s32[4]{0:T(128)S(1)} %pad_add_fusion.refs_0_, bf16[4,128,512]{2,1,0:T(8,128)(2,1)S(1)} %copy-done.32, bf16[4,128,768]{2,1,0:T(8,128)(2,1)} %collective-permute-done.11.refs_2_, bf16[4,512,256]{2,1,0:T(8,128)(2,1)S(1)} %copy-done.6, ...), custom_call_target="tpu_custom_call" | custom-call | flops 16000000000 | bytes 56000000 | tf_op jit(solution)/shard_map/mix_1_rotate_2/pallas_call | solution.py:84
  117.5 4.4 %collective-permute-start.13 = (bf16[2,4,128,512]{3,2,1,0:T(8,128)(2,1)}, bf16[2,4,128,512]{3,2,1,0:T(8,128)(2,1)}, u32[]{:S(2)}, u32[]{:S(2)}) collective-permute-start(bf16[2,4,128,512]{3,2,1,0:T(8,128)(2,1)} %mix_1_rotate_2.7.refs_3_.refs_0_), channel_id=1, source_target_pairs={{0,48},{8,56},{16,32},{24,40},{32,16},{40,24},{48,0},{56,8},{64,11... | collective-permute-start | bytes 3145736 | tf_op jit(solution)/shard_map/ppermute | solution.py:304
  121.9 2.3 %mix_2_other.6.refs_4_ = bf16[4,128,512]{2,1,0:T(8,128)(2,1)} custom-call(bf16[2,4,128,512]{3,2,1,0:T(8,128)(2,1)} %mix_1_rotate_2.6.refs_3_.refs_0_, bf16[2,4,128,512]{3,2,1,0:T(8,128)(2,1)} %collective-permute-done.10.refs_1_, bf16[4,512,256]{2,1,0:T(8,128)(2,1)S(1)} %copy-done.6, bf16[2,4,128,512]{3,2,1,0:T(8,128)(2,1)} %mix_1_rotate_2.7.refs_3_.refs_0_), custom_call_target="tpu_custom_call" | custom-call | flops 8000000000 | bytes 32000000 | tf_op jit(solution)/shard_map/mix_2_other/pallas_call | solution.py:84
  124.2 2.4 %mix_2_own_split.5.refs_3_ = bf16[8,2,4,16,512]{4,3,2,1,0:T(8,128)(2,1)} custom-call(bf16[2,4,128,512]{3,2,1,0:T(8,128)(2,1)S(1)} %copy-done.15, bf16[2,4,128,512]{3,2,1,0:T(8,128)(2,1)S(1)} %copy-done.17, bf16[4,512,256]{2,1,0:T(8,128)(2,1)S(1)} %copy-done.6, bf16[4,128,512]{2,1,0:T(8,128)(2,1)} %collective-permute-done.14.refs_3_, ...), custom_call_target="tpu_custom_call" | custom-call | flops 8000000000 | bytes 64000000 | tf_op jit(solution)/shard_map/mix_2_own_split/pallas_call | solution.py:84
  126.7 5.7 %all-to-all-start.1 = ((bf16[8,128,512]{2,1,0:T(8,128)(2,1)}), bf16[8,128,512]{2,1,0:T(8,128)(2,1)S(1)}, u32[]{:S(2)}, u32[]{:S(2)}) async-start(bf16[8,128,512]{2,1,0:T(8,128)(2,1)} %bitcast.13), calls=%async_computation.1 | async-start | bytes 2097152 | tf_op jit(solution)/shard_map/all_to_all | solution.py:362
  132.4 11.2 %collective-permute-done.13.refs_1_ = bf16[2,4,128,512]{3,2,1,0:T(8,128)(2,1)} collective-permute-done((bf16[2,4,128,512]{3,2,1,0:T(8,128)(2,1)}, bf16[2,4,128,512]{3,2,1,0:T(8,128)(2,1)}, u32[]{:S(2)}, u32[]{:S(2)}) %collective-permute-start.13) | collective-permute-done | bytes 1048608 | tf_op jit(solution)/shard_map/ppermute | solution.py:304
  143.6 2.4 %mix_2_other.7.refs_4_ = bf16[4,128,512]{2,1,0:T(8,128)(2,1)} custom-call(bf16[2,4,128,512]{3,2,1,0:T(8,128)(2,1)} %mix_1_rotate_2.7.refs_3_.refs_0_, bf16[2,4,128,512]{3,2,1,0:T(8,128)(2,1)} %collective-permute-done.13.refs_1_, bf16[4,512,256]{2,1,0:T(8,128)(2,1)S(1)} %copy-done.6, bf16[8,2,4,16,512]{4,3,2,1,0:T(8,128)(2,1)} %mix_2_own_split.5.refs_3_), custom_call_target="tpu_custom_call" | custom-call | flops 8000000000 | bytes 32000000 | tf_op jit(solution)/shard_map/mix_2_other/pallas_call | solution.py:84
  146.0 1.9 mix_2_own_split.6.refs_2_
  148.8 5.4 %all-to-all-start.2 = ((bf16[8,128,512]{2,1,0:T(8,128)(2,1)}), bf16[8,128,512]{2,1,0:T(8,128)(2,1)S(1)}, u32[]{:S(2)}, u32[]{:S(2)}) async-start(bf16[8,128,512]{2,1,0:T(8,128)(2,1)} %bitcast.29), calls=%async_computation.2 | async-start | bytes 2097152 | tf_op jit(solution)/shard_map/all_to_all | solution.py:362
  154.2 1.2 copy-done.3
  157.5 2.6 %mix_2_own_split.7.refs_2_ = bf16[8,2,4,16,512]{4,3,2,1,0:T(8,128)(2,1)} custom-call(bf16[2,4,128,512]{3,2,1,0:T(8,128)(2,1)} %mix_1_rotate_2.7.refs_3_.refs_0_, bf16[2,4,128,512]{3,2,1,0:T(8,128)(2,1)} %collective-permute-done.13.refs_1_, bf16[4,512,256]{2,1,0:T(8,128)(2,1)S(1)} %copy-done.7, bf16[4,128,512]{2,1,0:T(8,128)(2,1)} %collective-permute-done.15.refs_3_, ...), custom_call_target="tpu_custom_call" | custom-call | flops 8000000000 | bytes 64000000 | tf_op jit(solution)/shard_map/mix_2_own_split/pallas_call | solution.py:84
  161.1 6.1 %all-to-all-done.2 = bf16[8,128,512]{2,1,0:T(8,128)(2,1)S(1)} async-done(((bf16[8,128,512]{2,1,0:T(8,128)(2,1)}), bf16[8,128,512]{2,1,0:T(8,128)(2,1)S(1)}, u32[]{:S(2)}, u32[]{:S(2)}) %all-to-all-start.2) | async-done | bytes 1048608 | tf_op jit(solution)/shard_map/all_to_all | solution.py:362
  167.2 3.6 %all-to-all-start.3 = ((bf16[8,128,512]{2,1,0:T(8,128)(2,1)}), bf16[8,128,512]{2,1,0:T(8,128)(2,1)S(1)}, u32[]{:S(2)}, u32[]{:S(2)}) async-start(bf16[8,128,512]{2,1,0:T(8,128)(2,1)} %bitcast.17), calls=%async_computation.3 | async-start | bytes 2097152 | tf_op jit(solution)/shard_map/all_to_all | solution.py:362
  174.8 10.9 %all-to-all-done.3 = bf16[8,128,512]{2,1,0:T(8,128)(2,1)S(1)} async-done(((bf16[8,128,512]{2,1,0:T(8,128)(2,1)}), bf16[8,128,512]{2,1,0:T(8,128)(2,1)S(1)}, u32[]{:S(2)}, u32[]{:S(2)}) %all-to-all-start.3) | async-done | bytes 1048608 | tf_op jit(solution)/shard_map/all_to_all | solution.py:362
  185.6 1.2 copy-done.30
  188.4 7.6 %target_map.1 = f32[256,64,128]{2,1,0:T(8,128)} custom-call(bf16[256,256]{1,0:T(8,128)(2,1)S(1)} %fusion.refs_0_, bf16[16,64,512]{2,1,0:T(8,128)(2,1)S(1)} %copy-done.26, bf16[16,64,512]{2,1,0:T(8,128)(2,1)S(1)} %copy-done.28, bf16[16,64,512]{2,1,0:T(8,128)(2,1)S(1)} %copy-done.30, bf16[16,64,512]{2,1,0:T(8,128)(2,1)S(1)} %gather_frequencies.7.refs_4_), custom_call_target="tpu_custom_call" | custom-call | flops 20000000000 | bytes 251658240 | tf_op jit(solution)/shard_map/target_map/pallas_call | solution.py:84
  (106 shorter events, 16.5 us)
Async XLA Ops:
  0.0 10.9 %copy-start = (bf16[256,256]{1,0:T(8,128)(2,1)S(1)}, bf16[256,256]{1,0:T(8,128)(2,1)}, u32[]{:S(2)}) copy-start(bf16[256,256]{1,0:T(8,128)(2,1)} %param.12) | copy-start | bytes 393220
  0.0 3.4 %copy-start.37 = (s32[3,4,2]{1,2,0:T(2,128)S(1)}, s32[3,4,2]{1,2,0:T(2,128)}, u32[]{:S(2)}) copy-start(s32[3,4,2]{1,2,0:T(2,128)} %param.11) | copy-start | bytes 292
  0.0 3.7 %copy-start.1 = (bf16[3,2,2,256,256]{4,3,2,1,0:T(8,128)(2,1)S(1)}, bf16[3,2,2,256,256]{4,3,2,1,0:T(8,128)(2,1)}, u32[]{:S(2)}) copy-start(bf16[3,2,2,256,256]{4,3,2,1,0:T(8,128)(2,1)} %refs_2_.1) | copy-start | bytes 4718596
  3.4 7.7 %collective-permute-start = (bf16[2,4,128,512]{3,2,1,0:T(8,128)(2,1)}, bf16[2,4,128,512]{3,2,1,0:T(8,128)(2,1)}, u32[]{:S(2)}, u32[]{:S(2)}) collective-permute-start(bf16[2,4,128,512]{3,2,1,0:T(8,128)(2,1)} %rotate_0.4.refs_3_.refs_1_), channel_id=1, source_target_pairs={{0,8},{8,0},{16,24},{24,16},{32,40},{40,32},{48,56},{56,48},{64,72... | collective-permute-start | bytes 3145736 | tf_op jit(solution)/shard_map/ppermute | solution.py:304
  3.7 1.2 copy-start.8
  7.0 3.9 %copy-start.38 = (s32[256]{0:T(256)S(1)}, s32[256]{0:T(256)}, u32[]{:S(2)}) copy-start(s32[256]{0:T(256)} %constant.22.clone) | copy-start | bytes 3076
  7.0 4.1 %copy-start.9 = (bf16[2,4,128,512]{3,2,1,0:T(8,128)(2,1)S(1)}, bf16[2,4,128,512]{3,2,1,0:T(8,128)(2,1)}, u32[]{:S(2)}) copy-start(bf16[2,4,128,512]{3,2,1,0:T(8,128)(2,1)} %rotate_0.4.refs_3_.refs_1_) | copy-start | bytes 3145732
  10.4 16.0 %collective-permute-start.3 = (bf16[2,4,128,512]{3,2,1,0:T(8,128)(2,1)}, bf16[2,4,128,512]{3,2,1,0:T(8,128)(2,1)S(1)}, u32[]{:S(2)}, u32[]{:S(2)}) collective-permute-start(bf16[2,4,128,512]{3,2,1,0:T(8,128)(2,1)} %rotate_0.5.refs_6_.refs_1_), channel_id=1, source_target_pairs={{0,8},{8,0},{16,24},{24,16},{32,40},{40,32},{48,56},{56,48},{64,72... | collective-permute-start | bytes 3145736 | tf_op jit(solution)/shard_map/ppermute | solution.py:304
  11.1 1.2 copy-start.5
  12.3 2.8 %copy-start.10 = (bf16[3,32,128,256]{3,2,1,0:T(8,128)(2,1)S(1)}, bf16[3,32,128,256]{3,2,1,0:T(8,128)(2,1)}, u32[]{:S(2)}) copy-start(bf16[3,32,128,256]{3,2,1,0:T(8,128)(2,1)} %param.9) | copy-start | bytes 18874372
  20.9 24.2 %collective-permute-start.1 = (bf16[4,128,768]{2,1,0:T(8,128)(2,1)}, bf16[4,128,768]{2,1,0:T(8,128)(2,1)}, u32[]{:S(2)}, u32[]{:S(2)}) collective-permute-start(bf16[4,128,768]{2,1,0:T(8,128)(2,1)} %get-tuple-element.14), channel_id=1, source_target_pairs={{0,16},{8,24},{16,0},{24,8},{32,48},{40,56},{48,32},{56,40},{64,80... | collective-permute-start | bytes 2359304 | tf_op jit(solution)/shard_map/ppermute | solution.py:304
  22.9 3.5 %copy-start.6 = (bf16[4,512,256]{2,1,0:T(8,128)(2,1)S(1)}, bf16[4,512,256]{2,1,0:T(8,128)(2,1)}, u32[]{:S(2)}) copy-start(bf16[4,512,256]{2,1,0:T(8,128)(2,1)} %copy-done.4) | copy-start | bytes 3145732
  22.9 3.5 %copy-start.19 = (bf16[2,4,128,512]{3,2,1,0:T(8,128)(2,1)S(1)}, bf16[2,4,128,512]{3,2,1,0:T(8,128)(2,1)}, u32[]{:S(2)}) copy-start(bf16[2,4,128,512]{3,2,1,0:T(8,128)(2,1)} %rotate_0.5.refs_6_.refs_1_) | copy-start | bytes 3145732
  26.4 11.6 %collective-permute-start.2 = (bf16[2,4,128,512]{3,2,1,0:T(8,128)(2,1)}, bf16[2,4,128,512]{3,2,1,0:T(8,128)(2,1)}, u32[]{:S(2)}, u32[]{:S(2)}) collective-permute-start(bf16[2,4,128,512]{3,2,1,0:T(8,128)(2,1)} %rotate_0.6.refs_6_.refs_1_), channel_id=1, source_target_pairs={{0,8},{8,0},{16,24},{24,16},{32,40},{40,32},{48,56},{56,48},{64,72... | collective-permute-start | bytes 3145736 | tf_op jit(solution)/shard_map/ppermute | solution.py:304
  26.4 2.8 %copy-start.11 = (bf16[3,32,128,256]{3,2,1,0:T(8,128)(2,1)S(1)}, bf16[3,32,128,256]{3,2,1,0:T(8,128)(2,1)}, u32[]{:S(2)}) copy-start(bf16[3,32,128,256]{3,2,1,0:T(8,128)(2,1)} %param.9) | copy-start | bytes 18874372
  34.1 24.4 %collective-permute-start.5 = (bf16[4,128,768]{2,1,0:T(8,128)(2,1)}, bf16[4,128,768]{2,1,0:T(8,128)(2,1)}, u32[]{:S(2)}, u32[]{:S(2)}) collective-permute-start(bf16[4,128,768]{2,1,0:T(8,128)(2,1)} %get-tuple-element.17), channel_id=1, source_target_pairs={{0,16},{8,24},{16,0},{24,8},{32,48},{40,56},{48,32},{56,40},{64,80... | collective-permute-start | bytes 2359304 | tf_op jit(solution)/shard_map/ppermute | solution.py:304
  34.1 3.9 %copy-start.23 = (bf16[2,4,128,512]{3,2,1,0:T(8,128)(2,1)S(1)}, bf16[2,4,128,512]{3,2,1,0:T(8,128)(2,1)}, u32[]{:S(2)}) copy-start(bf16[2,4,128,512]{3,2,1,0:T(8,128)(2,1)} %rotate_0.6.refs_6_.refs_1_) | copy-start | bytes 3145732
  34.1 11.0 %copy-start.36 = (bf16[4,128,512]{2,1,0:T(8,128)(2,1)S(1)}, bf16[4,128,512]{2,1,0:T(8,128)(2,1)}, u32[]{:S(2)}) copy-start(bf16[4,128,512]{2,1,0:T(8,128)(2,1)} %copy-done.35) | copy-start | bytes 1572868
  37.5 14.6 %collective-permute-start.6 = (bf16[2,4,128,512]{3,2,1,0:T(8,128)(2,1)}, bf16[2,4,128,512]{3,2,1,0:T(8,128)(2,1)S(1)}, u32[]{:S(2)}, u32[]{:S(2)}) collective-permute-start(bf16[2,4,128,512]{3,2,1,0:T(8,128)(2,1)} %rotate_0.7.refs_6_.refs_1_), channel_id=1, source_target_pairs={{0,8},{8,0},{16,24},{24,16},{32,40},{40,32},{48,56},{56,48},{64,72... | collective-permute-start | bytes 3145736 | tf_op jit(solution)/shard_map/ppermute | solution.py:304
  38.0 2.8 %copy-start.12 = (bf16[3,32,128,256]{3,2,1,0:T(8,128)(2,1)S(1)}, bf16[3,32,128,256]{3,2,1,0:T(8,128)(2,1)}, u32[]{:S(2)}) copy-start(bf16[3,32,128,256]{3,2,1,0:T(8,128)(2,1)} %param.9) | copy-start | bytes 18874372
  45.1 7.0 %copy-start.21 = (bf16[2,4,128,512]{3,2,1,0:T(8,128)(2,1)S(1)}, bf16[2,4,128,512]{3,2,1,0:T(8,128)(2,1)}, u32[]{:S(2)}) copy-start(bf16[2,4,128,512]{3,2,1,0:T(8,128)(2,1)} %rotate_0.7.refs_6_.refs_1_) | copy-start | bytes 3145732
  48.2 10.3 %copy-start.34 = (bf16[4,128,512]{2,1,0:T(8,128)(2,1)S(1)}, bf16[4,128,512]{2,1,0:T(8,128)(2,1)}, u32[]{:S(2)}) copy-start(bf16[4,128,512]{2,1,0:T(8,128)(2,1)} %copy-done.33) | copy-start | bytes 1572868
  48.2 27.9 %collective-permute-start.4 = (bf16[2,4,128,512]{3,2,1,0:T(8,128)(2,1)S(1)}, bf16[2,4,128,512]{3,2,1,0:T(8,128)(2,1)S(1)}, u32[]{:S(2)}, u32[]{:S(2)}) collective-permute-start(bf16[2,4,128,512]{3,2,1,0:T(8,128)(2,1)S(1)} %mix_1_rotate_2.4.refs_6_.refs_0_), channel_id=1, source_target_pairs={{0,48},{8,56},{16,32},{24,40},{32,16},{40,24},{48,0},{56,8},{64,11... | collective-permute-start | bytes 3145736 | tf_op jit(solution)/shard_map/ppermute | solution.py:304
  54.4 7.4 %copy-start.31 = (bf16[4,128,512]{2,1,0:T(8,128)(2,1)}, bf16[4,128,512]{2,1,0:T(8,128)(2,1)S(1)}, u32[]{:S(2)}) copy-start(bf16[4,128,512]{2,1,0:T(8,128)(2,1)S(1)} %get-tuple-element.18.refs_5_.refs_1_) | copy-start | bytes 1572868
  54.4 55.5 %collective-permute-start.11 = (bf16[4,128,768]{2,1,0:T(8,128)(2,1)S(1)}, bf16[4,128,768]{2,1,0:T(8,128)(2,1)}, u32[]{:S(2)}, u32[]{:S(2)}) collective-permute-start(bf16[4,128,768]{2,1,0:T(8,128)(2,1)S(1)} %get-tuple-element.20), channel_id=1, source_target_pairs={{0,16},{8,24},{16,0},{24,8},{32,48},{40,56},{48,32},{56,40},{64,80... | collective-permute-start | bytes 2359304 | tf_op jit(solution)/shard_map/ppermute | solution.py:304
  54.5 37.6 %collective-permute-start.9 = (bf16[4,128,768]{2,1,0:T(8,128)(2,1)S(1)}, bf16[4,128,768]{2,1,0:T(8,128)(2,1)S(1)}, u32[]{:S(2)}, u32[]{:S(2)}) collective-permute-start(bf16[4,128,768]{2,1,0:T(8,128)(2,1)S(1)} %get-tuple-element.19), channel_id=1, source_target_pairs={{0,16},{8,24},{16,0},{24,8},{32,48},{40,56},{48,32},{56,40},{64,80... | collective-permute-start | bytes 2359304 | tf_op jit(solution)/shard_map/ppermute | solution.py:304
  58.5 33.6 %slice-start = ((s8[6291456]{0:T(1024)(128)(4,1)}), s8[4194304]{0:T(1024)(128)(4,1)S(1)}, s32[]{:S(2)}) async-start(s8[6291456]{0:T(1024)(128)(4,1)} %bitcast.45), calls=%async_computation.4 | async-start | bytes 8388608
  58.5 33.6 %slice-start.1 = ((s8[6291456]{0:T(1024)(128)(4,1)}), s8[2097152]{0:T(1024)(128)(4,1)S(1)}, s32[]{:S(2)}) async-start(s8[6291456]{0:T(1024)(128)(4,1)} %bitcast.45), calls=%async_computation.5 | async-start | bytes 4194304
  61.8 37.2 %copy-start.14 = (bf16[2,4,128,512]{3,2,1,0:T(8,128)(2,1)}, bf16[2,4,128,512]{3,2,1,0:T(8,128)(2,1)S(1)}, u32[]{:S(2)}) copy-start(bf16[2,4,128,512]{3,2,1,0:T(8,128)(2,1)S(1)} %mix_1_rotate_2.5.refs_3_.refs_0_) | copy-start | bytes 3145732
  61.8 37.2 %collective-permute-start.8 = (bf16[2,4,128,512]{3,2,1,0:T(8,128)(2,1)S(1)}, bf16[2,4,128,512]{3,2,1,0:T(8,128)(2,1)S(1)}, u32[]{:S(2)}, u32[]{:S(2)}) collective-permute-start(bf16[2,4,128,512]{3,2,1,0:T(8,128)(2,1)S(1)} %mix_1_rotate_2.5.refs_3_.refs_0_), channel_id=1, source_target_pairs={{0,48},{8,56},{16,32},{24,40},{32,16},{40,24},{48,0},{56,8},{64,11... | collective-permute-start | bytes 3145736 | tf_op jit(solution)/shard_map/ppermute | solution.py:304
  76.7 26.4 %collective-permute-start.7 = (bf16[4,128,512]{2,1,0:T(8,128)(2,1)S(1)}, bf16[4,128,512]{2,1,0:T(8,128)(2,1)S(1)}, u32[]{:S(2)}, u32[]{:S(2)}) collective-permute-start(bf16[4,128,512]{2,1,0:T(8,128)(2,1)S(1)} %mix_2_other.4.refs_5_), channel_id=1, source_target_pairs={{0,16},{8,24},{16,0},{24,8},{32,48},{40,56},{48,32},{56,40},{64,80... | collective-permute-start | bytes 1572872 | tf_op jit(solution)/shard_map/ppermute | solution.py:304
  94.9 27.0 %collective-permute-start.10 = (bf16[2,4,128,512]{3,2,1,0:T(8,128)(2,1)}, bf16[2,4,128,512]{3,2,1,0:T(8,128)(2,1)}, u32[]{:S(2)}, u32[]{:S(2)}) collective-permute-start(bf16[2,4,128,512]{3,2,1,0:T(8,128)(2,1)} %mix_1_rotate_2.6.refs_3_.refs_0_), channel_id=1, source_target_pairs={{0,48},{8,56},{16,32},{24,40},{32,16},{40,24},{48,0},{56,8},{64,11... | collective-permute-start | bytes 3145736 | tf_op jit(solution)/shard_map/ppermute | solution.py:304
  99.0 1.3 copy-start.16
  100.4 23.9 %collective-permute-start.14 = (bf16[4,128,512]{2,1,0:T(8,128)(2,1)}, bf16[4,128,512]{2,1,0:T(8,128)(2,1)}, u32[]{:S(2)}, u32[]{:S(2)}) collective-permute-start(bf16[4,128,512]{2,1,0:T(8,128)(2,1)} %mix_2_other.5.refs_4_), channel_id=1, source_target_pairs={{0,16},{8,24},{16,0},{24,8},{32,48},{40,56},{48,32},{56,40},{64,80... | collective-permute-start | bytes 1572872 | tf_op jit(solution)/shard_map/ppermute | solution.py:304
  104.5 22.2 %all-to-all-start = ((bf16[8,128,512]{2,1,0:T(8,128)(2,1)}), bf16[8,128,512]{2,1,0:T(8,128)(2,1)S(1)}, u32[]{:S(2)}, u32[]{:S(2)}) async-start(bf16[8,128,512]{2,1,0:T(8,128)(2,1)} %bitcast.11), calls=%async_computation | async-start | bytes 2097152 | tf_op jit(solution)/shard_map/all_to_all | solution.py:362
  109.9 2.8 %copy-start.13 = (bf16[3,32,128,256]{3,2,1,0:T(8,128)(2,1)S(1)}, bf16[3,32,128,256]{3,2,1,0:T(8,128)(2,1)}, u32[]{:S(2)}) copy-start(bf16[3,32,128,256]{3,2,1,0:T(8,128)(2,1)} %param.9) | copy-start | bytes 18874372
  117.5 6.7 %copy-start.15 = (bf16[2,4,128,512]{3,2,1,0:T(8,128)(2,1)S(1)}, bf16[2,4,128,512]{3,2,1,0:T(8,128)(2,1)}, u32[]{:S(2)}) copy-start(bf16[2,4,128,512]{3,2,1,0:T(8,128)(2,1)} %copy-done.14) | copy-start | bytes 3145732
  117.5 6.7 %copy-start.17 = (bf16[2,4,128,512]{3,2,1,0:T(8,128)(2,1)S(1)}, bf16[2,4,128,512]{3,2,1,0:T(8,128)(2,1)}, u32[]{:S(2)}) copy-start(bf16[2,4,128,512]{3,2,1,0:T(8,128)(2,1)} %copy-done.16) | copy-start | bytes 3145732
  117.5 26.1 %collective-permute-start.13 = (bf16[2,4,128,512]{3,2,1,0:T(8,128)(2,1)}, bf16[2,4,128,512]{3,2,1,0:T(8,128)(2,1)}, u32[]{:S(2)}, u32[]{:S(2)}) collective-permute-start(bf16[2,4,128,512]{3,2,1,0:T(8,128)(2,1)} %mix_1_rotate_2.7.refs_3_.refs_0_), channel_id=1, source_target_pairs={{0,48},{8,56},{16,32},{24,40},{32,16},{40,24},{48,0},{56,8},{64,11... | collective-permute-start | bytes 3145736 | tf_op jit(solution)/shard_map/ppermute | solution.py:304
  124.2 21.7 %collective-permute-start.12 = (bf16[4,128,512]{2,1,0:T(8,128)(2,1)}, bf16[4,128,512]{2,1,0:T(8,128)(2,1)}, u32[]{:S(2)}, u32[]{:S(2)}) collective-permute-start(bf16[4,128,512]{2,1,0:T(8,128)(2,1)} %mix_2_other.6.refs_4_), channel_id=1, source_target_pairs={{0,16},{8,24},{16,0},{24,8},{32,48},{40,56},{48,32},{56,40},{64,80... | collective-permute-start | bytes 1572872 | tf_op jit(solution)/shard_map/ppermute | solution.py:304
  126.7 22.1 %all-to-all-start.1 = ((bf16[8,128,512]{2,1,0:T(8,128)(2,1)}), bf16[8,128,512]{2,1,0:T(8,128)(2,1)S(1)}, u32[]{:S(2)}, u32[]{:S(2)}) async-start(bf16[8,128,512]{2,1,0:T(8,128)(2,1)} %bitcast.13), calls=%async_computation.1 | async-start | bytes 2097152 | tf_op jit(solution)/shard_map/all_to_all | solution.py:362
  145.9 8.3 %copy-start.24 = (bf16[256,256]{1,0:T(8,128)(2,1)S(1)}, bf16[256,256]{1,0:T(8,128)(2,1)}, u32[]{:S(2)}) copy-start(bf16[256,256]{1,0:T(8,128)(2,1)} %constant.21.clone.refs_0_) | copy-start | bytes 393220
  145.9 11.6 %collective-permute-start.15 = (bf16[4,128,512]{2,1,0:T(8,128)(2,1)}, bf16[4,128,512]{2,1,0:T(8,128)(2,1)}, u32[]{:S(2)}, u32[]{:S(2)}) collective-permute-start(bf16[4,128,512]{2,1,0:T(8,128)(2,1)} %mix_2_other.7.refs_4_), channel_id=1, source_target_pairs={{0,16},{8,24},{16,0},{24,8},{32,48},{40,56},{48,32},{56,40},{64,80... | collective-permute-start | bytes 1572872 | tf_op jit(solution)/shard_map/ppermute | solution.py:304
  148.8 18.4 %all-to-all-start.2 = ((bf16[8,128,512]{2,1,0:T(8,128)(2,1)}), bf16[8,128,512]{2,1,0:T(8,128)(2,1)S(1)}, u32[]{:S(2)}, u32[]{:S(2)}) async-start(bf16[8,128,512]{2,1,0:T(8,128)(2,1)} %bitcast.29), calls=%async_computation.2 | async-start | bytes 2097152 | tf_op jit(solution)/shard_map/all_to_all | solution.py:362
  154.2 1.3 copy-start.3
  155.5 2.0 %copy-start.7 = (bf16[4,512,256]{2,1,0:T(8,128)(2,1)S(1)}, bf16[4,512,256]{2,1,0:T(8,128)(2,1)}, u32[]{:S(2)}) copy-start(bf16[4,512,256]{2,1,0:T(8,128)(2,1)} %copy-done.4) | copy-start | bytes 3145732
  167.2 18.4 %all-to-all-start.3 = ((bf16[8,128,512]{2,1,0:T(8,128)(2,1)}), bf16[8,128,512]{2,1,0:T(8,128)(2,1)S(1)}, u32[]{:S(2)}, u32[]{:S(2)}) async-start(bf16[8,128,512]{2,1,0:T(8,128)(2,1)} %bitcast.17), calls=%async_computation.3 | async-start | bytes 2097152 | tf_op jit(solution)/shard_map/all_to_all | solution.py:362
  186.9 1.5 copy-start.28
  (13 other events, 13.8 us)

commit v3 on v2

--- a/solution.py
+++ b/solution.py
@@ -12,13 +12,13 @@
 LEVELS = 3
 CHUNKS = (4, 4, 4, 4)
 STEPS = (
-    "F0", "W0", "F1", "S0", "F2", "S1", "F3", "S2", "T0", "S3", "T1", "B0",
-    "T2", "B1", "X0", "T3", "B2", "X1", "B3", "X2", "G0", "X3", "G1", "G2",
-    "G3",
+    "F0", "F1", "W0", "S0", "S1", "T0", "S2", "T1", "S3", "B0", "T2", "X0",
+    "B1", "G0", "T3", "X1", "B2", "G1", "X2", "B3", "G2", "X3", "G3",
 )
-AFTER = {"W0": ("F0",), "F1": ("W0",), "S0": ("F1",), "F2": ("S0",), "S1": ("F2",), "F3": ("S1",), "S2": ("F3",), "T0": ("S2",), "S3": ("T0",), "T1": ("S3",), "B0": ("T1",), "T2": ("B0",), "B1": ("T2",), "X0": ("B1",), "T3": ("X0",), "B2": ("T3",), "X1": ("B2",), "B3": ("X1",), "X2": ("B3",), "G0": ("X2",), "X3": ("G0",), "G1": ("X3",), "G2": ("G1",), "G3": ("G2",)}
+AFTER = {"F1": ("F0",), "W0": ("F1",), "S0": ("W0",), "S1": ("S0",), "T0": ("S1",), "S2": ("T0",), "T1": ("S2",), "S3": ("T1",), "B0": ("S3",), "T2": ("B0",), "X0": ("T2",), "B1": ("X0",), "G0": ("B1",), "T3": ("G0",), "X1": ("T3",), "B2": ("X1",), "G1": ("B2",), "X2": ("G1",), "B3": ("X2",), "G2": ("B3",), "X3": ("G2",), "G3": ("X3",)}
 STEP = 2
 FIRST_LIMIT = 60
+FIRST = ((0,), (1, 2, 3))
 LIMIT = 40
 COST = 20.0
 SB = 128
@@ -119,7 +119,10 @@
     )(meta, pattern, interp)
 
 
-def first_kernel(shuffle, coeffs, angles, out):
+def first_kernel(ahead, meta, shuffle, coeffs, angles, *refs):
+    out = refs[-2] if ahead else refs[-1]
+    if ahead:
+        refs[-1][...] = refs[0][0, 0]
     for a in range(2):
         for i in range(STEP):
             x = jnp.concatenate([coeffs[a, i, : 2 * SB], coeffs[a, i, 2 * SB :]], axis=1)
@@ -136,17 +139,23 @@
                     out[a, i, at : at + 32, W:] = im
 
 
-def first(call, shuffle, coeffs, angles, off, n):
-    return call(
-        first_kernel, "rotate_0", (n // STEP,),
-        [
-            pl.BlockSpec((W, W), lambda t: (0, 0)),
-            pl.BlockSpec((2, STEP, 4 * SB, 128), lambda t: (0, off // STEP + t, 0, 0)),
-            pl.BlockSpec((1, 2, STEP, SB, W), lambda t: (0, 0, off // STEP + t, 0, 0)),
-        ],
-        pl.BlockSpec((2, STEP, SB, 2 * W), lambda t: (0, t, 0, 0)),
-        jax.ShapeDtypeStruct((2, n, SB, 2 * W), BF), flops=n * 2e8, nbytes=n * 700e3, limit=FIRST_LIMIT,
-    )(shuffle, coeffs, angles)
+def first(call, meta, shuffle, coeffs, angles, off, n, ahead):
+    steps = n // STEP
+    out_specs = [pl.BlockSpec((2, STEP, SB, 2 * W), lambda t, *_: (0, t, 0, 0))]
+    shapes = [jax.ShapeDtypeStruct((2, n, SB, 2 * W), BF)]
+    in_specs = [
+        pl.BlockSpec((W, W), lambda t, *_: (0, 0)),
+        pl.BlockSpec((2, STEP, 4 * SB, 128), lambda t, *_: (0, off // STEP + t, 0, 0)),
+        pl.BlockSpec((1, 2, STEP, SB, W), lambda t, *_: (0, 0, off // STEP + t, 0, 0)),
+    ]
+    if ahead:
+        in_specs.append(pl.BlockSpec((1, 1, 16 // steps, SB, W), lambda t, meta: (2, 1 - meta[3], t, 0, 0)))
+        out_specs.append(pl.BlockSpec((16 // steps, SB, W), lambda t, *_: (t, 0, 0)))
+        shapes.append(jax.ShapeDtypeStruct((16, SB, W), BF))
+    return call(
+        functools.partial(first_kernel, ahead), "rotate_0", (steps,), in_specs, out_specs, shapes,
+        prefetch=1, flops=n * 2e8, nbytes=n * 700e3, limit=FIRST_LIMIT,
+    )(meta, shuffle, coeffs, angles, *([angles] if ahead else []))
 
 
 def sides(own, other):
@@ -161,22 +170,22 @@
         store(r, re, im)
 
 
-def second_kernel(meta, own, other, w, angles, ahead, keep, send):
+def second_kernel(meta, own, other, w, angles, keep, send):
     h = meta[3]
-    send[:, :, 2 * W :] = ahead[0, 0]
     for out, a in ((send, 1 - h), (keep, h)):
         for i in range(STEP):
             y = dot(sides(own[a, i], other[a, i]), w[0])
 
             def store(r, re, im, out=out, i=i):
                 out[i, r : r + 32, :W] = re
-                out[i, r : r + 32, W : 2 * W] = im
+                out[i, r : r + 32, W:] = im
 
             turn_rows(y, angles.at[0, a, i], store)
 
 
-def second(call, meta, own, other, w, angles, off, n):
-    both = pl.BlockSpec((2, STEP, SB, 2 * W), lambda t, *_: (0, t, 0, 0))
+def second(call, meta, own, other, w, angles, off, skip, n):
+    both = pl.BlockSpec((2, STEP, SB, 2 * W), lambda t, *_: (0, (off - skip) // STEP + t, 0, 0))
+    one = pl.BlockSpec((STEP, SB, 2 * W), lambda t, *_: (t, 0, 0))
     return call(
         second_kernel, "mix_0_rotate_1", (n // STEP,),
         [
@@ -184,21 +193,17 @@
             both,
             pl.BlockSpec((1, 2 * W, W), lambda t, *_: (2, 0, 0)),
             pl.BlockSpec((1, 2, STEP, SB, W), lambda t, *_: (1, 0, off // STEP + t, 0, 0)),
-            pl.BlockSpec((1, 1, STEP, SB, W), lambda t, meta: (2, 1 - meta[3], off // STEP + t, 0, 0)),
         ],
-        [
-            pl.BlockSpec((STEP, SB, 2 * W), lambda t, *_: (t, 0, 0)),
-            pl.BlockSpec((STEP, SB, 3 * W), lambda t, *_: (t, 0, 0)),
-        ],
-        [jax.ShapeDtypeStruct((n, SB, 2 * W), BF), jax.ShapeDtypeStruct((n, SB, 3 * W), BF)],
+        [one, one],
+        [jax.ShapeDtypeStruct((n, SB, 2 * W), BF)] * 2,
         prefetch=1, flops=n * 2e8, nbytes=n * 1e6,
-    )(meta, own, other, w, angles, angles)
-
-
-def third_kernel(meta, own, other, w, angles, out):
+    )(meta, own, other, w, angles)
+
+
+def third_kernel(meta, own, other, w, angles, angles_other, out):
     for i in range(STEP):
         x = sides(own[i], other[i])
-        for g, angle in ((0, angles.at[0, 0, i]), (1, other.at[i, :, 2 * W :])):
+        for g, angle in ((0, angles.at[0, 0, i]), (1, angles_other.at[i])):
             y = dot(x, w[g])
 
             def store(r, re, im, g=g, i=i):
@@ -208,18 +213,20 @@
             turn_rows(y, angle, store)
 
 
-def third(call, meta, own, other, w, angles, off, n):
+def third(call, meta, own, other, w, angles, angles_other, off, n):
+    one = pl.BlockSpec((STEP, SB, 2 * W), lambda t, *_: (t, 0, 0))
     return call(
         third_kernel, "mix_1_rotate_2", (n // STEP,),
         [
-            pl.BlockSpec((STEP, SB, 2 * W), lambda t, *_: (t, 0, 0)),
-            pl.BlockSpec((STEP, SB, 3 * W), lambda t, *_: (t, 0, 0)),
+            one,
+            one,
             pl.BlockSpec((2, 2 * W, W), lambda t, *_: (0, 0, 0)),
             pl.BlockSpec((1, 1, STEP, SB, W), lambda t, meta: (2, meta[3], off // STEP + t, 0, 0)),
+            pl.BlockSpec((STEP, SB, W), lambda t, *_: (off // STEP + t, 0, 0)),
         ],
         pl.BlockSpec((2, STEP, SB, 2 * W), lambda t, *_: (0, t, 0, 0)),
         jax.ShapeDtypeStruct((2, n, SB, 2 * W), BF), prefetch=1, flops=n * 2e8, nbytes=n * 700e3,
-    )(meta, own, other, w, angles)
+    )(meta, own, other, w, angles, angles_other)
 
 
 def back_kernel(own, other, w, out):
@@ -345,15 +352,22 @@
         if kind == "W":
             state["w"] = weights(call, meta, pattern.reshape(-1), interp)
             return
-        off, n = offs[c], CHUNKS[c]
+        off, n = (offs[c], CHUNKS[c]) if kind != "F" else (0, 0)
         if kind == "F":
-            turned = first(call, spread, coeffs, angles, off, n)
-            state["F", c] = turned, swap(turned, "src", 1)
+            group = FIRST[c]
+            skip, ahead = offs[group[0]], c == 0
+            turned = first(call, meta, spread, coeffs, angles, skip, sum(CHUNKS[k] for k in group), ahead)
+            if ahead:
+                state["A"] = swap(turned[1], "src", 2)
+            other = swap(turned[0], "src", 1)
+            for k in group:
+                state["F", k] = turned[0], other, skip
         if kind == "S":
-            keep, send = second(call, meta, *state["F", c], w, angles, off, n)
+            own, other, skip = state["F", c]
+            keep, send = second(call, meta, own, other, w, angles, off, skip, n)
             state["S", c] = keep, swap(send, "src", 2)
         if kind == "T":
-            turned = third(call, meta, *state["S", c], w, angles, off, n)
+            turned = third(call, meta, *state["S", c], w, angles, state["A"], off, n)
             state["T", c] = turned, swap(turned, "src", 6)
         if kind == "B":
             state["B", c] = swap(back(call, *state["T", c], w, n), "src", 2)

time: 198 us -> 193 us (0.975)
  local copies, waits for them, and re-layouts: 28.2 us -> 11.4 us
  waiting for transfers between devices: 59.2 us -> 70.2 us
    unnamed x83 -> x53, local copies, waits for them, and re-layouts: 28.1 us -> 11.3 us
    all_to_all x4, waiting for transfers between devices: 17 us -> 30.5 us  [step(): pieces = lax.all_to_all(pieces.reshape(-1, 2 * W), 'frq', 0, 0, tiled=True)]
    ppermute x16 -> x15, waiting for transfers between devices: 42.2 us -> 39.8 us  [swap(): lax.ppermute(value, axis, [(i, i ^ mask) for i in range(lax.axis_size(axi...]
    pallas_call x26 -> x24, Pallas kernels: 66.1 us -> 67.8 us  [go(): out = run(*operands, *before)]
    ppermute x16 -> x15, starting transfers between devices: 21.9 us -> 20.4 us  [swap(): lax.ppermute(value, axis, [(i, i ^ mask) for i in range(lax.axis_size(axi...]
  transfers between devices with their start and end apart: 20 -> 19, of which waited for: 8 -> 14; matrix products, arithmetic and copies ran while one was open for 0% -> 0% of each run, Pallas kernels for 28% -> 23%
where the time goes in v3:
time: 193 us; the launch traced here: 192 us
  waiting for transfers between devices  70.2 us (36%)
  Pallas kernels  67.8 us (35%)
  starting transfers between devices  41.7 us (22%)
  local copies, waits for them, and re-layouts  11.4 us (6%)
    pallas_call x24, Pallas kernels, go(): out = run(*operands, *before)  67.8 us
    ppermute x15, waiting for transfers between devices, swap(): lax.ppermute(value, axis, [(i, i ^ mask) for i in range(lax.axis_size(axi...  39.8 us
    all_to_all x4, waiting for transfers between devices, step(): pieces = lax.all_to_all(pieces.reshape(-1, 2 * W), 'frq', 0, 0, tiled=True)  30.5 us
    all_to_all x4, starting transfers between devices, step(): pieces = lax.all_to_all(pieces.reshape(-1, 2 * W), 'frq', 0, 0, tiled=True)  21.2 us
    ppermute x15, starting transfers between devices, swap(): lax.ppermute(value, axis, [(i, i ^ mask) for i in range(lax.axis_size(axi...  20.4 us
    unnamed x53, local copies, waits for them, and re-layouts  11.3 us
  transfers between devices with their start and end apart: 19, of which 14 were waited for; matrix products, arithmetic and copies ran while one was open for 0% of the time, Pallas kernels for 23%

profile of v3, /device:TPU:0, one launch (start us, length us, event | category | flops | bytes accessed | tf_op | source)
XLA Modules:
  0.0 192.3 jit_solution(3374586655324296249)
XLA Ops:
  0.6 4.4 %rotate_0.2 = (bf16[2,4,128,512]{3,2,1,0:T(8,128)(2,1)}, bf16[16,128,256]{2,1,0:T(8,128)(2,1)}) custom-call(s32[4]{0:T(128)} %pad_add_fusion.refs_0_, bf16[256,256]{1,0:T(8,128)(2,1)} %constant.20.clone.refs_1_, bf16[2,16,512,128]{3,2,1,0:T(8,128)(2,1)} %bitcast.45, bf16[3,2,16,128,256]{4,3,2,1,0:T(8,128)(2,1)} %bitcast.30, ...), custom_call_target="tpu_custom_call" | custom-call | flops 16000000000 | bytes 56000000 | tf_op jit(solution)/shard_map/rotate_0/pallas_call | solution.py:84
  5.0 8.2 %rotate_0.3.refs_3_.refs_1_ = bf16[2,12,128,512]{3,2,1,0:T(8,128)(2,1)} custom-call(s32[4]{0:T(128)} %pad_add_fusion.refs_0_, bf16[256,256]{1,0:T(8,128)(2,1)} %constant.20.clone.refs_1_, bf16[2,16,512,128]{3,2,1,0:T(8,128)(2,1)} %bitcast.46, bf16[3,2,16,128,256]{4,3,2,1,0:T(8,128)(2,1)} %bitcast.32, bf16[2,4,128,512]{3,2,1,0:T(8,128)(2,1)} %get-tuple-element.15.refs_4_.refs_1_), custom_call_target="tpu_custom_call" | custom-call | flops 48000000000 | bytes 168000000 | tf_op jit(solution)/shard_map/rotate_0/pallas_call | solution.py:84
  13.7 2.0 %collective-permute-start.2 = (bf16[16,128,256]{2,1,0:T(8,128)(2,1)}, bf16[16,128,256]{2,1,0:T(8,128)(2,1)}, u32[]{:S(2)}, u32[]{:S(2)}) collective-permute-start(bf16[16,128,256]{2,1,0:T(8,128)(2,1)} %get-tuple-element.18), channel_id=1, source_target_pairs={{0,16},{8,24},{16,0},{24,8},{32,48},{40,56},{48,32},{56,40},{64,80... | collective-permute-start | bytes 3145736 | tf_op jit(solution)/shard_map/ppermute | solution.py:311
  15.9 1.9 copy-done.1
  17.8 1.0 masked_weights.1.refs_3_.refs_5_.refs_2_
  18.8 1.9 collective-permute-done.refs_2_
  20.7 2.8 %copy-done.5 = bf16[3,32,128,256]{3,2,1,0:T(8,128)(2,1)S(1)} copy-done((bf16[3,32,128,256]{3,2,1,0:T(8,128)(2,1)S(1)}, bf16[3,32,128,256]{3,2,1,0:T(8,128)(2,1)}, u32[]{:S(2)}) %copy-start.5) | copy-done | bytes 6291480
  23.5 3.5 %mix_0_rotate_1.4 = (bf16[4,128,512]{2,1,0:T(8,128)(2,1)S(1)}, bf16[4,128,512]{2,1,0:T(8,128)(2,1)S(1)}) custom-call(s32[4]{0:T(128)S(1)} %copy-done.4, bf16[2,4,128,512]{3,2,1,0:T(8,128)(2,1)} %get-tuple-element.15.refs_4_.refs_1_, bf16[2,4,128,512]{3,2,1,0:T(8,128)(2,1)} %collective-permute-done.refs_2_, ...), custom_call_target="tpu_custom_call" | custom-call | flops 16000000000 | bytes 80000000 | tf_op jit(solution)/shard_map/mix_0_rotate_1/pallas_call | solution.py:84
  27.0 2.1 %collective-permute-start.1 = (bf16[4,128,512]{2,1,0:T(8,128)(2,1)S(1)}, bf16[4,128,512]{2,1,0:T(8,128)(2,1)S(1)}, u32[]{:S(2)}, u32[]{:S(2)}) collective-permute-start(bf16[4,128,512]{2,1,0:T(8,128)(2,1)S(1)} %get-tuple-element.17), channel_id=1, source_target_pairs={{0,16},{8,24},{16,0},{24,8},{32,48},{40,56},{48,32},{56,40},{64,80... | collective-permute-start | bytes 1572872 | tf_op jit(solution)/shard_map/ppermute | solution.py:311
  29.1 3.2 %mix_0_rotate_1.5 = (bf16[4,128,512]{2,1,0:T(8,128)(2,1)S(1)}, bf16[4,128,512]{2,1,0:T(8,128)(2,1)S(1)}) custom-call(s32[4]{0:T(128)S(1)} %copy-done.4, bf16[2,12,128,512]{3,2,1,0:T(8,128)(2,1)S(1)} %copy-done.2, bf16[2,12,128,512]{3,2,1,0:T(8,128)(2,1)} %collective-permute-done.3.refs_2_, bf16[4,512,256]{2,1,0:T(8,128)(2,1)S(1)} %masked_weights.1.refs_3_.refs_5_.refs_2_, ...), custom_call_target="tpu_custom_call" | custom-call | flops 16000000000 | bytes 80000000 | tf_op jit(solution)/shard_map/mix_0_rotate_1/pallas_call | solution.py:84
  32.4 7.6 %collective-permute-done.2.refs_5_ = bf16[16,128,256]{2,1,0:T(8,128)(2,1)} collective-permute-done((bf16[16,128,256]{2,1,0:T(8,128)(2,1)}, bf16[16,128,256]{2,1,0:T(8,128)(2,1)}, u32[]{:S(2)}, u32[]{:S(2)}) %collective-permute-start.2) | collective-permute-done | bytes 1048608 | tf_op jit(solution)/shard_map/ppermute | solution.py:311
  40.0 11.1 %collective-permute-done.1.refs_2_ = bf16[4,128,512]{2,1,0:T(8,128)(2,1)S(1)} collective-permute-done((bf16[4,128,512]{2,1,0:T(8,128)(2,1)S(1)}, bf16[4,128,512]{2,1,0:T(8,128)(2,1)S(1)}, u32[]{:S(2)}, u32[]{:S(2)}) %collective-permute-start.1) | collective-permute-done | bytes 524320 | tf_op jit(solution)/shard_map/ppermute | solution.py:311
  51.2 3.1 %mix_1_rotate_2.4.refs_5_.refs_0_ = bf16[2,4,128,512]{3,2,1,0:T(8,128)(2,1)S(1)} custom-call(s32[4]{0:T(128)S(1)} %copy-done.4, bf16[4,128,512]{2,1,0:T(8,128)(2,1)S(1)} %get-tuple-element.16.refs_5_.refs_1_, bf16[4,128,512]{2,1,0:T(8,128)(2,1)S(1)} %collective-permute-done.1.refs_2_, bf16[4,512,256]{2,1,0:T(8,128)(2,1)S(1)} %masked_weights.1.refs_3_.refs_5_.refs_2_, ...), custom_call_target="tpu_custom_call" | custom-call | flops 16000000000 | bytes 56000000 | tf_op jit(solution)/shard_map/mix_1_rotate_2/pallas_call | solution.py:84
  54.2 4.2 %collective-permute-start.4 = (bf16[2,4,128,512]{3,2,1,0:T(8,128)(2,1)S(1)}, bf16[2,4,128,512]{3,2,1,0:T(8,128)(2,1)S(1)}, u32[]{:S(2)}, u32[]{:S(2)}) collective-permute-start(bf16[2,4,128,512]{3,2,1,0:T(8,128)(2,1)S(1)} %mix_1_rotate_2.4.refs_5_.refs_0_), channel_id=1, source_target_pairs={{0,48},{8,56},{16,32},{24,40},{32,16},{40,24},{48,0},{56,8},{64,11... | collective-permute-start | bytes 3145736 | tf_op jit(solution)/shard_map/ppermute | solution.py:311
  58.5 3.2 %mix_0_rotate_1.6 = (bf16[4,128,512]{2,1,0:T(8,128)(2,1)S(1)}, bf16[4,128,512]{2,1,0:T(8,128)(2,1)S(1)}) custom-call(s32[4]{0:T(128)S(1)} %copy-done.4, bf16[2,12,128,512]{3,2,1,0:T(8,128)(2,1)S(1)} %copy-done.2, bf16[2,12,128,512]{3,2,1,0:T(8,128)(2,1)} %collective-permute-done.3.refs_2_, bf16[4,512,256]{2,1,0:T(8,128)(2,1)S(1)} %masked_weights.1.refs_3_.refs_5_.refs_2_, ...), custom_call_target="tpu_custom_call" | custom-call | flops 16000000000 | bytes 80000000 | tf_op jit(solution)/shard_map/mix_0_rotate_1/pallas_call | solution.py:84
  61.9 3.7 %mix_1_rotate_2.5.refs_5_.refs_0_ = bf16[2,4,128,512]{3,2,1,0:T(8,128)(2,1)} custom-call(s32[4]{0:T(128)S(1)} %copy-done.4, bf16[4,128,512]{2,1,0:T(8,128)(2,1)S(1)} %get-tuple-element.19.refs_6_.refs_1_, bf16[4,128,512]{2,1,0:T(8,128)(2,1)S(1)} %collective-permute-done.5.refs_2_, bf16[4,512,256]{2,1,0:T(8,128)(2,1)S(1)} %masked_weights.1.refs_3_.refs_5_.refs_2_, ...), custom_call_target="tpu_custom_call" | custom-call | flops 16000000000 | bytes 56000000 | tf_op jit(solution)/shard_map/mix_1_rotate_2/pallas_call | solution.py:84
  65.6 4.7 %collective-permute-start.8 = (bf16[2,4,128,512]{3,2,1,0:T(8,128)(2,1)}, bf16[2,4,128,512]{3,2,1,0:T(8,128)(2,1)}, u32[]{:S(2)}, u32[]{:S(2)}) collective-permute-start(bf16[2,4,128,512]{3,2,1,0:T(8,128)(2,1)} %mix_1_rotate_2.5.refs_5_.refs_0_), channel_id=1, source_target_pairs={{0,48},{8,56},{16,32},{24,40},{32,16},{40,24},{48,0},{56,8},{64,11... | collective-permute-start | bytes 3145736 | tf_op jit(solution)/shard_map/ppermute | solution.py:311
  70.3 3.2 %mix_0_rotate_1.7 = (bf16[4,128,512]{2,1,0:T(8,128)(2,1)S(1)}, bf16[4,128,512]{2,1,0:T(8,128)(2,1)S(1)}) custom-call(s32[4]{0:T(128)S(1)} %copy-done.4, bf16[2,12,128,512]{3,2,1,0:T(8,128)(2,1)S(1)} %copy-done.2, bf16[2,12,128,512]{3,2,1,0:T(8,128)(2,1)} %collective-permute-done.3.refs_2_, bf16[4,512,256]{2,1,0:T(8,128)(2,1)S(1)} %masked_weights.1.refs_3_.refs_5_.refs_2_, ...), custom_call_target="tpu_custom_call" | custom-call | flops 16000000000 | bytes 80000000 | tf_op jit(solution)/shard_map/mix_0_rotate_1/pallas_call | solution.py:84
  73.5 9.1 %collective-permute-done.4.refs_1_ = bf16[2,4,128,512]{3,2,1,0:T(8,128)(2,1)S(1)} collective-permute-done((bf16[2,4,128,512]{3,2,1,0:T(8,128)(2,1)S(1)}, bf16[2,4,128,512]{3,2,1,0:T(8,128)(2,1)S(1)}, u32[]{:S(2)}, u32[]{:S(2)}) %collective-permute-start.4) | collective-permute-done | bytes 1048608 | tf_op jit(solution)/shard_map/ppermute | solution.py:311
  83.3 2.8 %copy-done.6 = bf16[3,32,128,256]{3,2,1,0:T(8,128)(2,1)S(1)} copy-done((bf16[3,32,128,256]{3,2,1,0:T(8,128)(2,1)S(1)}, bf16[3,32,128,256]{3,2,1,0:T(8,128)(2,1)}, u32[]{:S(2)}) %copy-start.6) | copy-done | bytes 6291480
  86.1 3.0 %mix_1_rotate_2.6.refs_4_.refs_0_ = bf16[2,4,128,512]{3,2,1,0:T(8,128)(2,1)S(1)} custom-call(s32[4]{0:T(128)S(1)} %copy-done.4, bf16[4,128,512]{2,1,0:T(8,128)(2,1)S(1)} %get-tuple-element.21.refs_6_.refs_1_, bf16[4,128,512]{2,1,0:T(8,128)(2,1)S(1)} %collective-permute-done.7.refs_2_, bf16[4,512,256]{2,1,0:T(8,128)(2,1)S(1)} %masked_weights.1.refs_3_.refs_5_.refs_2_, ...), custom_call_target="tpu_custom_call" | custom-call | flops 16000000000 | bytes 56000000 | tf_op jit(solution)/shard_map/mix_1_rotate_2/pallas_call | solution.py:84
  89.1 3.4 %collective-permute-done.6.refs_3_ = bf16[4,128,512]{2,1,0:T(8,128)(2,1)S(1)} collective-permute-done((bf16[4,128,512]{2,1,0:T(8,128)(2,1)S(1)}, bf16[4,128,512]{2,1,0:T(8,128)(2,1)S(1)}, u32[]{:S(2)}, u32[]{:S(2)}) %collective-permute-start.6) | collective-permute-done | bytes 524320 | tf_op jit(solution)/shard_map/ppermute | solution.py:311
  92.5 1.4 mix_2_own_split.4.refs_3_
  93.9 5.3 %all-to-all-start = ((bf16[8,128,512]{2,1,0:T(8,128)(2,1)}), bf16[8,128,512]{2,1,0:T(8,128)(2,1)S(1)}, u32[]{:S(2)}, u32[]{:S(2)}) async-start(bf16[8,128,512]{2,1,0:T(8,128)(2,1)} %bitcast.11), calls=%async_computation | async-start | bytes 2097152 | tf_op jit(solution)/shard_map/all_to_all | solution.py:376
  99.3 3.3 %collective-permute-start.11 = (bf16[2,4,128,512]{3,2,1,0:T(8,128)(2,1)S(1)}, bf16[2,4,128,512]{3,2,1,0:T(8,128)(2,1)}, u32[]{:S(2)}, u32[]{:S(2)}) collective-permute-start(bf16[2,4,128,512]{3,2,1,0:T(8,128)(2,1)S(1)} %mix_1_rotate_2.6.refs_4_.refs_0_), channel_id=1, source_target_pairs={{0,48},{8,56},{16,32},{24,40},{32,16},{40,24},{48,0},{56,8},{64,11... | collective-permute-start | bytes 3145736 | tf_op jit(solution)/shard_map/ppermute | solution.py:311
  102.6 2.6 %collective-permute-done.8.refs_1_ = bf16[2,4,128,512]{3,2,1,0:T(8,128)(2,1)} collective-permute-done((bf16[2,4,128,512]{3,2,1,0:T(8,128)(2,1)}, bf16[2,4,128,512]{3,2,1,0:T(8,128)(2,1)}, u32[]{:S(2)}, u32[]{:S(2)}) %collective-permute-start.8) | collective-permute-done | bytes 1048608 | tf_op jit(solution)/shard_map/ppermute | solution.py:311
  105.1 2.4 %mix_2_other.5.refs_2_ = bf16[4,128,512]{2,1,0:T(8,128)(2,1)} custom-call(bf16[2,4,128,512]{3,2,1,0:T(8,128)(2,1)} %mix_1_rotate_2.5.refs_5_.refs_0_, bf16[2,4,128,512]{3,2,1,0:T(8,128)(2,1)} %collective-permute-done.8.refs_1_, bf16[4,512,256]{2,1,0:T(8,128)(2,1)S(1)} %masked_weights.1.refs_3_.refs_5_.refs_2_, bf16[8,2,4,16,512]{4,3,2,1,0:T(8,128)(2,1)} %mix_2_own_split.4.refs_3_), custom_call_target="tpu_custom_call" | custom-call | flops 8000000000 | bytes 32000000 | tf_op jit(solution)/shard_map/mix_2_other/pallas_call | solution.py:84
  107.5 3.2 %all-to-all-done = bf16[8,128,512]{2,1,0:T(8,128)(2,1)S(1)} async-done(((bf16[8,128,512]{2,1,0:T(8,128)(2,1)}), bf16[8,128,512]{2,1,0:T(8,128)(2,1)S(1)}, u32[]{:S(2)}, u32[]{:S(2)}) %all-to-all-start) | async-done | bytes 1048608 | tf_op jit(solution)/shard_map/all_to_all | solution.py:376
  110.7 1.0 gather_frequencies.4.refs_6_.refs_1_
  112.1 2.8 %copy-done.7 = bf16[3,32,128,256]{3,2,1,0:T(8,128)(2,1)S(1)} copy-done((bf16[3,32,128,256]{3,2,1,0:T(8,128)(2,1)S(1)}, bf16[3,32,128,256]{3,2,1,0:T(8,128)(2,1)}, u32[]{:S(2)}) %copy-start.7) | copy-done | bytes 6291480
  114.9 3.1 %mix_1_rotate_2.7.refs_4_.refs_0_ = bf16[2,4,128,512]{3,2,1,0:T(8,128)(2,1)S(1)} custom-call(s32[4]{0:T(128)S(1)} %copy-done.4, bf16[4,128,512]{2,1,0:T(8,128)(2,1)S(1)} %copy-done.19, bf16[4,128,512]{2,1,0:T(8,128)(2,1)} %collective-permute-done.10.refs_2_, bf16[4,512,256]{2,1,0:T(8,128)(2,1)S(1)} %masked_weights.1.refs_3_.refs_5_.refs_2_, ...), custom_call_target="tpu_custom_call" | custom-call | flops 16000000000 | bytes 56000000 | tf_op jit(solution)/shard_map/mix_1_rotate_2/pallas_call | solution.py:84
  118.0 2.0 %collective-permute-done.9.refs_3_ = bf16[4,128,512]{2,1,0:T(8,128)(2,1)} collective-permute-done((bf16[4,128,512]{2,1,0:T(8,128)(2,1)}, bf16[4,128,512]{2,1,0:T(8,128)(2,1)}, u32[]{:S(2)}, u32[]{:S(2)}) %collective-permute-start.9) | collective-permute-done | bytes 524320 | tf_op jit(solution)/shard_map/ppermute | solution.py:311
  120.0 2.6 %mix_2_own_split.5.refs_3_ = bf16[8,2,4,16,512]{4,3,2,1,0:T(8,128)(2,1)} custom-call(bf16[2,4,128,512]{3,2,1,0:T(8,128)(2,1)} %mix_1_rotate_2.5.refs_5_.refs_0_, bf16[2,4,128,512]{3,2,1,0:T(8,128)(2,1)} %collective-permute-done.8.refs_1_, bf16[4,512,256]{2,1,0:T(8,128)(2,1)S(1)} %masked_weights.1.refs_3_.refs_5_.refs_2_, ...), custom_call_target="tpu_custom_call" | custom-call | flops 8000000000 | bytes 64000000 | tf_op jit(solution)/shard_map/mix_2_own_split/pallas_call | solution.py:84
  122.6 5.6 %all-to-all-start.1 = ((bf16[8,128,512]{2,1,0:T(8,128)(2,1)}), bf16[8,128,512]{2,1,0:T(8,128)(2,1)S(1)}, u32[]{:S(2)}, u32[]{:S(2)}) async-start(bf16[8,128,512]{2,1,0:T(8,128)(2,1)} %bitcast.13), calls=%async_computation.1 | async-start | bytes 2097152 | tf_op jit(solution)/shard_map/all_to_all | solution.py:376
  128.2 3.2 %collective-permute-start.13 = (bf16[2,4,128,512]{3,2,1,0:T(8,128)(2,1)}, bf16[2,4,128,512]{3,2,1,0:T(8,128)(2,1)}, u32[]{:S(2)}, u32[]{:S(2)}) collective-permute-start(bf16[2,4,128,512]{3,2,1,0:T(8,128)(2,1)} %copy-done.8), channel_id=1, source_target_pairs={{0,48},{8,56},{16,32},{24,40},{32,16},{40,24},{48,0},{56,8},{64,11... | collective-permute-start | bytes 3145736 | tf_op jit(solution)/shard_map/ppermute | solution.py:311
  131.4 2.3 %mix_2_other.6.refs_2_ = bf16[4,128,512]{2,1,0:T(8,128)(2,1)} custom-call(bf16[2,4,128,512]{3,2,1,0:T(8,128)(2,1)S(1)} %mix_1_rotate_2.6.refs_4_.refs_0_, bf16[2,4,128,512]{3,2,1,0:T(8,128)(2,1)} %collective-permute-done.11.refs_1_, bf16[4,512,256]{2,1,0:T(8,128)(2,1)S(1)} %masked_weights.1.refs_3_.refs_5_.refs_2_, ...), custom_call_target="tpu_custom_call" | custom-call | flops 8000000000 | bytes 32000000 | tf_op jit(solution)/shard_map/mix_2_other/pallas_call | solution.py:84
  133.7 6.8 %all-to-all-done.1 = bf16[8,128,512]{2,1,0:T(8,128)(2,1)S(1)} async-done(((bf16[8,128,512]{2,1,0:T(8,128)(2,1)}), bf16[8,128,512]{2,1,0:T(8,128)(2,1)S(1)}, u32[]{:S(2)}, u32[]{:S(2)}) %all-to-all-start.1) | async-done | bytes 1048608 | tf_op jit(solution)/shard_map/all_to_all | solution.py:376
  140.6 1.0 gather_frequencies.5.refs_4_.refs_2_
  141.6 1.7 collective-permute-done.12.refs_3_
  143.2 2.5 %mix_2_own_split.6.refs_3_ = bf16[8,2,4,16,512]{4,3,2,1,0:T(8,128)(2,1)} custom-call(bf16[2,4,128,512]{3,2,1,0:T(8,128)(2,1)S(1)} %mix_1_rotate_2.6.refs_4_.refs_0_, bf16[2,4,128,512]{3,2,1,0:T(8,128)(2,1)} %collective-permute-done.11.refs_1_, bf16[4,512,256]{2,1,0:T(8,128)(2,1)S(1)} %masked_weights.1.refs_3_.refs_5_.refs_2_, ...), custom_call_target="tpu_custom_call" | custom-call | flops 8000000000 | bytes 64000000 | tf_op jit(solution)/shard_map/mix_2_own_split/pallas_call | solution.py:84
  145.7 5.7 %all-to-all-start.2 = ((bf16[8,128,512]{2,1,0:T(8,128)(2,1)}), bf16[8,128,512]{2,1,0:T(8,128)(2,1)S(1)}, u32[]{:S(2)}, u32[]{:S(2)}) async-start(bf16[8,128,512]{2,1,0:T(8,128)(2,1)} %bitcast.15), calls=%async_computation.2 | async-start | bytes 2097152 | tf_op jit(solution)/shard_map/all_to_all | solution.py:376
  151.4 2.3 %mix_2_other.7.refs_2_ = bf16[4,128,512]{2,1,0:T(8,128)(2,1)} custom-call(bf16[2,4,128,512]{3,2,1,0:T(8,128)(2,1)S(1)} %copy-done.9, bf16[2,4,128,512]{3,2,1,0:T(8,128)(2,1)} %collective-permute-done.13.refs_1_, bf16[4,512,256]{2,1,0:T(8,128)(2,1)S(1)} %masked_weights.1.refs_3_.refs_5_.refs_2_, bf16[8,2,4,16,512]{4,3,2,1,0:T(8,128)(2,1)} %mix_2_own_split.6.refs_3_), custom_call_target="tpu_custom_call" | custom-call | flops 8000000000 | bytes 32000000 | tf_op jit(solution)/shard_map/mix_2_other/pallas_call | solution.py:84
  153.7 9.2 %all-to-all-done.2 = bf16[8,128,512]{2,1,0:T(8,128)(2,1)S(1)} async-done(((bf16[8,128,512]{2,1,0:T(8,128)(2,1)}), bf16[8,128,512]{2,1,0:T(8,128)(2,1)S(1)}, u32[]{:S(2)}, u32[]{:S(2)}) %all-to-all-start.2) | async-done | bytes 1048608 | tf_op jit(solution)/shard_map/all_to_all | solution.py:376
  162.9 1.0 gather_frequencies.6.refs_4_.refs_3_
  163.9 2.9 %mix_2_own_split.7.refs_2_ = bf16[8,2,4,16,512]{4,3,2,1,0:T(8,128)(2,1)} custom-call(bf16[2,4,128,512]{3,2,1,0:T(8,128)(2,1)S(1)} %copy-done.9, bf16[2,4,128,512]{3,2,1,0:T(8,128)(2,1)} %collective-permute-done.13.refs_1_, bf16[4,512,256]{2,1,0:T(8,128)(2,1)S(1)} %masked_weights.1.refs_3_.refs_5_.refs_2_, ...), custom_call_target="tpu_custom_call" | custom-call | flops 8000000000 | bytes 64000000 | tf_op jit(solution)/shard_map/mix_2_own_split/pallas_call | solution.py:84
  166.8 4.6 %all-to-all-start.3 = ((bf16[8,128,512]{2,1,0:T(8,128)(2,1)}), bf16[8,128,512]{2,1,0:T(8,128)(2,1)S(1)}, u32[]{:S(2)}, u32[]{:S(2)}) async-start(bf16[8,128,512]{2,1,0:T(8,128)(2,1)} %bitcast.17), calls=%async_computation.3 | async-start | bytes 2097152 | tf_op jit(solution)/shard_map/all_to_all | solution.py:376
  171.6 11.3 %all-to-all-done.3 = bf16[8,128,512]{2,1,0:T(8,128)(2,1)S(1)} async-done(((bf16[8,128,512]{2,1,0:T(8,128)(2,1)}), bf16[8,128,512]{2,1,0:T(8,128)(2,1)S(1)}, u32[]{:S(2)}, u32[]{:S(2)}) %all-to-all-start.3) | async-done | bytes 1048608 | tf_op jit(solution)/shard_map/all_to_all | solution.py:376
  184.7 7.6 %target_map.1 = f32[256,64,128]{2,1,0:T(8,128)} custom-call(bf16[256,256]{1,0:T(8,128)(2,1)S(1)} %fusion.refs_0_, bf16[16,64,512]{2,1,0:T(8,128)(2,1)S(1)} %copy-done.17, bf16[16,64,512]{2,1,0:T(8,128)(2,1)S(1)} %copy-done.13, bf16[16,64,512]{2,1,0:T(8,128)(2,1)S(1)} %copy-done.15, bf16[16,64,512]{2,1,0:T(8,128)(2,1)S(1)} %gather_frequencies.7.refs_4_), custom_call_target="tpu_custom_call" | custom-call | flops 20000000000 | bytes 251658240 | tf_op jit(solution)/shard_map/target_map/pallas_call | solution.py:84
  (73 shorter events, 4.9 us)
Async XLA Ops:
  0.0 171.4 %copy-start = (bf16[256,256]{1,0:T(8,128)(2,1)S(1)}, bf16[256,256]{1,0:T(8,128)(2,1)}, u32[]{:S(2)}) copy-start(bf16[256,256]{1,0:T(8,128)(2,1)} %param.12) | copy-start | bytes 393220
  5.0 10.7 %copy-start.20 = (s32[3,4,2]{1,2,0:T(2,128)S(1)}, s32[3,4,2]{1,2,0:T(2,128)}, u32[]{:S(2)}) copy-start(s32[3,4,2]{1,2,0:T(2,128)} %param.11) | copy-start | bytes 292
  5.0 10.9 %copy-start.3 = (bf16[3,2,2,256,256]{4,3,2,1,0:T(8,128)(2,1)S(1)}, bf16[3,2,2,256,256]{4,3,2,1,0:T(8,128)(2,1)}, u32[]{:S(2)}) copy-start(bf16[3,2,2,256,256]{4,3,2,1,0:T(8,128)(2,1)} %refs_2_.1) | copy-start | bytes 4718596
  5.0 10.9 %copy-start.4 = (s32[4]{0:T(128)S(1)}, s32[4]{0:T(128)}, u32[]{:S(2)}) copy-start(s32[4]{0:T(128)} %pad_add_fusion.refs_0_) | copy-start | bytes 52
  13.2 15.9 %collective-permute-start.3 = (bf16[2,12,128,512]{3,2,1,0:T(8,128)(2,1)}, bf16[2,12,128,512]{3,2,1,0:T(8,128)(2,1)}, u32[]{:S(2)}, u32[]{:S(2)}) collective-permute-start(bf16[2,12,128,512]{3,2,1,0:T(8,128)(2,1)} %rotate_0.3.refs_3_.refs_1_), channel_id=1, source_target_pairs={{0,8},{8,0},{16,24},{24,16},{32,40},{40,32},{48,56},{56,48},{64,72... | collective-permute-start | bytes 9437192 | tf_op jit(solution)/shard_map/ppermute | solution.py:311
  13.2 7.5 %collective-permute-start = (bf16[2,4,128,512]{3,2,1,0:T(8,128)(2,1)}, bf16[2,4,128,512]{3,2,1,0:T(8,128)(2,1)}, u32[]{:S(2)}, u32[]{:S(2)}) collective-permute-start(bf16[2,4,128,512]{3,2,1,0:T(8,128)(2,1)} %get-tuple-element.15.refs_4_.refs_1_), channel_id=1, source_target_pairs={{0,8},{8,0},{16,24},{24,16},{32,40},{40,32},{48,56},{56,48},{64,72... | collective-permute-start | bytes 3145736 | tf_op jit(solution)/shard_map/ppermute | solution.py:311
  13.7 26.3 %collective-permute-start.2 = (bf16[16,128,256]{2,1,0:T(8,128)(2,1)}, bf16[16,128,256]{2,1,0:T(8,128)(2,1)}, u32[]{:S(2)}, u32[]{:S(2)}) collective-permute-start(bf16[16,128,256]{2,1,0:T(8,128)(2,1)} %get-tuple-element.18), channel_id=1, source_target_pairs={{0,16},{8,24},{16,0},{24,8},{32,48},{40,56},{48,32},{56,40},{64,80... | collective-permute-start | bytes 3145736 | tf_op jit(solution)/shard_map/ppermute | solution.py:311
  15.9 1.9 copy-start.1
  18.8 10.3 %copy-start.2 = (bf16[2,12,128,512]{3,2,1,0:T(8,128)(2,1)S(1)}, bf16[2,12,128,512]{3,2,1,0:T(8,128)(2,1)}, u32[]{:S(2)}) copy-start(bf16[2,12,128,512]{3,2,1,0:T(8,128)(2,1)} %rotate_0.3.refs_3_.refs_1_) | copy-start | bytes 9437188
  20.7 2.8 %copy-start.5 = (bf16[3,32,128,256]{3,2,1,0:T(8,128)(2,1)S(1)}, bf16[3,32,128,256]{3,2,1,0:T(8,128)(2,1)}, u32[]{:S(2)}) copy-start(bf16[3,32,128,256]{3,2,1,0:T(8,128)(2,1)} %param.9) | copy-start | bytes 18874372
  23.5 27.7 %slice-start = ((s8[6291456]{0:T(1024)(128)(4,1)}), s8[4194304]{0:T(1024)(128)(4,1)S(1)}, s32[]{:S(2)}) async-start(s8[6291456]{0:T(1024)(128)(4,1)} %bitcast.37), calls=%async_computation.4 | async-start | bytes 8388608
  27.0 24.2 %collective-permute-start.1 = (bf16[4,128,512]{2,1,0:T(8,128)(2,1)S(1)}, bf16[4,128,512]{2,1,0:T(8,128)(2,1)S(1)}, u32[]{:S(2)}, u32[]{:S(2)}) collective-permute-start(bf16[4,128,512]{2,1,0:T(8,128)(2,1)S(1)} %get-tuple-element.17), channel_id=1, source_target_pairs={{0,16},{8,24},{16,0},{24,8},{32,48},{40,56},{48,32},{56,40},{64,80... | collective-permute-start | bytes 1572872 | tf_op jit(solution)/shard_map/ppermute | solution.py:311
  29.1 22.1 %slice-start.1 = ((s8[6291456]{0:T(1024)(128)(4,1)}), s8[2097152]{0:T(1024)(128)(4,1)S(1)}, s32[]{:S(2)}) async-start(s8[6291456]{0:T(1024)(128)(4,1)} %bitcast.37), calls=%async_computation.5 | async-start | bytes 4194304
  32.3 29.5 %collective-permute-start.5 = (bf16[4,128,512]{2,1,0:T(8,128)(2,1)S(1)}, bf16[4,128,512]{2,1,0:T(8,128)(2,1)S(1)}, u32[]{:S(2)}, u32[]{:S(2)}) collective-permute-start(bf16[4,128,512]{2,1,0:T(8,128)(2,1)S(1)} %get-tuple-element.20), channel_id=1, source_target_pairs={{0,16},{8,24},{16,0},{24,8},{32,48},{40,56},{48,32},{56,40},{64,80... | collective-permute-start | bytes 1572872 | tf_op jit(solution)/shard_map/ppermute | solution.py:311
  51.2 10.7 %slice-start.2 = ((s8[6291456]{0:T(1024)(128)(4,1)}), s8[2097152]{0:T(1024)(128)(4,1)S(1)}, s32[]{:S(2)}) async-start(s8[6291456]{0:T(1024)(128)(4,1)} %bitcast.40), calls=%async_computation.6 | async-start | bytes 4194304
  54.2 7.6 %slice-start.3 = ((s8[6291456]{0:T(1024)(128)(4,1)}), s8[4194304]{0:T(1024)(128)(4,1)S(1)}, s32[]{:S(2)}) async-start(s8[6291456]{0:T(1024)(128)(4,1)} %bitcast.40), calls=%async_computation.7 | async-start | bytes 8388608
  54.2 28.3 %collective-permute-start.4 = (bf16[2,4,128,512]{3,2,1,0:T(8,128)(2,1)S(1)}, bf16[2,4,128,512]{3,2,1,0:T(8,128)(2,1)S(1)}, u32[]{:S(2)}, u32[]{:S(2)}) collective-permute-start(bf16[2,4,128,512]{3,2,1,0:T(8,128)(2,1)S(1)} %mix_1_rotate_2.4.refs_5_.refs_0_), channel_id=1, source_target_pairs={{0,48},{8,56},{16,32},{24,40},{32,16},{40,24},{48,0},{56,8},{64,11... | collective-permute-start | bytes 3145736 | tf_op jit(solution)/shard_map/ppermute | solution.py:311
  61.7 21.6 %collective-permute-start.7 = (bf16[4,128,512]{2,1,0:T(8,128)(2,1)S(1)}, bf16[4,128,512]{2,1,0:T(8,128)(2,1)S(1)}, u32[]{:S(2)}, u32[]{:S(2)}) collective-permute-start(bf16[4,128,512]{2,1,0:T(8,128)(2,1)S(1)} %get-tuple-element.23), channel_id=1, source_target_pairs={{0,16},{8,24},{16,0},{24,8},{32,48},{40,56},{48,32},{56,40},{64,80... | collective-permute-start | bytes 1572872 | tf_op jit(solution)/shard_map/ppermute | solution.py:311
  65.6 39.6 %collective-permute-start.8 = (bf16[2,4,128,512]{3,2,1,0:T(8,128)(2,1)}, bf16[2,4,128,512]{3,2,1,0:T(8,128)(2,1)}, u32[]{:S(2)}, u32[]{:S(2)}) collective-permute-start(bf16[2,4,128,512]{3,2,1,0:T(8,128)(2,1)} %mix_1_rotate_2.5.refs_5_.refs_0_), channel_id=1, source_target_pairs={{0,48},{8,56},{16,32},{24,40},{32,16},{40,24},{48,0},{56,8},{64,11... | collective-permute-start | bytes 3145736 | tf_op jit(solution)/shard_map/ppermute | solution.py:311
  73.5 9.7 %copy-start.10 = (bf16[4,128,512]{2,1,0:T(8,128)(2,1)}, bf16[4,128,512]{2,1,0:T(8,128)(2,1)S(1)}, u32[]{:S(2)}) copy-start(bf16[4,128,512]{2,1,0:T(8,128)(2,1)S(1)} %get-tuple-element.24) | copy-start | bytes 1572868
  73.5 9.7 %copy-start.18 = (bf16[4,128,512]{2,1,0:T(8,128)(2,1)}, bf16[4,128,512]{2,1,0:T(8,128)(2,1)S(1)}, u32[]{:S(2)}) copy-start(bf16[4,128,512]{2,1,0:T(8,128)(2,1)S(1)} %get-tuple-element.22.refs_3_.refs_1_) | copy-start | bytes 1572868
  83.2 9.3 %collective-permute-start.6 = (bf16[4,128,512]{2,1,0:T(8,128)(2,1)S(1)}, bf16[4,128,512]{2,1,0:T(8,128)(2,1)S(1)}, u32[]{:S(2)}, u32[]{:S(2)}) collective-permute-start(bf16[4,128,512]{2,1,0:T(8,128)(2,1)S(1)} %mix_2_other.4.refs_6_), channel_id=1, source_target_pairs={{0,16},{8,24},{16,0},{24,8},{32,48},{40,56},{48,32},{56,40},{64,80... | collective-permute-start | bytes 1572872 | tf_op jit(solution)/shard_map/ppermute | solution.py:311
  83.3 2.8 %copy-start.6 = (bf16[3,32,128,256]{3,2,1,0:T(8,128)(2,1)S(1)}, bf16[3,32,128,256]{3,2,1,0:T(8,128)(2,1)}, u32[]{:S(2)}) copy-start(bf16[3,32,128,256]{3,2,1,0:T(8,128)(2,1)} %param.9) | copy-start | bytes 18874372
  93.9 16.8 %all-to-all-start = ((bf16[8,128,512]{2,1,0:T(8,128)(2,1)}), bf16[8,128,512]{2,1,0:T(8,128)(2,1)S(1)}, u32[]{:S(2)}, u32[]{:S(2)}) async-start(bf16[8,128,512]{2,1,0:T(8,128)(2,1)} %bitcast.11), calls=%async_computation | async-start | bytes 2097152 | tf_op jit(solution)/shard_map/all_to_all | solution.py:376
  99.2 11.5 %copy-start.11 = (bf16[256,256]{1,0:T(8,128)(2,1)S(1)}, bf16[256,256]{1,0:T(8,128)(2,1)}, u32[]{:S(2)}) copy-start(bf16[256,256]{1,0:T(8,128)(2,1)} %constant.21.clone.refs_0_) | copy-start | bytes 393220
  99.2 12.9 %collective-permute-start.10 = (bf16[4,128,512]{2,1,0:T(8,128)(2,1)}, bf16[4,128,512]{2,1,0:T(8,128)(2,1)}, u32[]{:S(2)}, u32[]{:S(2)}) collective-permute-start(bf16[4,128,512]{2,1,0:T(8,128)(2,1)} %copy-done.10), channel_id=1, source_target_pairs={{0,16},{8,24},{16,0},{24,8},{32,48},{40,56},{48,32},{56,40},{64,80... | collective-permute-start | bytes 1572872 | tf_op jit(solution)/shard_map/ppermute | solution.py:311
  99.3 32.2 %collective-permute-start.11 = (bf16[2,4,128,512]{3,2,1,0:T(8,128)(2,1)S(1)}, bf16[2,4,128,512]{3,2,1,0:T(8,128)(2,1)}, u32[]{:S(2)}, u32[]{:S(2)}) collective-permute-start(bf16[2,4,128,512]{3,2,1,0:T(8,128)(2,1)S(1)} %mix_1_rotate_2.6.refs_4_.refs_0_), channel_id=1, source_target_pairs={{0,48},{8,56},{16,32},{24,40},{32,16},{40,24},{48,0},{56,8},{64,11... | collective-permute-start | bytes 3145736 | tf_op jit(solution)/shard_map/ppermute | solution.py:311
  107.5 12.5 %collective-permute-start.9 = (bf16[4,128,512]{2,1,0:T(8,128)(2,1)}, bf16[4,128,512]{2,1,0:T(8,128)(2,1)}, u32[]{:S(2)}, u32[]{:S(2)}) collective-permute-start(bf16[4,128,512]{2,1,0:T(8,128)(2,1)} %mix_2_other.5.refs_2_), channel_id=1, source_target_pairs={{0,16},{8,24},{16,0},{24,8},{32,48},{40,56},{48,32},{56,40},{64,80... | collective-permute-start | bytes 1572872 | tf_op jit(solution)/shard_map/ppermute | solution.py:311
  110.7 1.4 copy-start.19
  111.7 6.3 %copy-start.16 = (bf16[16,64,512]{2,1,0:T(8,128)(2,1)}, bf16[16,64,512]{2,1,0:T(8,128)(2,1)S(1)}, u32[]{:S(2)}) copy-start(bf16[16,64,512]{2,1,0:T(8,128)(2,1)S(1)} %gather_frequencies.4.refs_6_.refs_1_) | copy-start | bytes 3145732
  112.1 2.8 %copy-start.7 = (bf16[3,32,128,256]{3,2,1,0:T(8,128)(2,1)S(1)}, bf16[3,32,128,256]{3,2,1,0:T(8,128)(2,1)}, u32[]{:S(2)}) copy-start(bf16[3,32,128,256]{3,2,1,0:T(8,128)(2,1)} %param.9) | copy-start | bytes 18874372
  118.0 4.6 %copy-start.8 = (bf16[2,4,128,512]{3,2,1,0:T(8,128)(2,1)}, bf16[2,4,128,512]{3,2,1,0:T(8,128)(2,1)S(1)}, u32[]{:S(2)}) copy-start(bf16[2,4,128,512]{3,2,1,0:T(8,128)(2,1)S(1)} %mix_1_rotate_2.7.refs_4_.refs_0_) | copy-start | bytes 3145732
  122.6 18.0 %all-to-all-start.1 = ((bf16[8,128,512]{2,1,0:T(8,128)(2,1)}), bf16[8,128,512]{2,1,0:T(8,128)(2,1)S(1)}, u32[]{:S(2)}, u32[]{:S(2)}) async-start(bf16[8,128,512]{2,1,0:T(8,128)(2,1)} %bitcast.13), calls=%async_computation.1 | async-start | bytes 2097152 | tf_op jit(solution)/shard_map/all_to_all | solution.py:376
  128.2 23.2 %collective-permute-start.13 = (bf16[2,4,128,512]{3,2,1,0:T(8,128)(2,1)}, bf16[2,4,128,512]{3,2,1,0:T(8,128)(2,1)}, u32[]{:S(2)}, u32[]{:S(2)}) collective-permute-start(bf16[2,4,128,512]{3,2,1,0:T(8,128)(2,1)} %copy-done.8), channel_id=1, source_target_pairs={{0,48},{8,56},{16,32},{24,40},{32,16},{40,24},{48,0},{56,8},{64,11... | collective-permute-start | bytes 3145736 | tf_op jit(solution)/shard_map/ppermute | solution.py:311
  133.7 9.5 %collective-permute-start.12 = (bf16[4,128,512]{2,1,0:T(8,128)(2,1)}, bf16[4,128,512]{2,1,0:T(8,128)(2,1)}, u32[]{:S(2)}, u32[]{:S(2)}) collective-permute-start(bf16[4,128,512]{2,1,0:T(8,128)(2,1)} %mix_2_other.6.refs_2_), channel_id=1, source_target_pairs={{0,16},{8,24},{16,0},{24,8},{32,48},{40,56},{48,32},{56,40},{64,80... | collective-permute-start | bytes 1572872 | tf_op jit(solution)/shard_map/ppermute | solution.py:311
  141.5 4.2 %copy-start.12 = (bf16[16,64,512]{2,1,0:T(8,128)(2,1)}, bf16[16,64,512]{2,1,0:T(8,128)(2,1)S(1)}, u32[]{:S(2)}) copy-start(bf16[16,64,512]{2,1,0:T(8,128)(2,1)S(1)} %gather_frequencies.5.refs_4_.refs_2_) | copy-start | bytes 3145732
  141.6 9.9 %copy-start.9 = (bf16[2,4,128,512]{3,2,1,0:T(8,128)(2,1)S(1)}, bf16[2,4,128,512]{3,2,1,0:T(8,128)(2,1)}, u32[]{:S(2)}) copy-start(bf16[2,4,128,512]{3,2,1,0:T(8,128)(2,1)} %copy-done.8) | copy-start | bytes 3145732
  145.7 17.2 %all-to-all-start.2 = ((bf16[8,128,512]{2,1,0:T(8,128)(2,1)}), bf16[8,128,512]{2,1,0:T(8,128)(2,1)S(1)}, u32[]{:S(2)}, u32[]{:S(2)}) async-start(bf16[8,128,512]{2,1,0:T(8,128)(2,1)} %bitcast.15), calls=%async_computation.2 | async-start | bytes 2097152 | tf_op jit(solution)/shard_map/all_to_all | solution.py:376
  153.7 10.2 %collective-permute-start.14 = (bf16[4,128,512]{2,1,0:T(8,128)(2,1)}, bf16[4,128,512]{2,1,0:T(8,128)(2,1)}, u32[]{:S(2)}, u32[]{:S(2)}) collective-permute-start(bf16[4,128,512]{2,1,0:T(8,128)(2,1)} %mix_2_other.7.refs_2_), channel_id=1, source_target_pairs={{0,16},{8,24},{16,0},{24,8},{32,48},{40,56},{48,32},{56,40},{64,80... | collective-permute-start | bytes 1572872 | tf_op jit(solution)/shard_map/ppermute | solution.py:311
  163.9 2.9 %copy-start.14 = (bf16[16,64,512]{2,1,0:T(8,128)(2,1)}, bf16[16,64,512]{2,1,0:T(8,128)(2,1)S(1)}, u32[]{:S(2)}) copy-start(bf16[16,64,512]{2,1,0:T(8,128)(2,1)S(1)} %gather_frequencies.6.refs_4_.refs_3_) | copy-start | bytes 3145732
  163.9 7.5 %copy-start.21 = (s32[256]{0:T(256)S(1)}, s32[256]{0:T(256)}, u32[]{:S(2)}) copy-start(s32[256]{0:T(256)} %constant.22.clone) | copy-start | bytes 3076
  166.8 16.1 %all-to-all-start.3 = ((bf16[8,128,512]{2,1,0:T(8,128)(2,1)}), bf16[8,128,512]{2,1,0:T(8,128)(2,1)S(1)}, u32[]{:S(2)}, u32[]{:S(2)}) async-start(bf16[8,128,512]{2,1,0:T(8,128)(2,1)} %bitcast.17), calls=%async_computation.3 | async-start | bytes 2097152 | tf_op jit(solution)/shard_map/all_to_all | solution.py:376
  182.9 1.2 copy-start.13
  182.9 1.5 copy-start.15
  182.9 1.9 copy-start.17

commit v4 on v3

--- a/solution.py
+++ b/solution.py
@@ -16,6 +16,7 @@
     "B1", "G0", "T3", "X1", "B2", "G1", "X2", "B3", "G2", "X3", "G3",
 )
 AFTER = {"F1": ("F0",), "W0": ("F1",), "S0": ("W0",), "S1": ("S0",), "T0": ("S1",), "S2": ("T0",), "T1": ("S2",), "S3": ("T1",), "B0": ("S3",), "T2": ("B0",), "X0": ("T2",), "B1": ("X0",), "G0": ("B1",), "T3": ("G0",), "X1": ("T3",), "B2": ("X1",), "G1": ("B2",), "X2": ("G1",), "B3": ("X2",), "G2": ("B3",), "X3": ("G2",), "G3": ("X3",)}
+LIGHT = ("G0", "T3", "X1", "B2", "G1", "X2", "B3", "G2", "X3", "G3")
 STEP = 2
 FIRST_LIMIT = 60
 FIRST = ((0,), (1, 2, 3))
@@ -57,6 +58,7 @@
 class Order:
     def __init__(self):
         self.last = []
+        self.scale = COST
 
     def __call__(self, kernel, name, grid, in_specs, out_specs, out_shape, prefetch=0, scratch=(), flops=0, nbytes=0, limit=None):
         at = prefetch + len(in_specs)
@@ -64,7 +66,7 @@
         def body(*refs):
             kernel(*refs[:at], *refs[at + len(before) :])
 
-        before = list(self.last)
+        before, scale = list(self.last), self.scale
         run = pl.pallas_call(
             body,
             out_shape=out_shape,
@@ -76,7 +78,7 @@
                 scratch_shapes=list(scratch),
             ),
             compiler_params=pltpu.CompilerParams(vmem_limit_bytes=(limit or LIMIT) << 20),
-            cost_estimate=pl.CostEstimate(flops=int(flops * COST), bytes_accessed=int(nbytes * COST), transcendentals=0),
+            cost_estimate=pl.CostEstimate(flops=int(flops * scale), bytes_accessed=int(nbytes * scale), transcendentals=0),
             name=name,
         )
 
@@ -380,6 +382,7 @@
 
     for name in STEPS:
         call.last = [done[other] for other in AFTER.get(name, ())]
+        call.scale = COST / 8 if name in LIGHT else COST
         step(name[0], int(name[1:]))
         done[name] = call.result
     call.last = []

time: 193 us -> 213 us (1.10)
  waiting for transfers between devices: 70.2 us -> 84.7 us
  Pallas kernels: 67.8 us -> 72.6 us
    all_to_all x4, waiting for transfers between devices: 30.5 us -> 44 us  [step(): pieces = lax.all_to_all(pieces.reshape(-1, 2 * W), 'frq', 0, 0, tiled=True)]
    pallas_call x24, Pallas kernels: 67.8 us -> 72.6 us  [go(): out = run(*operands, *before)]
  transfers between devices with their start and end apart: 19 -> 19, of which waited for: 14 -> 12; matrix products, arithmetic and copies ran while one was open for 0% -> 0% of each run, Pallas kernels for 23% -> 23%
where the time goes in v4:
time: 213 us; the launch traced here: 211 us
  waiting for transfers between devices  84.7 us (40%)
  Pallas kernels  72.6 us (34%)
  starting transfers between devices  40.7 us (19%)
  local copies, waits for them, and re-layouts  11.9 us (6%)
    pallas_call x24, Pallas kernels, go(): out = run(*operands, *before)  72.6 us
    all_to_all x4, waiting for transfers between devices, step(): pieces = lax.all_to_all(pieces.reshape(-1, 2 * W), 'frq', 0, 0, tiled=True)  44 us
    ppermute x15, waiting for transfers between devices, swap(): lax.ppermute(value, axis, [(i, i ^ mask) for i in range(lax.axis_size(axi...  40.7 us
    ppermute x15, starting transfers between devices, swap(): lax.ppermute(value, axis, [(i, i ^ mask) for i in range(lax.axis_size(axi...  21.5 us
    all_to_all x4, starting transfers between devices, step(): pieces = lax.all_to_all(pieces.reshape(-1, 2 * W), 'frq', 0, 0, tiled=True)  19.2 us
    unnamed x53, local copies, waits for them, and re-layouts  11.8 us
  transfers between devices with their start and end apart: 19, of which 12 were waited for; matrix products, arithmetic and copies ran while one was open for 0% of the time, Pallas kernels for 23%

profile of v4, /device:TPU:0, one launch (start us, length us, event | category | flops | bytes accessed | tf_op | source)
XLA Modules:
  0.0 211.2 jit_solution(5168334727555603322)
XLA Ops:
  0.6 4.4 %rotate_0.2 = (bf16[2,4,128,512]{3,2,1,0:T(8,128)(2,1)}, bf16[16,128,256]{2,1,0:T(8,128)(2,1)}) custom-call(s32[4]{0:T(128)} %pad_add_fusion.refs_0_, bf16[256,256]{1,0:T(8,128)(2,1)} %constant.20.clone.refs_1_, bf16[2,16,512,128]{3,2,1,0:T(8,128)(2,1)} %bitcast.45, bf16[3,2,16,128,256]{4,3,2,1,0:T(8,128)(2,1)} %bitcast.26, ...), custom_call_target="tpu_custom_call" | custom-call | flops 16000000000 | bytes 56000000 | tf_op jit(solution)/shard_map/rotate_0/pallas_call | solution.py:86
  5.0 8.2 %rotate_0.3.refs_3_.refs_1_ = bf16[2,12,128,512]{3,2,1,0:T(8,128)(2,1)} custom-call(s32[4]{0:T(128)} %pad_add_fusion.refs_0_, bf16[256,256]{1,0:T(8,128)(2,1)} %constant.20.clone.refs_1_, bf16[2,16,512,128]{3,2,1,0:T(8,128)(2,1)} %bitcast.46, bf16[3,2,16,128,256]{4,3,2,1,0:T(8,128)(2,1)} %bitcast.28, bf16[2,4,128,512]{3,2,1,0:T(8,128)(2,1)} %get-tuple-element.15.refs_4_.refs_1_), custom_call_target="tpu_custom_call" | custom-call | flops 48000000000 | bytes 168000000 | tf_op jit(solution)/shard_map/rotate_0/pallas_call | solution.py:86
  13.7 2.0 collective-permute-start.2
  15.9 1.9 copy-done.9
  17.8 1.0 masked_weights.1.refs_3_.refs_5_.refs_2_
  18.8 1.9 collective-permute-done.refs_2_
  20.7 2.8 %copy-done.1 = bf16[3,32,128,256]{3,2,1,0:T(8,128)(2,1)S(1)} copy-done((bf16[3,32,128,256]{3,2,1,0:T(8,128)(2,1)S(1)}, bf16[3,32,128,256]{3,2,1,0:T(8,128)(2,1)}, u32[]{:S(2)}) %copy-start.1) | copy-done | bytes 6291480
  23.5 3.5 %mix_0_rotate_1.4 = (bf16[4,128,512]{2,1,0:T(8,128)(2,1)S(1)}, bf16[4,128,512]{2,1,0:T(8,128)(2,1)S(1)}) custom-call(s32[4]{0:T(128)S(1)} %copy-done.16, bf16[2,4,128,512]{3,2,1,0:T(8,128)(2,1)} %get-tuple-element.15.refs_4_.refs_1_, bf16[2,4,128,512]{3,2,1,0:T(8,128)(2,1)} %collective-permute-done.refs_2_, ...), custom_call_target="tpu_custom_call" | custom-call | flops 16000000000 | bytes 80000000 | tf_op jit(solution)/shard_map/mix_0_rotate_1/pallas_call | solution.py:86
  27.0 2.1 collective-permute-start.1
  29.1 3.2 %mix_0_rotate_1.5 = (bf16[4,128,512]{2,1,0:T(8,128)(2,1)S(1)}, bf16[4,128,512]{2,1,0:T(8,128)(2,1)S(1)}) custom-call(s32[4]{0:T(128)S(1)} %copy-done.16, bf16[2,12,128,512]{3,2,1,0:T(8,128)(2,1)S(1)} %copy-done.10, bf16[2,12,128,512]{3,2,1,0:T(8,128)(2,1)} %collective-permute-done.3.refs_2_, bf16[4,512,256]{2,1,0:T(8,128)(2,1)S(1)} %masked_weights.1.refs_3_.refs_5_.refs_2_, ...), custom_call_target="tpu_custom_call" | custom-call | flops 16000000000 | bytes 80000000 | tf_op jit(solution)/shard_map/mix_0_rotate_1/pallas_call | solution.py:86
  32.4 7.6 %collective-permute-done.2.refs_5_ = bf16[16,128,256]{2,1,0:T(8,128)(2,1)} collective-permute-done((bf16[16,128,256]{2,1,0:T(8,128)(2,1)}, bf16[16,128,256]{2,1,0:T(8,128)(2,1)}, u32[]{:S(2)}, u32[]{:S(2)}) %collective-permute-start.2) | collective-permute-done | bytes 1048608 | tf_op jit(solution)/shard_map/ppermute | solution.py:313
  40.0 11.1 %collective-permute-done.1.refs_2_ = bf16[4,128,512]{2,1,0:T(8,128)(2,1)S(1)} collective-permute-done((bf16[4,128,512]{2,1,0:T(8,128)(2,1)S(1)}, bf16[4,128,512]{2,1,0:T(8,128)(2,1)S(1)}, u32[]{:S(2)}, u32[]{:S(2)}) %collective-permute-start.1) | collective-permute-done | bytes 524320 | tf_op jit(solution)/shard_map/ppermute | solution.py:313
  51.1 3.1 %mix_1_rotate_2.4.refs_5_.refs_0_ = bf16[2,4,128,512]{3,2,1,0:T(8,128)(2,1)S(1)} custom-call(s32[4]{0:T(128)S(1)} %copy-done.16, bf16[4,128,512]{2,1,0:T(8,128)(2,1)S(1)} %get-tuple-element.16.refs_5_.refs_1_, bf16[4,128,512]{2,1,0:T(8,128)(2,1)S(1)} %collective-permute-done.1.refs_2_, bf16[4,512,256]{2,1,0:T(8,128)(2,1)S(1)} %masked_weights.1.refs_3_.refs_5_.refs_2_, ...), custom_call_target="tpu_custom_call" | custom-call | flops 16000000000 | bytes 56000000 | tf_op jit(solution)/shard_map/mix_1_rotate_2/pallas_call | solution.py:86
  54.2 4.2 %collective-permute-start.4 = (bf16[2,4,128,512]{3,2,1,0:T(8,128)(2,1)S(1)}, bf16[2,4,128,512]{3,2,1,0:T(8,128)(2,1)S(1)}, u32[]{:S(2)}, u32[]{:S(2)}) collective-permute-start(bf16[2,4,128,512]{3,2,1,0:T(8,128)(2,1)S(1)} %mix_1_rotate_2.4.refs_5_.refs_0_), channel_id=1, source_target_pairs={{0,48},{8,56},{16,32},{24,40},{32,16},{40,24},{48,0},{56,8},{64,11... | collective-permute-start | bytes 3145736 | tf_op jit(solution)/shard_map/ppermute | solution.py:313
  58.4 3.2 %mix_0_rotate_1.6 = (bf16[4,128,512]{2,1,0:T(8,128)(2,1)S(1)}, bf16[4,128,512]{2,1,0:T(8,128)(2,1)S(1)}) custom-call(s32[4]{0:T(128)S(1)} %copy-done.16, bf16[2,12,128,512]{3,2,1,0:T(8,128)(2,1)S(1)} %copy-done.10, bf16[2,12,128,512]{3,2,1,0:T(8,128)(2,1)} %collective-permute-done.3.refs_2_, bf16[4,512,256]{2,1,0:T(8,128)(2,1)S(1)} %masked_weights.1.refs_3_.refs_5_.refs_2_, ...), custom_call_target="tpu_custom_call" | custom-call | flops 16000000000 | bytes 80000000 | tf_op jit(solution)/shard_map/mix_0_rotate_1/pallas_call | solution.py:86
  61.8 3.1 %mix_1_rotate_2.5.refs_5_.refs_0_ = bf16[2,4,128,512]{3,2,1,0:T(8,128)(2,1)S(1)} custom-call(s32[4]{0:T(128)S(1)} %copy-done.16, bf16[4,128,512]{2,1,0:T(8,128)(2,1)S(1)} %get-tuple-element.19.refs_6_.refs_1_, bf16[4,128,512]{2,1,0:T(8,128)(2,1)S(1)} %collective-permute-done.5.refs_2_, bf16[4,512,256]{2,1,0:T(8,128)(2,1)S(1)} %masked_weights.1.refs_3_.refs_5_.refs_2_, ...), custom_call_target="tpu_custom_call" | custom-call | flops 16000000000 | bytes 56000000 | tf_op jit(solution)/shard_map/mix_1_rotate_2/pallas_call | solution.py:86
  64.9 4.8 %collective-permute-start.8 = (bf16[2,4,128,512]{3,2,1,0:T(8,128)(2,1)S(1)}, bf16[2,4,128,512]{3,2,1,0:T(8,128)(2,1)}, u32[]{:S(2)}, u32[]{:S(2)}) collective-permute-start(bf16[2,4,128,512]{3,2,1,0:T(8,128)(2,1)S(1)} %mix_1_rotate_2.5.refs_5_.refs_0_), channel_id=1, source_target_pairs={{0,48},{8,56},{16,32},{24,40},{32,16},{40,24},{48,0},{56,8},{64,11... | collective-permute-start | bytes 3145736 | tf_op jit(solution)/shard_map/ppermute | solution.py:313
  69.7 3.6 %mix_0_rotate_1.7 = (bf16[4,128,512]{2,1,0:T(8,128)(2,1)S(1)}, bf16[4,128,512]{2,1,0:T(8,128)(2,1)}) custom-call(s32[4]{0:T(128)S(1)} %copy-done.16, bf16[2,12,128,512]{3,2,1,0:T(8,128)(2,1)S(1)} %copy-done.10, bf16[2,12,128,512]{3,2,1,0:T(8,128)(2,1)} %collective-permute-done.3.refs_2_, bf16[4,512,256]{2,1,0:T(8,128)(2,1)S(1)} %masked_weights.1.refs_3_.refs_5_.refs_2_, ...), custom_call_target="tpu_custom_call" | custom-call | flops 16000000000 | bytes 80000000 | tf_op jit(solution)/shard_map/mix_0_rotate_1/pallas_call | solution.py:86
  73.3 9.2 %collective-permute-done.4.refs_1_ = bf16[2,4,128,512]{3,2,1,0:T(8,128)(2,1)S(1)} collective-permute-done((bf16[2,4,128,512]{3,2,1,0:T(8,128)(2,1)S(1)}, bf16[2,4,128,512]{3,2,1,0:T(8,128)(2,1)S(1)}, u32[]{:S(2)}, u32[]{:S(2)}) %collective-permute-start.4) | collective-permute-done | bytes 1048608 | tf_op jit(solution)/shard_map/ppermute | solution.py:313
  83.3 3.7 %mix_1_rotate_2.6.refs_4_.refs_0_ = bf16[2,4,128,512]{3,2,1,0:T(8,128)(2,1)} custom-call(s32[4]{0:T(128)S(1)} %copy-done.16, bf16[4,128,512]{2,1,0:T(8,128)(2,1)S(1)} %get-tuple-element.21.refs_6_.refs_1_, bf16[4,128,512]{2,1,0:T(8,128)(2,1)S(1)} %collective-permute-done.7.refs_2_, bf16[4,512,256]{2,1,0:T(8,128)(2,1)S(1)} %masked_weights.1.refs_3_.refs_5_.refs_2_, ...), custom_call_target="tpu_custom_call" | custom-call | flops 16000000000 | bytes 56000000 | tf_op jit(solution)/shard_map/mix_1_rotate_2/pallas_call | solution.py:86
  87.0 3.2 %collective-permute-start.11 = (bf16[2,4,128,512]{3,2,1,0:T(8,128)(2,1)}, bf16[2,4,128,512]{3,2,1,0:T(8,128)(2,1)}, u32[]{:S(2)}, u32[]{:S(2)}) collective-permute-start(bf16[2,4,128,512]{3,2,1,0:T(8,128)(2,1)} %mix_1_rotate_2.6.refs_4_.refs_0_), channel_id=1, source_target_pairs={{0,48},{8,56},{16,32},{24,40},{32,16},{40,24},{48,0},{56,8},{64,11... | collective-permute-start | bytes 3145736 | tf_op jit(solution)/shard_map/ppermute | solution.py:313
  90.2 6.3 %collective-permute-done.6.refs_3_ = bf16[4,128,512]{2,1,0:T(8,128)(2,1)S(1)} collective-permute-done((bf16[4,128,512]{2,1,0:T(8,128)(2,1)S(1)}, bf16[4,128,512]{2,1,0:T(8,128)(2,1)S(1)}, u32[]{:S(2)}, u32[]{:S(2)}) %collective-permute-start.6) | collective-permute-done | bytes 524320 | tf_op jit(solution)/shard_map/ppermute | solution.py:313
  96.5 1.4 mix_2_own_split.4.refs_3_
  97.9 5.3 %all-to-all-start = ((bf16[8,128,512]{2,1,0:T(8,128)(2,1)}), bf16[8,128,512]{2,1,0:T(8,128)(2,1)S(1)}, u32[]{:S(2)}, u32[]{:S(2)}) async-start(bf16[8,128,512]{2,1,0:T(8,128)(2,1)} %bitcast.11), calls=%async_computation | async-start | bytes 2097152 | tf_op jit(solution)/shard_map/all_to_all | solution.py:378
  103.2 1.9 collective-permute-done.8.refs_1_
  105.1 2.3 %mix_2_other.5.refs_2_ = bf16[4,128,512]{2,1,0:T(8,128)(2,1)} custom-call(bf16[2,4,128,512]{3,2,1,0:T(8,128)(2,1)S(1)} %mix_1_rotate_2.5.refs_5_.refs_0_, bf16[2,4,128,512]{3,2,1,0:T(8,128)(2,1)} %collective-permute-done.8.refs_1_, bf16[4,512,256]{2,1,0:T(8,128)(2,1)S(1)} %masked_weights.1.refs_3_.refs_5_.refs_2_, ...), custom_call_target="tpu_custom_call" | custom-call | flops 8000000000 | bytes 32000000 | tf_op jit(solution)/shard_map/mix_2_other/pallas_call | solution.py:86
  107.4 8.8 %all-to-all-done = bf16[8,128,512]{2,1,0:T(8,128)(2,1)S(1)} async-done(((bf16[8,128,512]{2,1,0:T(8,128)(2,1)}), bf16[8,128,512]{2,1,0:T(8,128)(2,1)S(1)}, u32[]{:S(2)}, u32[]{:S(2)}) %all-to-all-start) | async-done | bytes 1048608 | tf_op jit(solution)/shard_map/all_to_all | solution.py:378
  117.2 2.8 %copy-done.2 = bf16[3,32,128,256]{3,2,1,0:T(8,128)(2,1)S(1)} copy-done((bf16[3,32,128,256]{3,2,1,0:T(8,128)(2,1)S(1)}, bf16[3,32,128,256]{3,2,1,0:T(8,128)(2,1)}, u32[]{:S(2)}) %copy-start.2) | copy-done | bytes 6291480
  119.9 1.0 copy-done.15
  121.0 3.1 %mix_1_rotate_2.7.refs_4_.refs_0_ = bf16[2,4,128,512]{3,2,1,0:T(8,128)(2,1)S(1)} custom-call(s32[4]{0:T(128)S(1)} %copy-done.16, bf16[4,128,512]{2,1,0:T(8,128)(2,1)S(1)} %copy-done.15, bf16[4,128,512]{2,1,0:T(8,128)(2,1)} %collective-permute-done.10.refs_2_, bf16[4,512,256]{2,1,0:T(8,128)(2,1)S(1)} %masked_weights.1.refs_3_.refs_5_.refs_2_, ...), custom_call_target="tpu_custom_call" | custom-call | flops 2000000000 | bytes 7000000 | tf_op jit(solution)/shard_map/mix_1_rotate_2/pallas_call | solution.py:86
  124.1 2.5 %mix_2_own_split.5.refs_3_ = bf16[8,2,4,16,512]{4,3,2,1,0:T(8,128)(2,1)} custom-call(bf16[2,4,128,512]{3,2,1,0:T(8,128)(2,1)S(1)} %copy-done.13, bf16[2,4,128,512]{3,2,1,0:T(8,128)(2,1)} %collective-permute-done.8.refs_1_, bf16[4,512,256]{2,1,0:T(8,128)(2,1)S(1)} %masked_weights.1.refs_3_.refs_5_.refs_2_, ...), custom_call_target="tpu_custom_call" | custom-call | flops 1000000000 | bytes 8000000 | tf_op jit(solution)/shard_map/mix_2_own_split/pallas_call | solution.py:86
  126.6 4.2 %all-to-all-start.1 = ((bf16[8,128,512]{2,1,0:T(8,128)(2,1)}), bf16[8,128,512]{2,1,0:T(8,128)(2,1)}, u32[]{:S(2)}, u32[]{:S(2)}) async-start(bf16[8,128,512]{2,1,0:T(8,128)(2,1)} %bitcast.13), calls=%async_computation.1 | async-start | bytes 2097152 | tf_op jit(solution)/shard_map/all_to_all | solution.py:378
  130.8 3.9 %collective-permute-start.13 = (bf16[2,4,128,512]{3,2,1,0:T(8,128)(2,1)S(1)}, bf16[2,4,128,512]{3,2,1,0:T(8,128)(2,1)}, u32[]{:S(2)}, u32[]{:S(2)}) collective-permute-start(bf16[2,4,128,512]{3,2,1,0:T(8,128)(2,1)S(1)} %mix_1_rotate_2.7.refs_4_.refs_0_), channel_id=1, source_target_pairs={{0,48},{8,56},{16,32},{24,40},{32,16},{40,24},{48,0},{56,8},{64,11... | collective-permute-start | bytes 3145736 | tf_op jit(solution)/shard_map/ppermute | solution.py:313
  134.8 2.4 %mix_2_other.6.refs_2_ = bf16[4,128,512]{2,1,0:T(8,128)(2,1)} custom-call(bf16[2,4,128,512]{3,2,1,0:T(8,128)(2,1)} %mix_1_rotate_2.6.refs_4_.refs_0_, bf16[2,4,128,512]{3,2,1,0:T(8,128)(2,1)} %collective-permute-done.11.refs_1_, bf16[4,512,256]{2,1,0:T(8,128)(2,1)S(1)} %masked_weights.1.refs_3_.refs_5_.refs_2_, ...), custom_call_target="tpu_custom_call" | custom-call | flops 1000000000 | bytes 4000000 | tf_op jit(solution)/shard_map/mix_2_other/pallas_call | solution.py:86
  137.4 8.1 %all-to-all-done.1 = bf16[8,128,512]{2,1,0:T(8,128)(2,1)} async-done(((bf16[8,128,512]{2,1,0:T(8,128)(2,1)}), bf16[8,128,512]{2,1,0:T(8,128)(2,1)}, u32[]{:S(2)}, u32[]{:S(2)}) %all-to-all-start.1) | async-done | bytes 1048608 | tf_op jit(solution)/shard_map/all_to_all | solution.py:378
  145.4 2.7 %gather_frequencies.5.refs_4_.refs_2_ = bf16[16,64,512]{2,1,0:T(8,128)(2,1)S(1)} custom-call(bf16[256,256]{1,0:T(8,128)(2,1)S(1)} %copy-done.17, bf16[8,2,4,16,512]{4,3,2,1,0:T(8,128)(2,1)} %bitcast.14.refs_1_, bf16[4,128,512]{2,1,0:T(8,128)(2,1)} %mix_2_other.6.refs_2_), custom_call_target="tpu_custom_call" | custom-call | flops 1000000000 | bytes 5000000 | tf_op jit(solution)/shard_map/gather_frequencies/pallas_call | solution.py:86
  148.1 2.6 %collective-permute-done.12.refs_3_ = bf16[4,128,512]{2,1,0:T(8,128)(2,1)} collective-permute-done((bf16[4,128,512]{2,1,0:T(8,128)(2,1)}, bf16[4,128,512]{2,1,0:T(8,128)(2,1)}, u32[]{:S(2)}, u32[]{:S(2)}) %collective-permute-start.12) | collective-permute-done | bytes 524320 | tf_op jit(solution)/shard_map/ppermute | solution.py:313
  150.7 2.6 %mix_2_own_split.6.refs_3_ = bf16[8,2,4,16,512]{4,3,2,1,0:T(8,128)(2,1)} custom-call(bf16[2,4,128,512]{3,2,1,0:T(8,128)(2,1)} %mix_1_rotate_2.6.refs_4_.refs_0_, bf16[2,4,128,512]{3,2,1,0:T(8,128)(2,1)} %collective-permute-done.11.refs_1_, bf16[4,512,256]{2,1,0:T(8,128)(2,1)S(1)} %masked_weights.1.refs_3_.refs_5_.refs_2_, ...), custom_call_target="tpu_custom_call" | custom-call | flops 1000000000 | bytes 8000000 | tf_op jit(solution)/shard_map/mix_2_own_split/pallas_call | solution.py:86
  154.2 5.2 %all-to-all-start.2 = ((bf16[8,128,512]{2,1,0:T(8,128)(2,1)}), bf16[8,128,512]{2,1,0:T(8,128)(2,1)}, u32[]{:S(2)}, u32[]{:S(2)}) async-start(bf16[8,128,512]{2,1,0:T(8,128)(2,1)} %bitcast.15), calls=%async_computation.2 | async-start | bytes 2097152 | tf_op jit(solution)/shard_map/all_to_all | solution.py:378
  159.5 2.3 %mix_2_other.7.refs_2_ = bf16[4,128,512]{2,1,0:T(8,128)(2,1)} custom-call(bf16[2,4,128,512]{3,2,1,0:T(8,128)(2,1)S(1)} %mix_1_rotate_2.7.refs_4_.refs_0_, bf16[2,4,128,512]{3,2,1,0:T(8,128)(2,1)} %collective-permute-done.13.refs_1_, bf16[4,512,256]{2,1,0:T(8,128)(2,1)S(1)} %masked_weights.1.refs_3_.refs_5_.refs_2_, ...), custom_call_target="tpu_custom_call" | custom-call | flops 1000000000 | bytes 4000000 | tf_op jit(solution)/shard_map/mix_2_other/pallas_call | solution.py:86
  162.1 11.6 %all-to-all-done.2 = bf16[8,128,512]{2,1,0:T(8,128)(2,1)} async-done(((bf16[8,128,512]{2,1,0:T(8,128)(2,1)}), bf16[8,128,512]{2,1,0:T(8,128)(2,1)}, u32[]{:S(2)}, u32[]{:S(2)}) %all-to-all-start.2) | async-done | bytes 1048608 | tf_op jit(solution)/shard_map/all_to_all | solution.py:378
  173.6 2.7 %gather_frequencies.6.refs_4_.refs_3_ = bf16[16,64,512]{2,1,0:T(8,128)(2,1)S(1)} custom-call(bf16[256,256]{1,0:T(8,128)(2,1)S(1)} %copy-done.17, bf16[8,2,4,16,512]{4,3,2,1,0:T(8,128)(2,1)} %bitcast.16.refs_1_, bf16[4,128,512]{2,1,0:T(8,128)(2,1)} %mix_2_other.7.refs_2_), custom_call_target="tpu_custom_call" | custom-call | flops 1000000000 | bytes 5000000 | tf_op jit(solution)/shard_map/gather_frequencies/pallas_call | solution.py:86
  176.3 2.1 %mix_2_own_split.7.refs_2_ = bf16[8,2,4,16,512]{4,3,2,1,0:T(8,128)(2,1)S(1)} custom-call(bf16[2,4,128,512]{3,2,1,0:T(8,128)(2,1)S(1)} %mix_1_rotate_2.7.refs_4_.refs_0_, bf16[2,4,128,512]{3,2,1,0:T(8,128)(2,1)} %collective-permute-done.13.refs_1_, bf16[4,512,256]{2,1,0:T(8,128)(2,1)S(1)} %masked_weights.1.refs_3_.refs_5_.refs_2_, ...), custom_call_target="tpu_custom_call" | custom-call | flops 1000000000 | bytes 8000000 | tf_op jit(solution)/shard_map/mix_2_own_split/pallas_call | solution.py:86
  179.4 4.4 %all-to-all-start.3 = ((bf16[8,128,512]{2,1,0:T(8,128)(2,1)}), bf16[8,128,512]{2,1,0:T(8,128)(2,1)}, u32[]{:S(2)}, u32[]{:S(2)}) async-start(bf16[8,128,512]{2,1,0:T(8,128)(2,1)} %bitcast.43), calls=%async_computation.3 | async-start | bytes 2097152 | tf_op jit(solution)/shard_map/all_to_all | solution.py:378
  184.1 15.6 %all-to-all-done.3 = bf16[8,128,512]{2,1,0:T(8,128)(2,1)} async-done(((bf16[8,128,512]{2,1,0:T(8,128)(2,1)}), bf16[8,128,512]{2,1,0:T(8,128)(2,1)}, u32[]{:S(2)}, u32[]{:S(2)}) %all-to-all-start.3) | async-done | bytes 1048608 | tf_op jit(solution)/shard_map/all_to_all | solution.py:378
  199.6 1.2 copy-done.8
  200.9 2.7 %gather_frequencies.7.refs_4_ = bf16[16,64,512]{2,1,0:T(8,128)(2,1)S(1)} custom-call(bf16[256,256]{1,0:T(8,128)(2,1)S(1)} %copy-done.17, bf16[8,2,4,16,512]{4,3,2,1,0:T(8,128)(2,1)} %bitcast.18.refs_1_, bf16[8,2,4,16,512]{4,3,2,1,0:T(8,128)(2,1)S(1)} %copy-done.8), custom_call_target="tpu_custom_call" | custom-call | flops 1000000000 | bytes 5000000 | tf_op jit(solution)/shard_map/gather_frequencies/pallas_call | solution.py:86
  203.5 7.6 %target_map.1 = f32[256,64,128]{2,1,0:T(8,128)} custom-call(bf16[256,256]{1,0:T(8,128)(2,1)S(1)} %fusion.refs_0_, bf16[16,64,512]{2,1,0:T(8,128)(2,1)S(1)} %gather_frequencies.4.refs_6_.refs_1_, bf16[16,64,512]{2,1,0:T(8,128)(2,1)S(1)} %copy-done.4, bf16[16,64,512]{2,1,0:T(8,128)(2,1)S(1)} %copy-done.6, bf16[16,64,512]{2,1,0:T(8,128)(2,1)S(1)} %gather_frequencies.7.refs_4_), custom_call_target="tpu_custom_call" | custom-call | flops 2500000000 | bytes 31457280 | tf_op jit(solution)/shard_map/target_map/pallas_call | solution.py:86
  (74 shorter events, 6.0 us)
Async XLA Ops:
  0.0 183.8 %copy-start = (bf16[256,256]{1,0:T(8,128)(2,1)S(1)}, bf16[256,256]{1,0:T(8,128)(2,1)}, u32[]{:S(2)}) copy-start(bf16[256,256]{1,0:T(8,128)(2,1)} %param.12) | copy-start | bytes 393220
  5.0 10.7 %copy-start.18 = (s32[3,4,2]{1,2,0:T(2,128)S(1)}, s32[3,4,2]{1,2,0:T(2,128)}, u32[]{:S(2)}) copy-start(s32[3,4,2]{1,2,0:T(2,128)} %param.11) | copy-start | bytes 292
  5.0 10.9 %copy-start.11 = (bf16[3,2,2,256,256]{4,3,2,1,0:T(8,128)(2,1)S(1)}, bf16[3,2,2,256,256]{4,3,2,1,0:T(8,128)(2,1)}, u32[]{:S(2)}) copy-start(bf16[3,2,2,256,256]{4,3,2,1,0:T(8,128)(2,1)} %refs_2_.1) | copy-start | bytes 4718596
  5.0 10.9 %copy-start.16 = (s32[4]{0:T(128)S(1)}, s32[4]{0:T(128)}, u32[]{:S(2)}) copy-start(s32[4]{0:T(128)} %pad_add_fusion.refs_0_) | copy-start | bytes 52
  13.2 15.9 %collective-permute-start.3 = (bf16[2,12,128,512]{3,2,1,0:T(8,128)(2,1)}, bf16[2,12,128,512]{3,2,1,0:T(8,128)(2,1)}, u32[]{:S(2)}, u32[]{:S(2)}) collective-permute-start(bf16[2,12,128,512]{3,2,1,0:T(8,128)(2,1)} %rotate_0.3.refs_3_.refs_1_), channel_id=1, source_target_pairs={{0,8},{8,0},{16,24},{24,16},{32,40},{40,32},{48,56},{56,48},{64,72... | collective-permute-start | bytes 9437192 | tf_op jit(solution)/shard_map/ppermute | solution.py:313
  13.2 7.5 %collective-permute-start = (bf16[2,4,128,512]{3,2,1,0:T(8,128)(2,1)}, bf16[2,4,128,512]{3,2,1,0:T(8,128)(2,1)}, u32[]{:S(2)}, u32[]{:S(2)}) collective-permute-start(bf16[2,4,128,512]{3,2,1,0:T(8,128)(2,1)} %get-tuple-element.15.refs_4_.refs_1_), channel_id=1, source_target_pairs={{0,8},{8,0},{16,24},{24,16},{32,40},{40,32},{48,56},{56,48},{64,72... | collective-permute-start | bytes 3145736 | tf_op jit(solution)/shard_map/ppermute | solution.py:313
  13.7 26.3 %collective-permute-start.2 = (bf16[16,128,256]{2,1,0:T(8,128)(2,1)}, bf16[16,128,256]{2,1,0:T(8,128)(2,1)}, u32[]{:S(2)}, u32[]{:S(2)}) collective-permute-start(bf16[16,128,256]{2,1,0:T(8,128)(2,1)} %get-tuple-element.18), channel_id=1, source_target_pairs={{0,16},{8,24},{16,0},{24,8},{32,48},{40,56},{48,32},{56,40},{64,80... | collective-permute-start | bytes 3145736 | tf_op jit(solution)/shard_map/ppermute | solution.py:313
  15.9 1.9 copy-start.9
  20.7 2.8 %copy-start.1 = (bf16[3,32,128,256]{3,2,1,0:T(8,128)(2,1)S(1)}, bf16[3,32,128,256]{3,2,1,0:T(8,128)(2,1)}, u32[]{:S(2)}) copy-start(bf16[3,32,128,256]{3,2,1,0:T(8,128)(2,1)} %param.9) | copy-start | bytes 18874372
  23.5 5.6 %copy-start.10 = (bf16[2,12,128,512]{3,2,1,0:T(8,128)(2,1)S(1)}, bf16[2,12,128,512]{3,2,1,0:T(8,128)(2,1)}, u32[]{:S(2)}) copy-start(bf16[2,12,128,512]{3,2,1,0:T(8,128)(2,1)} %rotate_0.3.refs_3_.refs_1_) | copy-start | bytes 9437188
  23.5 27.7 %slice-start = ((s8[6291456]{0:T(1024)(128)(4,1)}), s8[4194304]{0:T(1024)(128)(4,1)S(1)}, s32[]{:S(2)}) async-start(s8[6291456]{0:T(1024)(128)(4,1)} %bitcast.33), calls=%async_computation.4 | async-start | bytes 8388608
  27.0 24.1 %collective-permute-start.1 = (bf16[4,128,512]{2,1,0:T(8,128)(2,1)S(1)}, bf16[4,128,512]{2,1,0:T(8,128)(2,1)S(1)}, u32[]{:S(2)}, u32[]{:S(2)}) collective-permute-start(bf16[4,128,512]{2,1,0:T(8,128)(2,1)S(1)} %get-tuple-element.17), channel_id=1, source_target_pairs={{0,16},{8,24},{16,0},{24,8},{32,48},{40,56},{48,32},{56,40},{64,80... | collective-permute-start | bytes 1572872 | tf_op jit(solution)/shard_map/ppermute | solution.py:313
  29.1 22.1 %slice-start.1 = ((s8[6291456]{0:T(1024)(128)(4,1)}), s8[2097152]{0:T(1024)(128)(4,1)S(1)}, s32[]{:S(2)}) async-start(s8[6291456]{0:T(1024)(128)(4,1)} %bitcast.33), calls=%async_computation.5 | async-start | bytes 4194304
  32.3 29.5 %collective-permute-start.5 = (bf16[4,128,512]{2,1,0:T(8,128)(2,1)S(1)}, bf16[4,128,512]{2,1,0:T(8,128)(2,1)S(1)}, u32[]{:S(2)}, u32[]{:S(2)}) collective-permute-start(bf16[4,128,512]{2,1,0:T(8,128)(2,1)S(1)} %get-tuple-element.20), channel_id=1, source_target_pairs={{0,16},{8,24},{16,0},{24,8},{32,48},{40,56},{48,32},{56,40},{64,80... | collective-permute-start | bytes 1572872 | tf_op jit(solution)/shard_map/ppermute | solution.py:313
  51.1 10.7 %slice-start.2 = ((s8[6291456]{0:T(1024)(128)(4,1)}), s8[2097152]{0:T(1024)(128)(4,1)S(1)}, s32[]{:S(2)}) async-start(s8[6291456]{0:T(1024)(128)(4,1)} %bitcast.36), calls=%async_computation.6 | async-start | bytes 4194304
  54.2 7.6 %slice-start.3 = ((s8[6291456]{0:T(1024)(128)(4,1)}), s8[4194304]{0:T(1024)(128)(4,1)S(1)}, s32[]{:S(2)}) async-start(s8[6291456]{0:T(1024)(128)(4,1)} %bitcast.36), calls=%async_computation.7 | async-start | bytes 8388608
  54.2 28.3 %collective-permute-start.4 = (bf16[2,4,128,512]{3,2,1,0:T(8,128)(2,1)S(1)}, bf16[2,4,128,512]{3,2,1,0:T(8,128)(2,1)S(1)}, u32[]{:S(2)}, u32[]{:S(2)}) collective-permute-start(bf16[2,4,128,512]{3,2,1,0:T(8,128)(2,1)S(1)} %mix_1_rotate_2.4.refs_5_.refs_0_), channel_id=1, source_target_pairs={{0,48},{8,56},{16,32},{24,40},{32,16},{40,24},{48,0},{56,8},{64,11... | collective-permute-start | bytes 3145736 | tf_op jit(solution)/shard_map/ppermute | solution.py:313
  61.6 21.6 %collective-permute-start.7 = (bf16[4,128,512]{2,1,0:T(8,128)(2,1)S(1)}, bf16[4,128,512]{2,1,0:T(8,128)(2,1)S(1)}, u32[]{:S(2)}, u32[]{:S(2)}) collective-permute-start(bf16[4,128,512]{2,1,0:T(8,128)(2,1)S(1)} %get-tuple-element.23), channel_id=1, source_target_pairs={{0,16},{8,24},{16,0},{24,8},{32,48},{40,56},{48,32},{56,40},{64,80... | collective-permute-start | bytes 1572872 | tf_op jit(solution)/shard_map/ppermute | solution.py:313
  61.8 21.4 %slice-start.4 = ((s8[6291456]{0:T(1024)(128)(4,1)}), s8[2097152]{0:T(1024)(128)(4,1)S(1)}, s32[]{:S(2)}) async-start(s8[6291456]{0:T(1024)(128)(4,1)} %bitcast.39), calls=%async_computation.8 | async-start | bytes 4194304
  64.9 40.2 %copy-start.12 = (bf16[2,4,128,512]{3,2,1,0:T(8,128)(2,1)}, bf16[2,4,128,512]{3,2,1,0:T(8,128)(2,1)S(1)}, u32[]{:S(2)}) copy-start(bf16[2,4,128,512]{3,2,1,0:T(8,128)(2,1)S(1)} %mix_1_rotate_2.5.refs_5_.refs_0_) | copy-start | bytes 3145732
  64.9 18.3 %slice-start.5 = ((s8[6291456]{0:T(1024)(128)(4,1)}), s8[4194304]{0:T(1024)(128)(4,1)S(1)}, s32[]{:S(2)}) async-start(s8[6291456]{0:T(1024)(128)(4,1)} %bitcast.39), calls=%async_computation.9 | async-start | bytes 8388608
  64.9 40.2 %collective-permute-start.8 = (bf16[2,4,128,512]{3,2,1,0:T(8,128)(2,1)S(1)}, bf16[2,4,128,512]{3,2,1,0:T(8,128)(2,1)}, u32[]{:S(2)}, u32[]{:S(2)}) collective-permute-start(bf16[2,4,128,512]{3,2,1,0:T(8,128)(2,1)S(1)} %mix_1_rotate_2.5.refs_5_.refs_0_), channel_id=1, source_target_pairs={{0,48},{8,56},{16,32},{24,40},{32,16},{40,24},{48,0},{56,8},{64,11... | collective-permute-start | bytes 3145736 | tf_op jit(solution)/shard_map/ppermute | solution.py:313
  73.3 9.9 %copy-start.14 = (bf16[4,128,512]{2,1,0:T(8,128)(2,1)}, bf16[4,128,512]{2,1,0:T(8,128)(2,1)S(1)}, u32[]{:S(2)}) copy-start(bf16[4,128,512]{2,1,0:T(8,128)(2,1)S(1)} %get-tuple-element.22.refs_3_.refs_1_) | copy-start | bytes 1572868
  73.3 43.9 %collective-permute-start.10 = (bf16[4,128,512]{2,1,0:T(8,128)(2,1)}, bf16[4,128,512]{2,1,0:T(8,128)(2,1)}, u32[]{:S(2)}, u32[]{:S(2)}) collective-permute-start(bf16[4,128,512]{2,1,0:T(8,128)(2,1)} %get-tuple-element.24), channel_id=1, source_target_pairs={{0,16},{8,24},{16,0},{24,8},{32,48},{40,56},{48,32},{56,40},{64,80... | collective-permute-start | bytes 1572872 | tf_op jit(solution)/shard_map/ppermute | solution.py:313
  83.1 13.3 %collective-permute-start.6 = (bf16[4,128,512]{2,1,0:T(8,128)(2,1)S(1)}, bf16[4,128,512]{2,1,0:T(8,128)(2,1)S(1)}, u32[]{:S(2)}, u32[]{:S(2)}) collective-permute-start(bf16[4,128,512]{2,1,0:T(8,128)(2,1)S(1)} %mix_2_other.4.refs_6_), channel_id=1, source_target_pairs={{0,16},{8,24},{16,0},{24,8},{32,48},{40,56},{48,32},{56,40},{64,80... | collective-permute-start | bytes 1572872 | tf_op jit(solution)/shard_map/ppermute | solution.py:313
  87.0 47.8 %collective-permute-start.11 = (bf16[2,4,128,512]{3,2,1,0:T(8,128)(2,1)}, bf16[2,4,128,512]{3,2,1,0:T(8,128)(2,1)}, u32[]{:S(2)}, u32[]{:S(2)}) collective-permute-start(bf16[2,4,128,512]{3,2,1,0:T(8,128)(2,1)} %mix_1_rotate_2.6.refs_4_.refs_0_), channel_id=1, source_target_pairs={{0,48},{8,56},{16,32},{24,40},{32,16},{40,24},{48,0},{56,8},{64,11... | collective-permute-start | bytes 3145736 | tf_op jit(solution)/shard_map/ppermute | solution.py:313
  97.9 18.3 %all-to-all-start = ((bf16[8,128,512]{2,1,0:T(8,128)(2,1)}), bf16[8,128,512]{2,1,0:T(8,128)(2,1)S(1)}, u32[]{:S(2)}, u32[]{:S(2)}) async-start(bf16[8,128,512]{2,1,0:T(8,128)(2,1)} %bitcast.11), calls=%async_computation | async-start | bytes 2097152 | tf_op jit(solution)/shard_map/all_to_all | solution.py:378
  103.2 13.0 %copy-start.17 = (bf16[256,256]{1,0:T(8,128)(2,1)S(1)}, bf16[256,256]{1,0:T(8,128)(2,1)}, u32[]{:S(2)}) copy-start(bf16[256,256]{1,0:T(8,128)(2,1)} %constant.21.clone.refs_0_) | copy-start | bytes 393220
  107.4 16.7 %collective-permute-start.9 = (bf16[4,128,512]{2,1,0:T(8,128)(2,1)}, bf16[4,128,512]{2,1,0:T(8,128)(2,1)}, u32[]{:S(2)}, u32[]{:S(2)}) collective-permute-start(bf16[4,128,512]{2,1,0:T(8,128)(2,1)} %mix_2_other.5.refs_2_), channel_id=1, source_target_pairs={{0,16},{8,24},{16,0},{24,8},{32,48},{40,56},{48,32},{56,40},{64,80... | collective-permute-start | bytes 1572872 | tf_op jit(solution)/shard_map/ppermute | solution.py:313
  117.1 2.8 %copy-start.2 = (bf16[3,32,128,256]{3,2,1,0:T(8,128)(2,1)S(1)}, bf16[3,32,128,256]{3,2,1,0:T(8,128)(2,1)}, u32[]{:S(2)}) copy-start(bf16[3,32,128,256]{3,2,1,0:T(8,128)(2,1)} %param.9) | copy-start | bytes 18874372
  119.9 1.0 copy-start.15
  121.0 3.1 %copy-start.13 = (bf16[2,4,128,512]{3,2,1,0:T(8,128)(2,1)S(1)}, bf16[2,4,128,512]{3,2,1,0:T(8,128)(2,1)}, u32[]{:S(2)}) copy-start(bf16[2,4,128,512]{3,2,1,0:T(8,128)(2,1)} %copy-done.12) | copy-start | bytes 3145732
  126.6 18.8 %all-to-all-start.1 = ((bf16[8,128,512]{2,1,0:T(8,128)(2,1)}), bf16[8,128,512]{2,1,0:T(8,128)(2,1)}, u32[]{:S(2)}, u32[]{:S(2)}) async-start(bf16[8,128,512]{2,1,0:T(8,128)(2,1)} %bitcast.13), calls=%async_computation.1 | async-start | bytes 2097152 | tf_op jit(solution)/shard_map/all_to_all | solution.py:378
  130.8 28.6 %collective-permute-start.13 = (bf16[2,4,128,512]{3,2,1,0:T(8,128)(2,1)S(1)}, bf16[2,4,128,512]{3,2,1,0:T(8,128)(2,1)}, u32[]{:S(2)}, u32[]{:S(2)}) collective-permute-start(bf16[2,4,128,512]{3,2,1,0:T(8,128)(2,1)S(1)} %mix_1_rotate_2.7.refs_4_.refs_0_), channel_id=1, source_target_pairs={{0,48},{8,56},{16,32},{24,40},{32,16},{40,24},{48,0},{56,8},{64,11... | collective-permute-start | bytes 3145736 | tf_op jit(solution)/shard_map/ppermute | solution.py:313
  137.2 13.5 %collective-permute-start.12 = (bf16[4,128,512]{2,1,0:T(8,128)(2,1)}, bf16[4,128,512]{2,1,0:T(8,128)(2,1)}, u32[]{:S(2)}, u32[]{:S(2)}) collective-permute-start(bf16[4,128,512]{2,1,0:T(8,128)(2,1)} %mix_2_other.6.refs_2_), channel_id=1, source_target_pairs={{0,16},{8,24},{16,0},{24,8},{32,48},{40,56},{48,32},{56,40},{64,80... | collective-permute-start | bytes 1572872 | tf_op jit(solution)/shard_map/ppermute | solution.py:313
  153.3 1.0 copy-start.3
  154.2 19.4 %all-to-all-start.2 = ((bf16[8,128,512]{2,1,0:T(8,128)(2,1)}), bf16[8,128,512]{2,1,0:T(8,128)(2,1)}, u32[]{:S(2)}, u32[]{:S(2)}) async-start(bf16[8,128,512]{2,1,0:T(8,128)(2,1)} %bitcast.15), calls=%async_computation.2 | async-start | bytes 2097152 | tf_op jit(solution)/shard_map/all_to_all | solution.py:378
  161.8 14.5 %collective-permute-start.14 = (bf16[4,128,512]{2,1,0:T(8,128)(2,1)}, bf16[4,128,512]{2,1,0:T(8,128)(2,1)}, u32[]{:S(2)}, u32[]{:S(2)}) collective-permute-start(bf16[4,128,512]{2,1,0:T(8,128)(2,1)} %mix_2_other.7.refs_2_), channel_id=1, source_target_pairs={{0,16},{8,24},{16,0},{24,8},{32,48},{40,56},{48,32},{56,40},{64,80... | collective-permute-start | bytes 1572872 | tf_op jit(solution)/shard_map/ppermute | solution.py:313
  176.3 2.2 %copy-start.5 = (bf16[16,64,512]{2,1,0:T(8,128)(2,1)}, bf16[16,64,512]{2,1,0:T(8,128)(2,1)S(1)}, u32[]{:S(2)}) copy-start(bf16[16,64,512]{2,1,0:T(8,128)(2,1)S(1)} %gather_frequencies.6.refs_4_.refs_3_) | copy-start | bytes 3145732
  176.3 7.5 %copy-start.19 = (s32[256]{0:T(256)S(1)}, s32[256]{0:T(256)}, u32[]{:S(2)}) copy-start(s32[256]{0:T(256)} %constant.22.clone) | copy-start | bytes 3076
  178.5 1.0 copy-start.7
  179.4 24.1 %copy-start.4 = (bf16[16,64,512]{2,1,0:T(8,128)(2,1)S(1)}, bf16[16,64,512]{2,1,0:T(8,128)(2,1)}, u32[]{:S(2)}) copy-start(bf16[16,64,512]{2,1,0:T(8,128)(2,1)} %copy-done.3) | copy-start | bytes 3145732
  179.4 24.1 %copy-start.6 = (bf16[16,64,512]{2,1,0:T(8,128)(2,1)S(1)}, bf16[16,64,512]{2,1,0:T(8,128)(2,1)}, u32[]{:S(2)}) copy-start(bf16[16,64,512]{2,1,0:T(8,128)(2,1)} %copy-done.5) | copy-start | bytes 3145732
  179.4 20.2 %all-to-all-start.3 = ((bf16[8,128,512]{2,1,0:T(8,128)(2,1)}), bf16[8,128,512]{2,1,0:T(8,128)(2,1)}, u32[]{:S(2)}, u32[]{:S(2)}) async-start(bf16[8,128,512]{2,1,0:T(8,128)(2,1)} %bitcast.43), calls=%async_computation.3 | async-start | bytes 2097152 | tf_op jit(solution)/shard_map/all_to_all | solution.py:378
  199.6 1.2 copy-start.8
